TPU v7x, 32 devices: a whole 2x2x4 slice. The times are simulated.
32 devices in a mesh: seq: 16 (over z, x, core), head: 2 (over y).
Axes of the slice: x: 2, y: 2, z: 4, core: 2. Of those that a mesh axis runs over, the one named last changes fastest.
Arguments:
- queries: bfloat16 [16384, 3072], P('seq', 'head'), may hold values from -6 to 6
- keys: bfloat16 [16384, 3072], P('seq', 'head'), may hold values from -6 to 6
- values: bfloat16 [16384, 3072], P('seq', 'head'), may hold values from -6 to 6
- tile_pool: int32 [24, 256], P('head'), may hold values from 0 to 127, as said below
- tile_lists: int32 [24, 128, 12], P('head', 'seq'), may hold values from 0 to 15, as said below
- key_slot: int32 [128], replicated, may hold values from 0 to 127, as said below
Outputs:
- attended: bfloat16 [16384, 3072], P(('seq', 'head'))
Inputs may be any that keep to these rules, and one draw needn't show every extreme that they name: `tile_pool`: for each index i of seq and each group of 12 heads (heads g * 12 onward), the pool entries of those heads for index i (columns i * 16 onward) name tiles whose slots lie on any one index of seq (slot // 8) at most 12 times, and exactly 12 times on some index. `tile_lists`: the 12 entries of one head and one query tile are distinct. `key_slot`: A permutation of the tiles that keeps tiles 0 to 3 at their own slots.
All inputs are finite; a program needn't handle non-finite values.
Results may differ from a plain program's by a relative error of at most 0.0043.
Values may be sent and summed in bfloat16 or wider, within the bound.
No kernel may reach another device: no remote copies, remote signals or barrier semaphores. Data moves between devices by JAX's collectives and lax.ppermute only.
A program may use at most 128 MiB of HBM per device.

v0:
```python
import jax
import jax.numpy as jnp
from jax import lax
from jax.sharding import PartitionSpec as P

TILE = 128
SHARED = 4


def from_root(value, axis, source):
    kept = jnp.where(lax.axis_index(axis) == source, value, 0).astype(value.dtype)
    return lax.psum(kept, axis)


def arrange(matrix, tile_count, head_count, head_size):
    return matrix.reshape(tile_count, TILE, head_count, head_size).transpose(2, 0, 1, 3)


def finish(scores, value_part, pattern):
    tile_top = jnp.max(scores, -1)
    weights = jnp.exp(scores - tile_top[..., None])
    row_total = jnp.sum(weights, -1)
    numerator = jnp.einsum(
        pattern, weights.astype(jnp.bfloat16), value_part, preferred_element_type=jnp.float32
    )
    return (numerator, tile_top, row_total)


def blend_tiles(numerator, tile_top, row_total):
    overall = jnp.max(tile_top, 1, keepdims=True)
    factor = jnp.exp(tile_top - overall)
    upper = jnp.sum(factor[..., None] * numerator, 1)
    lower = jnp.sum(factor * row_total, 1)
    return (upper / lower[..., None]).astype(jnp.bfloat16)


def body(queries, keys, values, tile_pool, tile_lists, key_slot):
    seq_count = lax.axis_size("seq")
    my_index = lax.axis_index("seq")
    head_count, pool_total = tile_pool.shape
    pool_len = pool_total // seq_count
    list_len = tile_lists.shape[2]
    rows, width = queries.shape
    head_size = width // head_count
    tile_count = rows // TILE
    bound_slots = (head_count * pool_len + seq_count - 1) // seq_count
    block_tiles = min(tile_count, max(1, 512 // TILE))
    block_count = tile_count // block_tiles
    scaling = head_size ** (-0.5)
    query_heads = arrange(queries, tile_count, head_count, head_size)
    key_value = jnp.concatenate(
        [
            arrange(keys, tile_count, head_count, head_size),
            arrange(values, tile_count, head_count, head_size),
        ],
        -1,
    )
    flat_kv = key_value.reshape(head_count * tile_count, TILE, 2 * head_size)
    shared = from_root(key_value[:, :SHARED], "seq", 0)
    own_pool = lax.dynamic_slice_in_dim(tile_pool, my_index * pool_len, pool_len, 1)
    storage = key_slot[own_pool]
    owner_dev = (storage // tile_count).reshape(-1)
    head_ids = jnp.arange(head_count, dtype=jnp.int32)[:, None]
    req_code = (head_ids * tile_count + storage % tile_count).reshape(-1)
    matches = (owner_dev[:, None] == jnp.arange(seq_count, dtype=jnp.int32)[None, :]).astype(
        jnp.int32
    )
    slot_pos = jnp.sum((jnp.cumsum(matches, 0) - matches) * matches, 1)
    owner_dev, slot_pos, req_code = (owner_dev, slot_pos, req_code)
    outgoing = jnp.zeros((seq_count, bound_slots), jnp.int32).at[owner_dev, slot_pos].set(req_code)
    incoming = lax.all_to_all(outgoing, "seq", split_axis=0, concat_axis=0, tiled=True)
    replies = lax.all_to_all(flat_kv[incoming], "seq", split_axis=0, concat_axis=0, tiled=True)
    pool_tiles = replies[
        owner_dev.reshape(head_count, pool_len), slot_pos.reshape(head_count, pool_len)
    ]
    query_blocks = query_heads.reshape(head_count * block_count, block_tiles, TILE, head_size)
    list_blocks = tile_lists.reshape(head_count * block_count, block_tiles, list_len)
    head_of = jnp.arange(head_count * block_count, dtype=jnp.int32) // block_count

    def per_block(member):
        query_blk, list_blk, head_id = member
        listed = pool_tiles[head_id][list_blk]
        shared_head = shared[head_id]
        common = jnp.broadcast_to(shared_head[None], (block_tiles,) + shared_head.shape)
        keyset = jnp.concatenate([common, listed], 1)
        scores = (
            jnp.einsum(
                "tqd,tjkd->tjqk",
                query_blk,
                keyset[..., :head_size],
                preferred_element_type=jnp.float32,
            )
            * scaling
        )
        numerator, tile_top, row_total = finish(scores, keyset[..., head_size:], "tjqk,tjkd->tjqd")
        return blend_tiles(numerator, tile_top, row_total)

    per_blocks = lax.map(per_block, (query_blocks, list_blocks, head_of))
    per_heads = per_blocks.reshape(head_count, tile_count, TILE, head_size)
    result = per_heads.transpose(1, 2, 0, 3).reshape(rows, width)
    return lax.all_to_all(result, "head", split_axis=0, concat_axis=1, tiled=True)


def solution(mesh):
    return jax.shard_map(
        body,
        mesh=mesh,
        in_specs=(
            P("seq", "head"),
            P("seq", "head"),
            P("seq", "head"),
            P("head", None),
            P("head", "seq", None),
            P(),
        ),
        out_specs=P(("seq", "head"), None),
        check_vma=False,
    )
```

profile of v0, /device:TPU:9, one launch (start us, length us, event | category | flops | bytes accessed | tf_op | source)
XLA Modules:
  0.0 853.6 jit_solution(8163207406751818542)
XLA Ops:
  10.7 26.9 %scatter_fusion = s32[16,12]{1,0:T(8,128)} fusion(s32[16,12]{1,0:T(8,128)} %broadcast.280, s32[192]{0:T(256)S(1)} %bitcast.128, s32[192]{0:T(256)S(1)} %get-tuple-element.84), kind=kCustom, calls=%fused_computation.4 | custom fusion | bytes 3840 | tf_op jit(solution)/shard_map/scatter | solution.py:70
  37.6 6.7 all-to-all-start
  44.3 2.9 copy.30
  47.2 2.7 copy.47
  49.9 4.6 copy.31
  54.5 2.7 copy.48
  58.9 3.2 pad_maximum_fusion.2
  62.1 9.1 %copy.32 = bf16[12,8,128,256]{3,2,1,0:T(8,128)(2,1)} copy(bf16[12,8,128,256]{2,1,3,0:T(8,128)(2,1)} %pad_maximum_fusion.2) | data formatting | bytes 12582912 | tf_op jit(solution)/shard_map/concatenate | solution.py:51
  71.3 11.0 %gather_fusion.2 = bf16[192,128,256]{2,1,0:T(8,128)(2,1)} fusion(bf16[96,128,256]{2,1,0:T(8,128)(2,1)} %bitcast.114, s32[1024]{0:T(1024)S(1)} %pad_clamp_fusion.1), kind=kCustom, calls=%fused_computation.2 | custom fusion | bytes 25166592 | tf_op jit(solution)/shard_map/gather | solution.py:72
  82.3 6.0 all-to-all-start.1
  88.5 5.2 fusion.19
  95.7 2.9 copy.36
  98.5 2.7 copy.49
  101.2 3.2 copy.37
  104.4 282.0 %all-to-all-done.1 = bf16[16,12,128,256]{3,2,1,0:T(8,128)(2,1)} async-done(((bf16[16,12,128,256]{3,2,1,0:T(8,128)(2,1)}), bf16[16,12,128,256]{3,2,1,0:T(8,128)(2,1)}, u32[]{:S(2)}, u32[]{:S(2)}) %all-to-all-start.1) | async-done | bytes 12582944 | tf_op jit(solution)/shard_map/all_to_all | solution.py:72
  386.4 13.7 %gather_fusion.3 = bf16[192,128,256]{2,1,0:T(8,128)(2,1)} fusion(bf16[16,12,128,256]{3,2,1,0:T(8,128)(2,1)} %all-to-all-done.1, s32[192]{0:T(256)S(1)} %reshape.347), kind=kCustom, calls=%fused_computation.3 | custom fusion | bytes 25167360 | tf_op jit(solution)/shard_map/gather | solution.py:73
  400.2 19.4 %all-reduce.3.cloned.1.call-done = bf16[12,4,128,256]{2,1,3,0:T(4,128)(2,1)} async-done(((bf16[12,4,128,256]{2,1,3,0:T(4,128)(2,1)}), bf16[12,4,128,256]{2,1,3,0:T(4,128)(2,1)}) %all-reduce.3.cloned.1.call-update) | async-done | bytes 3145744 | tf_op jit(solution)/shard_map/psum | solution.py:12
  419.5 378.5 %while.10 = (s32[]{:T(128)}, bf16[24,4,128,128]{3,2,1,0:T(8,128)(2,1)}, s32[24]{0:T(128)S(1)}, bf16[12,4,128,256]{2,1,3,0:T(4,128)(2,1)}, bf16[12,16,128,256]{3,...) while((s32[]{:T(128)}, ...), condition=%wide.region_11.12_spmd, body=%wide.region_5.11_spmd.sunk | while | flops 553721984 | bytes 45365560 | solution.py:98
  424.4 2.5 gather_fusion
  432.3 2.2 multiply_reduce_fusion.5
  440.1 2.5 gather_fusion
  448.0 2.2 multiply_reduce_fusion.5
  455.9 2.5 gather_fusion
  463.8 2.2 multiply_reduce_fusion.5
  471.7 2.5 gather_fusion
  479.6 2.2 multiply_reduce_fusion.5
  487.5 2.5 gather_fusion
  495.4 2.2 multiply_reduce_fusion.5
  503.2 2.5 gather_fusion
  511.1 2.2 multiply_reduce_fusion.5
  519.0 2.5 gather_fusion
  526.9 2.2 multiply_reduce_fusion.5
  534.8 2.5 gather_fusion
  542.7 2.2 multiply_reduce_fusion.5
  550.6 2.5 gather_fusion
  558.5 2.2 multiply_reduce_fusion.5
  566.3 2.5 gather_fusion
  574.2 2.2 multiply_reduce_fusion.5
  582.1 2.5 gather_fusion
  590.0 2.2 multiply_reduce_fusion.5
  597.9 2.5 gather_fusion
  605.8 2.2 multiply_reduce_fusion.5
  613.6 2.5 gather_fusion
  621.5 2.2 multiply_reduce_fusion.5
  629.4 2.5 gather_fusion
  637.3 2.2 multiply_reduce_fusion.5
  645.2 2.5 gather_fusion
  653.1 2.2 multiply_reduce_fusion.5
  661.0 2.5 gather_fusion
  668.9 2.2 multiply_reduce_fusion.5
  676.7 2.5 gather_fusion
  692.5 2.5 gather_fusion
  708.3 2.5 gather_fusion
  724.1 2.5 gather_fusion
  739.8 2.5 gather_fusion
  747.7 2.2 multiply_reduce_fusion.5
  755.6 2.5 gather_fusion
  771.4 2.5 gather_fusion
  787.1 2.5 gather_fusion
  798.1 3.6 copy.39
  801.7 3.2 all_to_all.29
  804.9 2.4 copy.40
  807.3 36.4 %all_to_all.36 = bf16[2,512,1536]{1,2,0:T(8,128)(2,1)S(1)} all-to-all(bf16[2,512,1536]{1,2,0:T(8,128)(2,1)S(1)} %copy.40), channel_id=1, replica_groups=mesh['seq'=16,'head'=2] {'head'}, dimensions={0} | all-to-all | bytes 6291456 | tf_op jit(solution)/shard_map/all_to_all | solution.py:101
  843.7 3.0 copy.41
  (383 shorter events, 236.9 us)
Async XLA Ops:
  6.5 1.0 copy-start
  7.6 36.7 %copy-start.4 = (bf16[1024,1536]{1,0:T(8,128)(2,1)S(1)}, bf16[1024,1536]{1,0:T(8,128)(2,1)}, u32[]{:S(2)}) copy-start(bf16[1024,1536]{1,0:T(8,128)(2,1)} %param.9) | copy-start | bytes 9437188
  37.6 33.5 %all-to-all-start = ((s32[16,1,12]{2,1,0:T(1,128)}), s32[16,1,12]{2,1,0:T(1,128)S(1)}, u32[]{:S(2)}, u32[]{:S(2)}) async-start(s32[16,1,12]{2,1,0:T(1,128)} %bitcast.18), calls=%async_computation | async-start | bytes 16384 | tf_op jit(solution)/shard_map/all_to_all | solution.py:71
  57.2 1.7 copy-start.3
  82.3 304.1 %all-to-all-start.1 = ((bf16[16,12,128,256]{3,2,1,0:T(8,128)(2,1)}), bf16[16,12,128,256]{3,2,1,0:T(8,128)(2,1)}, u32[]{:S(2)}, u32[]{:S(2)}) async-start(bf16[16,12,128,256]{3,2,1,0:T(8,128)(2,1)} %bitcast.115), calls=%async_computation.1 | async-start | bytes 25165824 | tf_op jit(solution)/shard_map/all_to_all | solution.py:72
  88.3 331.2 %all-reduce.3.cloned.1.call-start = ((), (), s32[]{:S(2)}) async-start(), calls=%async_computation.3 | async-start | bytes 6291456 | tf_op jit(solution)/shard_map/psum | solution.py:12
  93.8 1.9 copy-start.5
  430.4 1.9 copy-start.2
  446.2 1.9 copy-start.2
  461.9 1.9 copy-start.2
  477.7 1.9 copy-start.2
  493.5 1.9 copy-start.2
  509.2 1.9 copy-start.2
  525.0 1.9 copy-start.2
  540.8 1.9 copy-start.2
  556.6 1.9 copy-start.2
  572.3 1.9 copy-start.2
  588.1 1.9 copy-start.2
  603.9 1.9 copy-start.2
  619.7 1.9 copy-start.2
  635.4 1.9 copy-start.2
  651.2 1.9 copy-start.2
  667.0 1.9 copy-start.2
  682.7 1.9 copy-start.2
  698.5 1.9 copy-start.2
  714.3 1.9 copy-start.2
  730.1 1.9 copy-start.2
  745.8 1.9 copy-start.2
  761.6 1.9 copy-start.2
  777.4 1.9 copy-start.2
  793.2 1.9 copy-start.2
  843.7 3.0 copy-start.1
Sparse Core Ops, SparseCore 0:
  93.9 325.5 all-reduce.2
where the time goes:
time: 864 us; the launch traced here: 854 us
  waiting for transfers between devices  301 us (35%)
  local copies, waits for them, and re-layouts  255 us (30%)
  matrix products  105 us (12%)
  other arithmetic  77.8 us (9%)
  loops' own time  51 us (6%)
  blocking collectives  36.4 us (4%)
  between operations  13.5 us (2%)
  starting transfers between devices  12.9 us (1%)
    all_to_all x1, waiting for transfers between devices, body(): lax.all_to_all(flat_kv[incoming], 'seq', split_axis=0, concat_axis=0, til...  282 us
    gather x24, local copies, waits for them, and re-layouts, per_block(): listed = pool_tiles[head_id][list_blk]  60.6 us
    dot_general x24, matrix products, finish(): jnp.einsum(pattern, weights.astype(jnp.bfloat16), value_part, preferred_e...  53.6 us
    dot_general x24, matrix products, per_block(): jnp.einsum('tqd,tjkd->tjqk', query_blk, keyset[..., :head_size], preferre...  51.5 us
    another operation x1, loops' own time, body(): per_blocks = lax.map(per_block, (query_blocks, list_blocks, head_of))  51 us
    all_to_all x1, blocking collectives, body(): lax.all_to_all(result, 'head', split_axis=0, concat_axis=1, tiled=True)  36.4 us
    squeeze x24, local copies, waits for them, and re-layouts, per_block(): listed = pool_tiles[head_id][list_blk]  31.1 us
    reduce_sum x24, other arithmetic, finish(): row_total = jnp.sum(weights, -1)  30.9 us
  transfers between devices with their start and end apart: 3, of which 2 were waited for; matrix products, arithmetic and copies ran while one was open for 6% of the time, Pallas kernels for 0%

commit v1 on v0

v1 whole, which is shorter than its diff:
```python
import functools

import jax
import jax.numpy as jnp
from jax import lax
from jax.experimental import pallas as pl
from jax.experimental.pallas import tpu as pltpu
from jax.sharding import PartitionSpec as P

TILE = 128
SHARED = 4
FAR = 1e30
LOG2E = 1.4426950408889634
VMEM_BYTES = 56 * 1024 * 1024


def pack_kernel(head_size, codes_ref, keys_ref, values_ref, out_ref, sem):
    def start(i, _):
        code = codes_ref[i]
        slot = code % 65536
        head = code // 65536
        rows = pl.ds(pl.multiple_of(slot * TILE, TILE), TILE)
        cols = pl.ds(pl.multiple_of(head * head_size, head_size), head_size)
        pltpu.make_async_copy(keys_ref.at[rows, cols], out_ref.at[i, 0], sem).start()
        pltpu.make_async_copy(values_ref.at[rows, cols], out_ref.at[i, 1], sem).start()
        return 0

    lax.fori_loop(0, out_ref.shape[0], start, 0)
    pltpu.make_async_copy(out_ref, out_ref, sem).wait()


def pack(codes, keys, values, head_size):
    count = codes.shape[0]
    return pl.pallas_call(
        functools.partial(pack_kernel, head_size),
        out_shape=jax.ShapeDtypeStruct((count, 2, TILE, head_size), keys.dtype),
        in_specs=[
            pl.BlockSpec(memory_space=pltpu.SMEM),
            pl.BlockSpec(memory_space=pl.ANY),
            pl.BlockSpec(memory_space=pl.ANY),
        ],
        out_specs=pl.BlockSpec(memory_space=pl.ANY),
        scratch_shapes=[pltpu.SemaphoreType.DMA],
        cost_estimate=pl.CostEstimate(
            flops=0, bytes_accessed=4 * count * 2 * TILE * head_size, transcendentals=0
        ),
        name="pack_tiles",
    )(codes, keys, values)


def shared_kernel(scale, block, q_ref, kv_ref, qt_ref, acc_ref, m_ref, l_ref):
    rows = q_ref.shape[0]
    head_size = q_ref.shape[1]
    qt_ref[0] = q_ref[...].T
    k = kv_ref[0, :, 0].reshape(-1, head_size)
    vt = kv_ref[0, :, 1].reshape(-1, head_size).T
    for start in range(0, rows, block):
        cols = slice(start, start + block)
        s = jnp.dot(k, qt_ref[0, :, cols], preferred_element_type=jnp.float32)
        m = jnp.max(s, 0, keepdims=True) * scale
        p = jnp.exp2(s * scale - m)
        m_ref[0, :, cols] = m
        l_ref[0, :, cols] = jnp.sum(p, 0, keepdims=True)
        acc_ref[0, :, cols] = jnp.dot(
            vt, p.astype(jnp.bfloat16), preferred_element_type=jnp.float32
        )


def shared_part(queries, shared, head_count, head_size, scale):
    rows = queries.shape[0]
    state = jax.ShapeDtypeStruct((head_count, 1, rows), jnp.float32)
    stat_spec = pl.BlockSpec((1, 1, rows), lambda h: (h, 0, 0))
    wide_spec = pl.BlockSpec((1, head_size, rows), lambda h: (h, 0, 0))
    return pl.pallas_call(
        functools.partial(shared_kernel, scale, min(256, rows)),
        grid=(head_count,),
        out_shape=(
            jax.ShapeDtypeStruct((head_count, head_size, rows), jnp.bfloat16),
            jax.ShapeDtypeStruct((head_count, head_size, rows), jnp.float32),
            state,
            state,
        ),
        in_specs=[
            pl.BlockSpec((rows, head_size), lambda h: (0, h)),
            pl.BlockSpec((1, SHARED, 2, TILE, head_size), lambda h: (h, 0, 0, 0, 0)),
        ],
        out_specs=(wide_spec, wide_spec, stat_spec, stat_spec),
        compiler_params=pltpu.CompilerParams(vmem_limit_bytes=VMEM_BYTES),
        cost_estimate=pl.CostEstimate(
            flops=4 * head_count * rows * SHARED * TILE * head_size,
            bytes_accessed=16 * head_count * rows * head_size,
            transcendentals=head_count * rows * SHARED * TILE,
        ),
        name="shared_tiles",
    )(queries, shared)


def pool_kernel(
    scale, block, last, where_ref, entry_ref, count_ref,
    qt_ref, tiles_ref, bias_ref, acc_in, m_in, l_in, *rest,
):
    if last:
        out_ref, acc_ref, m_ref, l_ref = rest
    else:
        acc_ref, m_ref, l_ref = rest
    head = pl.program_id(0)
    rows = qt_ref.shape[2]
    acc_ref[...] = acc_in[...]
    m_ref[...] = m_in[...]
    l_ref[...] = l_in[...]

    def one(i, _):
        tile = where_ref[head, i]
        entry = entry_ref[head, i]
        k = tiles_ref[tile, 0]
        vt = tiles_ref[tile, 1].T
        for start in range(0, rows, block):
            cols = slice(start, start + block)
            s = jnp.dot(k, qt_ref[0, :, cols], preferred_element_type=jnp.float32)
            bias = bias_ref[0, pl.ds(entry, 1), cols]
            top = jnp.max(s, 0, keepdims=True) * scale + bias
            m_old = m_ref[0, :, cols]
            m_new = jnp.maximum(m_old, top)
            alpha = jnp.exp2(m_old - m_new)
            p = jnp.exp2(s * scale - (m_new - bias))
            m_ref[0, :, cols] = m_new
            l_ref[0, :, cols] = l_ref[0, :, cols] * alpha + jnp.sum(p, 0, keepdims=True)
            acc_ref[0, :, cols] = acc_ref[0, :, cols] * alpha + jnp.dot(
                vt, p.astype(jnp.bfloat16), preferred_element_type=jnp.float32
            )
        return 0

    lax.fori_loop(0, count_ref[head], one, 0)
    if last:
        for start in range(0, rows, block):
            cols = slice(start, start + block)
            out = (acc_ref[0, :, cols] / l_ref[0, :, cols]).astype(jnp.bfloat16)
            out_ref[cols, :] = out.T


def pool_part(tables, qt, tiles, bias, acc, m, l, scale, last):
    head_count, head_size, rows = qt.shape
    pool_len = bias.shape[1]
    stat_spec = pl.BlockSpec((1, 1, rows), lambda h, *_: (h, 0, 0))
    wide_spec = pl.BlockSpec((1, head_size, rows), lambda h, *_: (h, 0, 0))
    if last:
        out_shape = jax.ShapeDtypeStruct((rows, head_count * head_size), jnp.bfloat16)
        out_specs = pl.BlockSpec((rows, head_size), lambda h, *_: (0, h))
        scratch = [
            pltpu.VMEM((1, head_size, rows), jnp.float32),
            pltpu.VMEM((1, 1, rows), jnp.float32),
            pltpu.VMEM((1, 1, rows), jnp.float32),
        ]
    else:
        out_shape = tuple(jax.ShapeDtypeStruct(a.shape, a.dtype) for a in (acc, m, l))
        out_specs = (wide_spec, stat_spec, stat_spec)
        scratch = []
    work = tiles.shape[0] * rows * TILE
    return pl.pallas_call(
        functools.partial(pool_kernel, scale, min(256, rows), last),
        grid_spec=pltpu.PrefetchScalarGridSpec(
            num_scalar_prefetch=3,
            grid=(head_count,),
            in_specs=[
                wide_spec,
                pl.BlockSpec(tiles.shape, lambda h, *_: (0, 0, 0, 0), pipeline_mode=pl.Buffered(1)),
                pl.BlockSpec((1, pool_len, rows), lambda h, *_: (h, 0, 0)),
                wide_spec,
                stat_spec,
                stat_spec,
            ],
            out_specs=out_specs,
            scratch_shapes=scratch,
        ),
        out_shape=out_shape,
        compiler_params=pltpu.CompilerParams(vmem_limit_bytes=VMEM_BYTES),
        cost_estimate=pl.CostEstimate(
            flops=4 * work * head_size,
            bytes_accessed=10 * head_count * rows * head_size,
            transcendentals=work,
        ),
        name="pool_tiles",
    )(*tables, qt, tiles, bias, acc, m, l)


def spread_shared(pieces, axis):
    count = lax.axis_size(axis)
    me = lax.axis_index(axis)
    step = count // 2
    while step >= 1:
        pairs = [(i, i + step) for i in range(0, count, 2 * step)]
        got = lax.ppermute(pieces[step:], axis, pairs)
        pieces = jnp.where(me % (2 * step) == step, got, pieces[:step])
        step //= 2
    return pieces


def chunk_edges(total):
    if total < 6:
        return [0, total]
    last = max(1, total // 12)
    return [0, (total * 5) // 12, (total * 9) // 12, total - last, total]


def body(queries, keys, values, tile_pool, tile_lists, key_slot):
    seq_count = lax.axis_size("seq")
    me = lax.axis_index("seq")
    head_count, pool_total = tile_pool.shape
    pool_len = pool_total // seq_count
    rows, width = queries.shape
    head_size = width // head_count
    tile_count = rows // TILE
    bound = (head_count * pool_len + seq_count - 1) // seq_count
    scale = head_size ** (-0.5) * LOG2E
    entries = head_count * pool_len

    storage = key_slot[tile_pool].reshape(head_count, seq_count, pool_len)
    by_reader = storage.transpose(1, 0, 2).reshape(seq_count, entries)
    ids = jnp.arange(entries, dtype=jnp.int32)
    before = (ids[:, None] < ids[None, :]).astype(jnp.bfloat16)
    wanted = by_reader // tile_count == me
    place = jnp.dot(
        wanted.astype(jnp.bfloat16), before, preferred_element_type=jnp.float32
    ).astype(jnp.int32)
    place = jnp.where(wanted, place, -1)
    code = (ids // pool_len)[None, :] * 65536 + by_reader % tile_count
    slots = jnp.arange(bound, dtype=jnp.int32)
    send = jnp.sum(
        jnp.where(place[:, None, :] == slots[None, :, None], code[:, None, :], 0), -1
    )

    own = lax.dynamic_index_in_dim(by_reader, me, 0, keepdims=False)
    owner = own // tile_count
    same = (owner[:, None] == owner[None, :]) & (ids[:, None] < ids[None, :])
    position = jnp.sum(same.astype(jnp.int32), 0)

    edges = chunk_edges(bound)
    chunks = []
    for lo, hi in zip(edges[:-1], edges[1:]):
        part = pack(send[:, lo:hi].reshape(-1), keys, values, head_size)
        part = part.reshape(seq_count, hi - lo, 2, TILE, head_size)
        got = lax.all_to_all(part, "seq", split_axis=0, concat_axis=0, tiled=True)
        chunks.append(got.reshape(-1, 2, TILE, head_size))

    head_ids = jnp.arange(head_count, dtype=jnp.int32)
    shared_codes = (
        head_ids[:, None] * 65536 + jnp.arange(SHARED, dtype=jnp.int32)[None, :]
    ).reshape(-1)
    shared_own = pack(shared_codes, keys, values, head_size)
    pieces = shared_own.reshape(seq_count, -1, head_size)
    piece = spread_shared(pieces, "seq")
    shared = lax.all_gather(piece, "seq", axis=0, tiled=True).reshape(
        head_count, SHARED, 2, TILE, head_size
    )

    listed = jnp.any(
        tile_lists[:, :, :, None] == jnp.arange(pool_len, dtype=jnp.int32), 2
    )
    bias = jnp.where(listed, 0.0, -FAR).astype(jnp.float32).transpose(0, 2, 1)
    bias = jnp.repeat(bias, TILE, axis=2)

    qt, acc, m, l = shared_part(queries, shared, head_count, head_size, scale)
    position = position.reshape(head_count, pool_len)
    owner = owner.reshape(head_count, pool_len)
    pool_ids = jnp.arange(pool_len, dtype=jnp.int32)
    state = (acc, m, l)
    for c, (lo, hi) in enumerate(zip(edges[:-1], edges[1:])):
        here = (position >= lo) & (position < hi)
        rank = jnp.sum(
            (here[:, :, None] & (pool_ids[:, None] < pool_ids[None, :])).astype(jnp.int32), 1
        )
        rank = jnp.where(here, rank, -1)
        hit = rank[:, None, :] == pool_ids[None, :, None]
        entry = jnp.sum(jnp.where(hit, pool_ids, 0), -1)
        where = owner * (hi - lo) + position - lo
        where = jnp.sum(jnp.where(hit, where[:, None, :], 0), -1)
        count = jnp.sum(here.astype(jnp.int32), 1)
        last = c == len(edges) - 2
        state = pool_part(
            (where, entry, count), qt, chunks[c], bias, *state, scale, last
        )
    return lax.all_to_all(state, "head", split_axis=0, concat_axis=1, tiled=True)


def solution(mesh):
    return jax.shard_map(
        body,
        mesh=mesh,
        in_specs=(
            P("seq", "head"),
            P("seq", "head"),
            P("seq", "head"),
            P("head", None),
            P("head", "seq", None),
            P(),
        ),
        out_specs=P(("seq", "head"), None),
        check_vma=False,
    )
```

time: 864 us -> 807 us (0.934)
  Pallas kernels: 0 us -> 636 us
  waiting for transfers between devices: 301 us -> 40 us
  local copies, waits for them, and re-layouts: 255 us -> 34.3 us
  matrix products: 105 us -> 0.15 us
  other arithmetic: 77.8 us -> 7.84 us
  loops' own time: 51 us -> 0 us
  starting transfers between devices: 12.9 us -> 31.4 us
    pallas_call x0 -> x10, Pallas kernels: none -> 636 us  [the longest x5 485 us: pack(): pl.pallas_call(functools.partial(pack_kernel, head_size), out_shape=jax.S...]
    all_to_all x2 -> x4, waiting for transfers between devices: 282 us -> 0.01 us  [body(): got = lax.all_to_all(part, 'seq', split_axis=0, concat_axis=0, tiled=True)]
    dot_general x48 -> x1, matrix products: 105 us -> 0.15 us  [body(): jnp.dot(wanted.astype(jnp.bfloat16), before, preferred_element_type=jnp.f...]
    gather x28 -> x1, local copies, waits for them, and re-layouts: 87 us -> 18.7 us  [body(): storage = key_slot[tile_pool].reshape(head_count, seq_count, pool_len)]
    another operation x1 -> x0, loops' own time: 51 us -> none  [body(): per_blocks = lax.map(per_block, (query_blocks, list_blocks, head_of))]
    dynamic_slice x72 -> x2, local copies, waits for them, and re-layouts: 45.1 us -> 1.19 us  [body(): own = lax.dynamic_index_in_dim(by_reader, me, 0, keepdims=False)]
    ppermute x0 -> x4, waiting for transfers between devices: none -> 39.9 us  [spread_shared(): got = lax.ppermute(pieces[step:], axis, pairs)]
    squeeze x24 -> x1, local copies, waits for them, and re-layouts: 31.1 us -> 0.08 us  [body(): own = lax.dynamic_index_in_dim(by_reader, me, 0, keepdims=False)]
  transfers between devices with their start and end apart: 3 -> 9, of which waited for: 2 -> 1; matrix products, arithmetic and copies ran while one was open for 6% -> 2% of each run, Pallas kernels for 0% -> 69%
where the time goes in v1:
time: 807 us; the launch traced here: 802 us
  Pallas kernels  636 us (79%)
  waiting for transfers between devices  40 us (5%)
  blocking collectives  38.3 us (5%)
  local copies, waits for them, and re-layouts  34.3 us (4%)
  starting transfers between devices  31.4 us (4%)
  between operations  13.8 us (2%)
    pallas_call x5, Pallas kernels, pack(): pl.pallas_call(functools.partial(pack_kernel, head_size), out_shape=jax.S...  485 us
    pallas_call x4, Pallas kernels, pool_part(): pl.pallas_call(functools.partial(pool_kernel, scale, min(256, rows), last...  127 us
    ppermute x4, waiting for transfers between devices, spread_shared(): got = lax.ppermute(pieces[step:], axis, pairs)  39.9 us
    all_to_all x1, blocking collectives, body(): lax.all_to_all(state, 'head', split_axis=0, concat_axis=1, tiled=True)  38.3 us
    all_to_all x4, starting transfers between devices, body(): got = lax.all_to_all(part, 'seq', split_axis=0, concat_axis=0, tiled=True)  27.8 us
    pallas_call x1, Pallas kernels, shared_part(): pl.pallas_call(functools.partial(shared_kernel, scale, min(256, rows)), g...  24.5 us
    gather x1, local copies, waits for them, and re-layouts, body(): storage = key_slot[tile_pool].reshape(head_count, seq_count, pool_len)  18.7 us
  transfers between devices with their start and end apart: 9, of which 1 were waited for; matrix products, arithmetic and copies ran while one was open for 2% of the time, Pallas kernels for 69%

profile of v1, /device:TPU:9, one launch (start us, length us, event | category | flops | bytes accessed | tf_op | source)
XLA Modules:
  0.0 802.2 jit_solution(6777591008758539901)
XLA Ops:
  6.5 0.7 compare_select_fusion
  7.3 18.7 %gather_fusion = s32[3072]{0:T(1024)S(1)} fusion(s32[128]{0:T(128)S(1)} %copy-done, s32[3072]{0:T(1024)S(1)} %broadcast_clamp_fusion), kind=kCustom, calls=%fused_computation | custom fusion | bytes 36864 | tf_op jit(solution)/shard_map/gather | solution.py:217
  26.0 0.1 reshape.331
  26.1 0.1 reshape.332
  26.2 0.2 fusion
  26.4 0.3 select_reduce_fusion
  26.7 0.1 copy.17
  26.7 0.7 reshape.339.codes_ref
  27.4 65.3 %pack_tiles.7 = bf16[32,2,128,128]{3,2,1,0:T(8,128)(2,1)} custom-call(s32[32]{0:T(128)} %reshape.339.codes_ref, bf16[1024,1536]{1,0:T(8,128)(2,1)} %keys_ref.9, bf16[1024,1536]{1,0:T(8,128)(2,1)} %values_ref.9), custom_call_target="tpu_custom_call" | custom-call | bytes 4194304 | tf_op jit(solution)/shard_map/pack_tiles/pallas_call | solution.py:34
  92.7 6.6 all-to-all-start.1
  99.3 0.1 copy.18
  99.4 0.7 reshape.342.codes_ref
  100.1 128.8 %pack_tiles.8 = bf16[64,2,128,128]{3,2,1,0:T(8,128)(2,1)} custom-call(s32[64]{0:T(128)} %reshape.342.codes_ref, bf16[1024,1536]{1,0:T(8,128)(2,1)} %keys_ref.9, bf16[1024,1536]{1,0:T(8,128)(2,1)} %values_ref.9), custom_call_target="tpu_custom_call" | custom-call | bytes 8388608 | tf_op jit(solution)/shard_map/pack_tiles/pallas_call | solution.py:34
  229.0 1.4 copy-done.2
  230.4 6.0 all-to-all-start.2
  236.4 0.1 copy.19
  236.5 0.6 reshape.345.codes_ref
  237.1 160.6 %pack_tiles.9 = bf16[80,2,128,128]{3,2,1,0:T(8,128)(2,1)} custom-call(s32[80]{0:T(128)} %reshape.345.codes_ref, bf16[1024,1536]{1,0:T(8,128)(2,1)} %keys_ref.9, bf16[1024,1536]{1,0:T(8,128)(2,1)} %values_ref.9), custom_call_target="tpu_custom_call" | custom-call | bytes 10485760 | tf_op jit(solution)/shard_map/pack_tiles/pallas_call | solution.py:34
  397.7 6.0 all-to-all-start.3
  403.7 0.0 all-gather.2.cloned.1.call-start
  403.8 0.1 iota_add_fusion
  403.9 0.7 add.142.codes_ref
  404.5 97.1 %pack_tiles.5 = bf16[48,2,128,128]{3,2,1,0:T(8,128)(2,1)} custom-call(s32[48]{0:T(128)} %add.142.codes_ref, bf16[1024,1536]{1,0:T(8,128)(2,1)} %keys_ref.9, bf16[1024,1536]{1,0:T(8,128)(2,1)} %values_ref.9), custom_call_target="tpu_custom_call" | custom-call | bytes 6291456 | tf_op jit(solution)/shard_map/pack_tiles/pallas_call | solution.py:34
  501.6 3.4 fusion.25
  505.0 0.7 collective-permute-start
  505.8 0.0 copy-start.4
  505.8 1.1 copy-done.4
  506.9 0.3 broadcast_select_fusion
  507.2 0.1 slice.60
  507.3 0.0 copy-start.5
  507.3 0.8 collective-permute-start.1
  508.1 0.1 slice_select_fusion
  508.3 0.7 collective-permute-start.2
  509.1 1.3 collective-permute-start.3
  510.4 39.9 %collective-permute-done.3 = bf16[1,768,128]{2,1,0:T(8,128)(2,1)S(1)} collective-permute-done((bf16[1,768,128]{2,1,0:T(8,128)(2,1)S(1)}, bf16[1,768,128]{2,1,0:T(8,128)(2,1)S(1)}, u32[]{:S(2)}, u32[]{:S(2)}) %collective-permute-start.3) | collective-permute-done | bytes 196640 | tf_op jit(solution)/shard_map/ppermute | solution.py:192
  550.3 0.7 slice_select_fusion.2
  551.0 0.0 all-gather.2.cloned.1.call-update
  551.0 0.5 broadcast.416
  551.6 0.7 fusion.24
  552.3 0.1 convert_reduce_fusion
  552.4 0.1 reshape.333
  552.4 0.1 squeeze.7
  552.5 0.2 copy.15
  552.7 0.2 fusion.1
  552.9 0.1 copy.16
  553.0 0.3 broadcast_in_dim.134
  553.3 1.0 reshape.338.bias_ref
  554.3 0.5 slice_bitcast_fusion.codes_ref
  554.8 33.5 %pack_tiles.6 = bf16[16,2,128,128]{3,2,1,0:T(8,128)(2,1)} custom-call(s32[16]{0:T(128)} %slice_bitcast_fusion.codes_ref, bf16[1024,1536]{1,0:T(8,128)(2,1)} %keys_ref.9, bf16[1024,1536]{1,0:T(8,128)(2,1)} %values_ref.9), custom_call_target="tpu_custom_call" | custom-call | bytes 2097152 | tf_op jit(solution)/shard_map/pack_tiles/pallas_call | solution.py:34
  588.4 0.8 multiply_add_fusion
  589.2 0.2 convert_reduce_fusion.1
  589.4 1.1 select_reduce_fusion.1
  590.5 9.2 %all-to-all-start = ((bf16[16,1,2,128,128]{4,3,2,1,0:T(8,128)(2,1)}), bf16[16,1,2,128,128]{4,3,2,1,0:T(8,128)(2,1)S(1)}, u32[]{:S(2)}, u32[]{:S(2)}) async-start(bf16[16,1,2,128,128]{4,3,2,1,0:T(8,128)(2,1)} %bitcast.34), calls=%async_computation | async-start | bytes 2097152 | tf_op jit(solution)/shard_map/all_to_all | solution.py:242
  599.7 1.1 select_reduce_fusion.3
  600.7 1.1 select_reduce_fusion.5
  601.8 1.1 select_reduce_fusion.7
  602.9 24.5 %shared_tiles.1 = (bf16[12,128,1024]{2,1,0:T(8,128)(2,1)}, f32[12,128,1024]{2,1,0:T(8,128)}, f32[12,1,1024]{2,1,0:T(1,128)}, f32[12,1,1024]{2,1,0:T(1,128)}) custom-call(bf16[1024,1536]{1,0:T(8,128)(2,1)} %q_ref.1, bf16[12,4,2,128,128]{4,3,2,1,0:T(8,128)(2,1)} %bitcast.38), custom_call_target="tpu_custom_call" | custom-call | flops 3221225472 | bytes 25165824 | tf_op jit(solution)/shard_map/shared_tiles/pallas_call | solution.py:74
  627.4 46.7 %pool_tiles.4 = (f32[12,128,1024]{2,1,0:T(8,128)}, f32[12,1,1024]{2,1,0:T(1,128)}, f32[12,1,1024]{2,1,0:T(1,128)}) custom-call(s32[12,16]{1,0:T(8,128)} %get-tuple-element.32.where_ref, s32[12,16]{1,0:T(8,128)} %get-tuple-element.31.entry_ref, s32[12]{0:T(128)} %get-tuple-element.61.count_ref, bf16[12,128,1024]{2,1,0:T(8,128)(2,1)} %get-tuple-element.18.qt_ref, ...), custom_call_target="tpu_custom_call" | custom-call | flops 5368709120 | bytes 15728640 | tf_op jit(solution)/shard_map/pool_tiles/pallas_call | solution.py:159
  674.1 37.5 %pool_tiles.5 = (f32[12,128,1024]{2,1,0:T(8,128)}, f32[12,1,1024]{2,1,0:T(1,128)}, f32[12,1,1024]{2,1,0:T(1,128)}) custom-call(s32[12,16]{1,0:T(8,128)} %get-tuple-element.34.where_ref, s32[12,16]{1,0:T(8,128)} %get-tuple-element.33.entry_ref, s32[12]{0:T(128)} %get-tuple-element.59.count_ref, bf16[12,128,1024]{2,1,0:T(8,128)(2,1)} %get-tuple-element.18.qt_ref, ...), custom_call_target="tpu_custom_call" | custom-call | flops 4294967296 | bytes 15728640 | tf_op jit(solution)/shard_map/pool_tiles/pallas_call | solution.py:159
  711.6 24.2 %pool_tiles.6 = (f32[12,128,1024]{2,1,0:T(8,128)}, f32[12,1,1024]{2,1,0:T(1,128)}, f32[12,1,1024]{2,1,0:T(1,128)}) custom-call(s32[12,16]{1,0:T(8,128)} %get-tuple-element.36.where_ref, s32[12,16]{1,0:T(8,128)} %get-tuple-element.35.entry_ref, s32[12]{0:T(128)} %get-tuple-element.63.count_ref, bf16[12,128,1024]{2,1,0:T(8,128)(2,1)} %get-tuple-element.18.qt_ref, ...), custom_call_target="tpu_custom_call" | custom-call | flops 2147483648 | bytes 15728640 | tf_op jit(solution)/shard_map/pool_tiles/pallas_call | solution.py:159
  735.8 1.0 copy-done.3
  736.8 18.2 %pool_tiles.7 = bf16[1024,1536]{1,0:T(8,128)(2,1)} custom-call(s32[12,16]{1,0:T(8,128)} %get-tuple-element.38.where_ref, s32[12,16]{1,0:T(8,128)} %get-tuple-element.37.entry_ref, s32[12]{0:T(128)} %get-tuple-element.65.count_ref, bf16[12,128,1024]{2,1,0:T(8,128)(2,1)} %get-tuple-element.18.qt_ref, bf16[16,2,128,128]{3,2,1,0:T(8,128)(2,1)} %bitcast.33, ...), custom_call_target="tpu_custom_call" | custom-call | flops 1073741824 | bytes 15728640 | tf_op jit(solution)/shard_map/pool_tiles/pallas_call | solution.py:159
  754.9 38.3 %all_to_all.39 = bf16[2,512,1536]{2,1,0:T(8,128)(2,1)S(1)} all-to-all(bf16[2,512,1536]{2,1,0:T(8,128)(2,1)} %bitcast.28), channel_id=1, replica_groups=mesh['seq'=16,'head'=2] {'head'}, dimensions={0} | all-to-all | bytes 6291456 | tf_op jit(solution)/shard_map/all_to_all | solution.py:282
  793.3 2.1 copy.21
  (33 shorter events, 0.2 us)
Async XLA Ops:
  6.5 0.8 copy-start
  92.7 136.2 %all-to-all-start.1 = ((bf16[16,2,2,128,128]{4,3,2,1,0:T(8,128)(2,1)}), bf16[16,2,2,128,128]{4,3,2,1,0:T(8,128)(2,1)S(1)}, u32[]{:S(2)}, u32[]{:S(2)}) async-start(bf16[16,2,2,128,128]{4,3,2,1,0:T(8,128)(2,1)} %bitcast.31), calls=%async_computation.1 | async-start | bytes 4194304 | tf_op jit(solution)/shard_map/all_to_all | solution.py:242
  229.0 1.4 copy-start.2
  230.4 167.3 %all-to-all-start.2 = ((bf16[16,4,2,128,128]{4,3,2,1,0:T(8,128)(2,1)}), bf16[16,4,2,128,128]{4,3,2,1,0:T(8,128)(2,1)}, u32[]{:S(2)}, u32[]{:S(2)}) async-start(bf16[16,4,2,128,128]{4,3,2,1,0:T(8,128)(2,1)} %bitcast.27), calls=%async_computation.2 | async-start | bytes 8388608 | tf_op jit(solution)/shard_map/all_to_all | solution.py:242
  397.7 192.8 %all-to-all-start.3 = ((bf16[16,5,2,128,128]{4,3,2,1,0:T(8,128)(2,1)}), bf16[16,5,2,128,128]{4,3,2,1,0:T(8,128)(2,1)}, u32[]{:S(2)}, u32[]{:S(2)}) async-start(bf16[16,5,2,128,128]{4,3,2,1,0:T(8,128)(2,1)} %bitcast.26), calls=%async_computation.3 | async-start | bytes 10485760 | tf_op jit(solution)/shard_map/all_to_all | solution.py:242
  403.7 199.2 %all-gather.2.cloned.1.call-start = ((), (), s32[]{:S(2)}) async-start(), calls=%async_computation.5 | async-start | bytes 3342336 | tf_op jit(solution)/shard_map/all_gather | solution.py:252
  505.0 0.8 collective-permute-start
  505.8 1.1 copy-start.4
  507.3 45.3 %copy-start.5 = (s32[12,8,12]{2,1,0:T(8,128)S(1)}, s32[12,8,12]{2,1,0:T(8,128)}, u32[]{:S(2)}) copy-start(s32[12,8,12]{2,1,0:T(8,128)} %param.10) | copy-start | bytes 13828
  507.3 0.9 collective-permute-start.1
  508.3 0.7 collective-permute-start.2
  509.1 41.2 %collective-permute-start.3 = (bf16[1,768,128]{2,1,0:T(8,128)(2,1)S(1)}, bf16[1,768,128]{2,1,0:T(8,128)(2,1)S(1)}, u32[]{:S(2)}, u32[]{:S(2)}) collective-permute-start(bf16[1,768,128]{2,1,0:T(8,128)(2,1)S(1)} %slice.64), channel_id=1, source_target_pairs={{0,2},{4,6},{8,10},{12,14},{16,18},{20,22},{24,26},{28,30},{1,3},{... | collective-permute-start | bytes 589832 | tf_op jit(solution)/shard_map/ppermute | solution.py:192
  590.5 145.3 %all-to-all-start = ((bf16[16,1,2,128,128]{4,3,2,1,0:T(8,128)(2,1)}), bf16[16,1,2,128,128]{4,3,2,1,0:T(8,128)(2,1)S(1)}, u32[]{:S(2)}, u32[]{:S(2)}) async-start(bf16[16,1,2,128,128]{4,3,2,1,0:T(8,128)(2,1)} %bitcast.34), calls=%async_computation | async-start | bytes 2097152 | tf_op jit(solution)/shard_map/all_to_all | solution.py:242
  735.8 1.0 copy-start.3
  793.3 2.1 copy-start.1
Sparse Core Ops, SparseCore 0:
  551.1 50.0 all-gather.1

commit v2 on v0

v2 whole, which is shorter than its diff:
```python
import functools

import jax
import jax.numpy as jnp
from jax import lax
from jax.experimental import pallas as pl
from jax.experimental.pallas import tpu as pltpu
from jax.sharding import PartitionSpec as P

TILE = 128
SHARED = 4
FAR = 1e30
LOG2E = 1.4426950408889634
VMEM_BYTES = 56 * 1024 * 1024


def pack_kernel(lo, bound, head_size, codes_ref, order_ref, keys_ref, values_ref, *out_refs):
    at = lo
    for out_ref in out_refs:
        readers = out_ref.shape[0] // bound

        def one(i, _):
            code = codes_ref[order_ref[at + i // bound] * bound + i % bound]
            rows = pl.ds(pl.multiple_of(code % 65536 * TILE, TILE), TILE)
            cols = pl.ds(pl.multiple_of(code // 65536 * head_size, head_size), head_size)
            out_ref[i, 0] = keys_ref[rows, cols]
            out_ref[i, 1] = values_ref[rows, cols]
            return 0

        lax.fori_loop(0, readers * bound, one, 0)
        at += readers


def pack(codes, order, keys, values, lo, sizes, bound, head_size):
    shapes = [
        jax.ShapeDtypeStruct((n * bound, 2, TILE, head_size), keys.dtype) for n in sizes
    ]
    whole = pl.BlockSpec(keys.shape, lambda i, *_: (0, 0))
    return pl.pallas_call(
        functools.partial(pack_kernel, lo, bound, head_size),
        grid_spec=pltpu.PrefetchScalarGridSpec(
            num_scalar_prefetch=2,
            grid=(1,),
            in_specs=[whole, whole],
            out_specs=[pl.BlockSpec(t.shape, lambda i, *_: (0, 0, 0, 0)) for t in shapes],
        ),
        out_shape=shapes,
        compiler_params=pltpu.CompilerParams(vmem_limit_bytes=VMEM_BYTES),
        name="pack_tiles",
    )(codes, order, keys, values)


def absorb(scale, block, k, vt, bias_row, qt_ref, acc_ref, m_ref, l_ref):
    for start in range(0, qt_ref.shape[2], block):
        cols = slice(start, start + block)
        s = jnp.dot(k, qt_ref[0, :, cols], preferred_element_type=jnp.float32)
        top = jnp.max(s, 0, keepdims=True) * scale
        m_old = m_ref[0, :, cols]
        if bias_row is None:
            m_new = jnp.maximum(m_old, top)
            shift = m_new
        else:
            bias = bias_row[:, cols]
            m_new = jnp.maximum(m_old, top + bias)
            shift = m_new - bias
        alpha = jnp.exp2(m_old - m_new)
        p = jnp.exp2(s * scale - shift)
        m_ref[0, :, cols] = m_new
        l_ref[0, :, cols] = l_ref[0, :, cols] * alpha + jnp.sum(p, 0, keepdims=True)
        acc_ref[0, :, cols] = acc_ref[0, :, cols] * alpha + jnp.dot(
            vt, p.astype(jnp.bfloat16), preferred_element_type=jnp.float32
        )


def shared_kernel(scale, block, qt_ref, k_ref, v_ref, acc_in, m_in, l_in, acc_ref, m_ref, l_ref):
    acc_ref[...] = acc_in[...]
    m_ref[...] = m_in[...]
    l_ref[...] = l_in[...]
    for j in range(SHARED):
        rows = slice(j * TILE, (j + 1) * TILE)
        absorb(
            scale, block, k_ref[rows, :], v_ref[rows, :].T, None, qt_ref, acc_ref, m_ref, l_ref
        )


def shared_part(qt, shared, state, scale):
    head_count, head_size, rows = qt.shape
    stat_spec = pl.BlockSpec((1, 1, rows), lambda h: (h, 0, 0))
    wide_spec = pl.BlockSpec((1, head_size, rows), lambda h: (h, 0, 0))
    keys = SHARED * TILE
    return pl.pallas_call(
        functools.partial(shared_kernel, scale, min(256, rows)),
        grid=(head_count,),
        out_shape=[jax.ShapeDtypeStruct(a.shape, a.dtype) for a in state],
        in_specs=[
            wide_spec,
            pl.BlockSpec((keys, head_size), lambda h: (0, h)),
            pl.BlockSpec((keys, head_size), lambda h: (1, h)),
            wide_spec,
            stat_spec,
            stat_spec,
        ],
        out_specs=[wide_spec, stat_spec, stat_spec],
        compiler_params=pltpu.CompilerParams(vmem_limit_bytes=VMEM_BYTES),
        name="shared_tiles",
    )(qt, shared, shared, *state)


def pool_kernel(
    scale, block, parts, first, split, head_lo,
    place_ref, entry_ref, count_ref, side_ref, q_ref, bias_ref, *refs,
):
    tiles = refs[:parts]
    held_ref, sems = refs[-2:]
    refs = refs[parts:-2]
    head = pl.program_id(0) + head_lo
    copies = []
    at = 0
    for k, tiles_ref in enumerate(tiles):
        span = pl.ds(at, tiles_ref.shape[0])
        copies.append(pltpu.make_async_copy(tiles_ref, held_ref.at[span], sems.at[k]))
        at += tiles_ref.shape[0]

    @pl.when(pl.program_id(0) == 0)
    def _():
        for copy in copies:
            copy.start()

    if first:
        qt_ref, acc_ref, m_ref, l_ref = refs
        qt_ref[0] = q_ref[...].T
        acc_ref[...] = jnp.zeros_like(acc_ref)
        m_ref[...] = jnp.full_like(m_ref, -0.5 * FAR)
        l_ref[...] = jnp.zeros_like(l_ref)
    else:
        qt_ref = q_ref
        acc_in, m_in, l_in = refs[:3]
        acc_ref, m_ref, l_ref = refs[-3:]
        acc_ref[...] = acc_in[...]
        m_ref[...] = m_in[...]
        l_ref[...] = l_in[...]

    @pl.when(pl.program_id(0) == 0)
    def _():
        for copy in copies:
            copy.wait()

    def one(i):
        place = place_ref[head, i]
        entry = entry_ref[head, i]
        absorb(
            scale, block, held_ref[place, 0], held_ref[place, 1].T,
            bias_ref[0, pl.ds(entry, 1), :], qt_ref, acc_ref, m_ref, l_ref,
        )

    def two(i, _):
        one(2 * i)
        one(2 * i + 1)
        return 0

    total = count_ref[head]
    lax.fori_loop(0, total // 2, two, 0)

    @pl.when(total % 2 == 1)
    def _():
        one(total - 1)

    if split:
        out_refs, whole = refs[3:-4], refs[-4]
        rows = qt_ref.shape[2]
        for start in range(0, rows, block):
            cols = slice(start, start + block)
            out = (acc_ref[0, :, cols] * (1.0 / l_ref[0, :, cols])).astype(jnp.bfloat16)
            whole[cols, :] = out.T
        if split == 1:
            out_refs[0][...] = whole[...]
        else:
            half = rows // split
            for ref, side in zip(out_refs, (side_ref[0], 1 - side_ref[0])):
                ref[...] = whole[pl.ds(pl.multiple_of(side * half, half), half), :]


def pool_part(tables, q, tiles, bias, state, scale, head_size, split=0, heads=None):
    first = state is None
    head_count, pool_len, rows = bias.shape
    lo, hi = heads or (0, head_count)
    count = hi - lo
    stat_spec = pl.BlockSpec((1, 1, rows), lambda h, *_: (h + lo, 0, 0))
    wide_spec = pl.BlockSpec((1, head_size, rows), lambda h, *_: (h + lo, 0, 0))
    acc = jax.ShapeDtypeStruct((head_count, head_size, rows), jnp.float32)
    stat = jax.ShapeDtypeStruct((head_count, 1, rows), jnp.float32)
    q_spec = pl.BlockSpec((rows, head_size), lambda h, *_: (0, h)) if first else wide_spec
    in_specs = [q_spec, pl.BlockSpec((1, pool_len, rows), lambda h, *_: (h + lo, 0, 0))]
    in_specs += [pl.BlockSpec(memory_space=pl.ANY)] * len(tiles)
    if not first:
        in_specs += [wide_spec, stat_spec, stat_spec]
    scratch = []
    if split:
        out_rows = rows // split
        out_shape = [
            jax.ShapeDtypeStruct((out_rows, count * head_size), jnp.bfloat16)
        ] * split
        out_specs = [pl.BlockSpec((out_rows, head_size), lambda h, *_: (0, h))] * split
        scratch = [
            pltpu.VMEM((rows, head_size), jnp.bfloat16),
            pltpu.VMEM((1, head_size, rows), jnp.float32),
            pltpu.VMEM((1, 1, rows), jnp.float32),
            pltpu.VMEM((1, 1, rows), jnp.float32),
        ]
    else:
        out_shape = [acc, stat, stat]
        out_specs = [wide_spec, stat_spec, stat_spec]
        if first:
            out_shape = [jax.ShapeDtypeStruct(acc.shape, jnp.bfloat16)] + out_shape
            out_specs = [wide_spec] + out_specs
    places = sum(t.shape[0] for t in tiles)
    scratch += [
        pltpu.VMEM((places, 2, TILE, head_size), jnp.bfloat16),
        pltpu.SemaphoreType.DMA((len(tiles),)),
    ]
    return pl.pallas_call(
        functools.partial(pool_kernel, scale, min(256, rows), len(tiles), first, split, lo),
        grid_spec=pltpu.PrefetchScalarGridSpec(
            num_scalar_prefetch=4,
            grid=(count,),
            in_specs=in_specs,
            out_specs=out_specs,
            scratch_shapes=scratch,
        ),
        out_shape=out_shape,
        compiler_params=pltpu.CompilerParams(vmem_limit_bytes=VMEM_BYTES),
        name="pool_tiles",
    )(*tables, q, bias, *tiles, *(() if first else state))


def scatter_shared(pieces, axis):
    me = lax.axis_index(axis)
    own = pieces[0]
    for k in range(1, pieces.shape[0]):
        own = jnp.where(me == k, lax.ppermute(pieces[k], axis, [(0, k)]), own)
    return own


def line_shared(own, size, axis):
    count = lax.axis_size(axis)
    me = lax.axis_index(axis)
    line = own
    for first in range(size, count, size):
        got = lax.ppermute(own, axis, [(k, first + k) for k in range(size)])
        line = jnp.where(me // size == first // size, got, line)
    return line


def body(queries, keys, values, tile_pool, tile_lists, key_slot):
    seq_count = lax.axis_size("seq")
    side_count = lax.axis_size("head")
    me = lax.axis_index("seq")
    side = lax.axis_index("head")
    head_count, pool_total = tile_pool.shape
    pool_len = pool_total // seq_count
    rows, width = queries.shape
    head_size = width // head_count
    tile_count = rows // TILE
    bound = (head_count * pool_len + seq_count - 1) // seq_count
    scale = head_size ** (-0.5) * LOG2E
    entries = head_count * pool_len

    stacked = jnp.concatenate([keys[: SHARED * TILE], values[: SHARED * TILE]], 0)
    stacked = stacked.reshape(min(4, seq_count), -1, width)

    tiles_all = jnp.arange(key_slot.shape[0], dtype=jnp.int32)
    storage = jnp.sum(
        jnp.where(tile_pool[:, :, None] == tiles_all, key_slot, 0), -1
    ).reshape(head_count, seq_count, pool_len)
    by_reader = storage.transpose(1, 0, 2).reshape(seq_count, entries)
    ids = jnp.arange(entries, dtype=jnp.int32)
    before = (ids[:, None] < ids[None, :]).astype(jnp.bfloat16)
    wanted = by_reader // tile_count == me
    place = jnp.dot(
        wanted.astype(jnp.bfloat16), before, preferred_element_type=jnp.float32
    ).astype(jnp.int32)
    place = jnp.where(wanted, place, -1)
    code = (ids // pool_len)[None, :] * 65536 + by_reader % tile_count
    slots = jnp.arange(bound, dtype=jnp.int32)
    send = jnp.sum(
        jnp.where(place[:, None, :] == slots[None, :, None], code[:, None, :], 0), -1
    ).reshape(-1)

    own = lax.dynamic_index_in_dim(by_reader, me, 0, keepdims=False)
    owner = own // tile_count
    same = (owner[:, None] == owner[None, :]) & (ids[:, None] < ids[None, :])
    position = jnp.sum(same.astype(jnp.int32), 0).reshape(head_count, pool_len)
    owner = owner.reshape(head_count, pool_len)
    pool_ids = jnp.arange(pool_len, dtype=jnp.int32)

    def listing(owners, bases):
        match = owner[:, :, None] == owners
        here = jnp.any(match, -1)
        base = jnp.sum(jnp.where(match, bases, 0), -1)
        rank = jnp.sum(
            (here[:, :, None] & (pool_ids[:, None] < pool_ids[None, :])).astype(jnp.int32), 1
        )
        rank = jnp.where(here, rank, -1)
        hit = rank[:, None, :] == pool_ids[None, :, None]
        entry = jnp.sum(jnp.where(hit, pool_ids, 0), -1)
        place = base + position
        place = jnp.sum(jnp.where(hit, place[:, None, :], 0), -1)
        return place, entry, jnp.sum(here.astype(jnp.int32), 1), side.reshape(1)

    half_count = seq_count // 2
    listed = jnp.any(
        tile_lists[:, :, :, None] == jnp.arange(pool_len, dtype=jnp.int32), 2
    )
    bias = jnp.where(listed, 0.0, -FAR).astype(jnp.float32).transpose(0, 2, 1)
    bias = jnp.repeat(bias, TILE, axis=2)
    split = 2 if side_count == 2 else 1
    part = functools.partial(pool_part, bias=bias, scale=scale, head_size=head_size)

    groups = [
        list(range(i, i + stacked.shape[0])) for i in range(0, seq_count, stacked.shape[0])
    ]

    if seq_count > 16:
        piece = line_shared(scatter_shared(stacked, "seq"), stacked.shape[0], "seq")
        shared = lax.all_gather(piece, "seq", axis=0, tiled=True, axis_index_groups=groups)
        everyone = jnp.arange(seq_count, dtype=jnp.int32)
        (sent,) = pack(send, everyone, keys, values, 0, [seq_count], bound, head_size)
        got = lax.all_to_all(sent, "seq", split_axis=0, concat_axis=0, tiled=True)
        tables = listing(everyone, everyone * bound)
        qt, *state = part(tables, queries, [got], state=None)
        state = shared_part(qt, shared, state, scale)
        tables = (*tables[:2], 0 * tables[2], tables[3])
        last = functools.partial(part, tables, qt, [got], state=state)
    else:
        order = [4, 8, 5, 9, 1, 2, 6, 10, 3, 7, 11, 12, 13, 14, 15, 0]
        partners = me ^ jnp.asarray(order, jnp.int32)
        where = {d: i for i, d in enumerate(order)}

        def use(state, blocks, ds, **kwargs):
            owners = jnp.stack([partners[where[d]] for d in ds])
            tables = listing(owners, bound * jnp.arange(len(ds)))
            q = queries if state is None else qt
            return part(tables, q, [blocks[d] for d in ds], state=state, **kwargs)

        def move(ds):
            return {
                d: lax.ppermute(parts[d], "seq", [(j, j ^ d) for j in range(seq_count)])
                for d in ds
            }

        def fence(*values):
            return lax.optimization_barrier(values)

        head_start = 4
        parts = list(pack(send, partners, keys, values, 0, [1] * head_start, bound, head_size))
        stacked, parts[0] = fence(stacked, parts[0])
        rest = len(order) - head_start
        parts += pack(send, partners, keys, values, head_start, [1] * rest, bound, head_size)
        parts = dict(zip(order, parts))

        piece = scatter_shared(stacked, "seq")
        first = order[:11]
        got = move([4, 8])
        held = [parts[d] for d in (5, 9, 1)]
        *held, piece = fence(*held, piece)
        parts.update(zip((5, 9, 1), held))
        got.update(move([5, 9, 1]))
        for d, earlier in ((6, 4), (10, 8), (2, 1), (7, 5), (11, 9), (3, 2)):
            parts[d], got[earlier] = fence(parts[d], got[earlier])
            got.update(move([d]))
        quarter = stacked.shape[0]
        piece, got[6] = fence(piece, got[6])
        over = lax.ppermute(piece, "seq", [(k, half_count + k) for k in range(quarter)])
        qt, *state = use(None, parts, [0])
        parts, got, piece, over, qt, state = fence(parts, got, piece, over, qt, state)

        halves = [list(range(half_count)), list(range(half_count, seq_count))]
        piece = jnp.where(me >= half_count, over, piece)
        shared = lax.all_gather(piece, "seq", axis=0, tiled=True, axis_index_groups=halves)
        new = move([12, 13, 14, 15])
        state = use(state, got, first)
        state = shared_part(qt, shared, state, scale)
        state = use(state, new, [12, 13])
        state = use(state, new, [14])
        last = functools.partial(use, state, new, [15])

    if split == 1:
        (out,) = last(split=1)
        return lax.all_to_all(out, "head", split_axis=0, concat_axis=1, tiled=True)

    half = head_count // 2
    result = jnp.zeros((rows // 2, 2 * width), jnp.bfloat16)
    kept = []
    arrived = []
    for lo, hi in ((0, half), (half, head_count)):
        keep, away = last(split=2, heads=(lo, hi))
        kept.append((lo, keep))
        arrived.append((lo, lax.ppermute(away, "head", [(0, 1), (1, 0)])))
    for lo, block in kept:
        result = lax.dynamic_update_slice(result, block, (0, side * width + lo * head_size))
    for lo, block in arrived:
        result = lax.dynamic_update_slice(
            result, block, (0, (1 - side) * width + lo * head_size)
        )
    return result


def solution(mesh):
    return jax.shard_map(
        body,
        mesh=mesh,
        in_specs=(
            P("seq", "head"),
            P("seq", "head"),
            P("seq", "head"),
            P("head", None),
            P("head", "seq", None),
            P(),
        ),
        out_specs=P(("seq", "head"), None),
        check_vma=False,
    )
```

time: 864 us -> 394 us (0.46)
  local copies, waits for them, and re-layouts: 255 us -> 10.1 us
  Pallas kernels: 0 us -> 153 us
  waiting for transfers between devices: 301 us -> 168 us
  matrix products: 105 us -> 0.15 us
  other arithmetic: 77.8 us -> 15.8 us
  loops' own time: 51 us -> 0 us
  blocking collectives: 36.4 us -> 0 us
  starting transfers between devices: 12.9 us -> 30.6 us
    all_to_all x2 -> x0, waiting for transfers between devices: 282 us -> none  [the longest x1 282 us: body(): lax.all_to_all(flat_kv[incoming], 'seq', split_axis=0, concat_axis=0, til...]
    ppermute x0 -> x21, waiting for transfers between devices: none -> 162 us  [the longest x15 138 us: move(): lax.ppermute(parts[d], 'seq', [(j, j ^ d) for j in range(seq_count)])]
    pallas_call x0 -> x9, Pallas kernels: none -> 153 us  [the longest x6 117 us: pool_part(): pl.pallas_call(functools.partial(pool_kernel, scale, min(256, rows), len(...]
    dot_general x48 -> x1, matrix products: 105 us -> 0.15 us  [body(): jnp.dot(wanted.astype(jnp.bfloat16), before, preferred_element_type=jnp.f...]
    gather x28 -> x0, local copies, waits for them, and re-layouts: 87 us -> none  [the longest x24 60.6 us: per_block(): listed = pool_tiles[head_id][list_blk]]
    another operation x1 -> x0, loops' own time: 51 us -> none  [body(): per_blocks = lax.map(per_block, (query_blocks, list_blocks, head_of))]
    dynamic_slice x72 -> x1, local copies, waits for them, and re-layouts: 45.1 us -> 0.51 us  [body(): own = lax.dynamic_index_in_dim(by_reader, me, 0, keepdims=False)]
    all_to_all x1 -> x0, blocking collectives: 36.4 us -> none  [body(): lax.all_to_all(result, 'head', split_axis=0, concat_axis=1, tiled=True)]
  transfers between devices with their start and end apart: 3 -> 22, of which waited for: 2 -> 10; matrix products, arithmetic and copies ran while one was open for 6% -> 4% of each run, Pallas kernels for 0% -> 35%
where the time goes in v2:
time: 394 us; the launch traced here: 392 us
  waiting for transfers between devices  168 us (43%)
  Pallas kernels  153 us (39%)
  starting transfers between devices  30.6 us (8%)
  other arithmetic  15.8 us (4%)
  between operations  13.8 us (4%)
  local copies, waits for them, and re-layouts  10.1 us (3%)
    ppermute x15, waiting for transfers between devices, move(): lax.ppermute(parts[d], 'seq', [(j, j ^ d) for j in range(seq_count)])  138 us
    pallas_call x6, Pallas kernels, pool_part(): pl.pallas_call(functools.partial(pool_kernel, scale, min(256, rows), len(...  117 us
    ppermute x15, starting transfers between devices, move(): lax.ppermute(parts[d], 'seq', [(j, j ^ d) for j in range(seq_count)])  24.1 us
    ppermute x2, waiting for transfers between devices, body(): arrived.append((lo, lax.ppermute(away, 'head', [(0, 1), (1, 0)])))  23.9 us
    pallas_call x2, Pallas kernels, pack(): pl.pallas_call(functools.partial(pack_kernel, lo, bound, head_size), grid...  20.7 us
    pallas_call x1, Pallas kernels, shared_part(): pl.pallas_call(functools.partial(shared_kernel, scale, min(256, rows)), g...  16.2 us
  transfers between devices with their start and end apart: 22, of which 10 were waited for; matrix products, arithmetic and copies ran while one was open for 4% of the time, Pallas kernels for 35%

profile of v2, /device:TPU:9, one launch (start us, length us, event | category | flops | bytes accessed | tf_op | source)
XLA Modules:
  0.0 391.7 jit_solution(18248139804977504824)
XLA Ops:
  6.5 1.7 select_reduce_fusion
  8.5 0.2 fusion
  8.7 0.3 select_reduce_fusion.1
  9.1 0.7 reshape.314.codes_ref
  9.7 1.2 broadcast_xor_fusion.order_ref
  11.0 7.4 %pack_tiles.3 = (bf16[12,2,128,128]{3,2,1,0:T(8,128)(2,1)}, bf16[12,2,128,128]{3,2,1,0:T(8,128)(2,1)}, bf16[12,2,128,128]{3,2,1,0:T(8,128)(2,1)}, bf16[12,2,128,128]{3,2,1,0:T(8,128)(2,1)}) custom-call(s32[192]{0:T(256)} %reshape.314.codes_ref, s32[16]{0:T(128)} %broadcast_xor_fusion.order_ref, bf16[1024,1536]{1,0:T(8,128)(2,1)} %keys_ref.3, ...), custom_call_target="tpu_custom_call" | custom-call | tf_op jit(solution)/shard_map/pack_tiles/pallas_call | solution.py:39
  18.4 0.2 pad_maximum_fusion
  18.6 1.5 slice_bitcast_fusion
  20.1 1.5 collective-permute-start
  21.6 1.6 collective-permute-start.1
  23.1 1.6 collective-permute-start.2
  24.7 13.3 %pack_tiles.2 = (bf16[12,2,128,128]{3,2,1,0:T(8,128)(2,1)}, bf16[12,2,128,128]{3,2,1,0:T(8,128)(2,1)}, bf16[12,2,128,128]{3,2,1,0:T(8,128)(2,1)}, bf16[12,2,128,...) custom-call(s32[192]{0:T(256)} %reshape.314.codes_ref, ...), custom_call_target="tpu_custom_call" | custom-call | tf_op jit(solution)/shard_map/pack_tiles/pallas_call | solution.py:39
  38.1 1.1 fusion.2
  39.2 4.6 %collective-permute-start.3 = (bf16[12,2,128,128]{3,2,1,0:T(8,128)(2,1)}, bf16[12,2,128,128]{3,2,1,0:T(8,128)(2,1)S(1)}, u32[]{:S(2)}, u32[]{:S(2)}) collective-permute-start(bf16[12,2,128,128]{3,2,1,0:T(8,128)(2,1)} %get-tuple-element.88), channel_id=1, source_target_pairs={{0,2},{2,0},{4,6},{6,4},{8,10},{10,8},{12,14},{14,12},{16,18},{18,... | collective-permute-start | bytes 2359304 | tf_op jit(solution)/shard_map/ppermute | solution.py:347
  43.8 0.5 broadcast.628
  44.3 0.6 reduce.3
  45.2 0.1 copy.15
  45.3 0.2 fusion.3
  45.7 0.3 broadcast_in_dim.201
  46.0 1.0 reshape.316.bias_ref
  47.0 2.4 collective-permute-start.10
  49.3 2.8 collective-permute-start.8
  52.3 0.7 fusion.29
  53.0 1.4 convert_reduce_fusion.8
  54.6 2.0 convert_reduce_fusion.10
  56.5 21.5 %collective-permute-done.7.refs_1_ = bf16[12,2,128,128]{3,2,1,0:T(8,128)(2,1)S(1)} collective-permute-done((bf16[12,2,128,128]{3,2,1,0:T(8,128)(2,1)}, bf16[12,2,128,128]{3,2,1,0:T(8,128)(2,1)S(1)}, u32[]{:S(2)}, u32[]{:S(2)}) %collective-permute-start.7) | collective-permute-done | bytes 786464 | tf_op jit(solution)/shard_map/ppermute | solution.py:347
  78.1 2.7 collective-permute-start.12
  80.8 2.8 collective-permute-done.10.refs_6_
  83.5 0.9 collective-permute-start.14
  84.4 27.4 %collective-permute-done.8.refs_3_ = bf16[12,2,128,128]{3,2,1,0:T(8,128)(2,1)} collective-permute-done((bf16[12,2,128,128]{3,2,1,0:T(8,128)(2,1)}, bf16[12,2,128,128]{3,2,1,0:T(8,128)(2,1)}, u32[]{:S(2)}, u32[]{:S(2)}) %collective-permute-start.8) | collective-permute-done | bytes 786464 | tf_op jit(solution)/shard_map/ppermute | solution.py:347
  111.8 3.1 collective-permute-start.13
  115.0 2.3 collective-permute-done.6.refs_2_
  117.2 0.9 collective-permute-start.11
  118.1 3.2 collective-permute-start.9
  121.3 0.2 convert_reduce_fusion.1
  121.6 1.9 select_reduce_fusion.6
  123.4 13.7 %pool_tiles.6 = (bf16[12,128,1024]{2,1,0:T(8,128)(2,1)}, f32[12,128,1024]{2,1,0:T(8,128)}, f32[12,1,1024]{2,1,0:T(1,128)}, f32[12,1,1024]{2,1,0:T(1,128)}) custom-call(s32[12,16]{1,0:T(8,128)} %get-tuple-element.165.place_ref, s32[12,16]{1,0:T(8,128)} %get-tuple-element.166.entry_ref, s32[12]{0:T(128)} %get-tuple-element.188.count_ref, s32[1]{0:T(128)} %bitcast.4.side_ref, ...), custom_call_target="tpu_custom_call" | custom-call | tf_op jit(solution)/shard_map/pool_tiles/pallas_call | solution.py:221
  137.2 42.2 %collective-permute-done.12.refs_7_ = bf16[12,2,128,128]{3,2,1,0:T(8,128)(2,1)} collective-permute-done((bf16[12,2,128,128]{3,2,1,0:T(8,128)(2,1)}, bf16[12,2,128,128]{3,2,1,0:T(8,128)(2,1)}, u32[]{:S(2)}, u32[]{:S(2)}) %collective-permute-start.12) | collective-permute-done | bytes 786464 | tf_op jit(solution)/shard_map/ppermute | solution.py:347
  179.4 16.8 %collective-permute-done.13.refs_10_ = bf16[12,2,128,128]{3,2,1,0:T(8,128)(2,1)} collective-permute-done((bf16[12,2,128,128]{3,2,1,0:T(8,128)(2,1)}, bf16[12,2,128,128]{3,2,1,0:T(8,128)(2,1)}, u32[]{:S(2)}, u32[]{:S(2)}) %collective-permute-start.13) | collective-permute-done | bytes 786464 | tf_op jit(solution)/shard_map/ppermute | solution.py:347
  196.2 1.0 broadcast_select_fusion
  197.3 0.7 convert_reduce_fusion.6
  198.0 2.0 collective-permute-start.18
  200.1 2.3 collective-permute-start.15
  202.5 1.1 select_reduce_fusion.2
  203.6 0.7 convert_reduce_fusion.7
  204.3 1.1 select_reduce_fusion.4
  205.4 50.2 %pool_tiles.7 = (f32[12,128,1024]{2,1,0:T(8,128)}, f32[12,1,1024]{2,1,0:T(1,128)}, f32[12,1,1024]{2,1,0:T(1,128)}) custom-call(s32[12,16]{1,0:T(8,128)} %get-tuple-element.160.place_ref, s32[12,16]{1,0:T(8,128)} %get-tuple-element.159.entry_ref, s32[12]{0:T(128)} %get-tuple-element.190.count_ref, s32[1]{0:T(128)} %bitcast.4.side_ref, ...), custom_call_target="tpu_custom_call" | custom-call | tf_op jit(solution)/shard_map/pool_tiles/pallas_call | solution.py:221
  255.6 6.1 %all-gather.2.cloned.1.call-done.k_ref.v_ref = bf16[2048,1536]{1,0:T(8,128)(2,1)} async-done(((bf16[256,1536]{1,0:T(8,128)(2,1)}), bf16[2048,1536]{1,0:T(8,128)(2,1)}) %all-gather.2.cloned.1.call-update) | async-done | bytes 6291472 | tf_op jit(solution)/shard_map/all_gather | solution.py:379
  261.7 16.2 %shared_tiles.1 = (f32[12,128,1024]{2,1,0:T(8,128)}, f32[12,1,1024]{2,1,0:T(1,128)}, f32[12,1,1024]{2,1,0:T(1,128)}) custom-call(bf16[12,128,1024]{2,1,0:T(8,128)(2,1)} %get-tuple-element.122.q_ref.qt_ref, bf16[2048,1536]{1,0:T(8,128)(2,1)} %all-gather.2.cloned.1.call-done.k_ref.v_ref, bf16[2048,1536]{1,0:T(8,128)(2,1)} %all-gather.2.cloned.1.call-done.k_ref.v_ref, ...), custom_call_target="tpu_custom_call" | custom-call | tf_op jit(solution)/shard_map/shared_tiles/pallas_call | solution.py:91
  277.9 24.7 %collective-permute-done.18.refs_1_ = bf16[12,2,128,128]{3,2,1,0:T(8,128)(2,1)S(1)} collective-permute-done((bf16[12,2,128,128]{3,2,1,0:T(8,128)(2,1)}, bf16[12,2,128,128]{3,2,1,0:T(8,128)(2,1)S(1)}, u32[]{:S(2)}, u32[]{:S(2)}) %collective-permute-start.18) | collective-permute-done | bytes 786464 | tf_op jit(solution)/shard_map/ppermute | solution.py:347
  302.6 0.9 copy-done.8
  303.5 17.9 %pool_tiles.8 = (f32[12,128,1024]{2,1,0:T(8,128)}, f32[12,1,1024]{2,1,0:T(1,128)}, f32[12,1,1024]{2,1,0:T(1,128)}) custom-call(s32[12,16]{1,0:T(8,128)} %get-tuple-element.162.place_ref, s32[12,16]{1,0:T(8,128)} %get-tuple-element.161.entry_ref, s32[12]{0:T(128)} %get-tuple-element.192.count_ref, s32[1]{0:T(128)} %bitcast.4.side_ref, ...), custom_call_target="tpu_custom_call" | custom-call | tf_op jit(solution)/shard_map/pool_tiles/pallas_call | solution.py:221
  321.4 0.9 copy-done.6
  322.3 15.5 %pool_tiles.9 = (f32[12,128,1024]{2,1,0:T(8,128)}, f32[12,1,1024]{2,1,0:T(1,128)}, f32[12,1,1024]{2,1,0:T(1,128)}) custom-call(s32[12,16]{1,0:T(8,128)} %get-tuple-element.164.place_ref, s32[12,16]{1,0:T(8,128)} %get-tuple-element.163.entry_ref, s32[12]{0:T(128)} %get-tuple-element.174.count_ref, s32[1]{0:T(128)} %bitcast.4.side_ref, ...), custom_call_target="tpu_custom_call" | custom-call | tf_op jit(solution)/shard_map/pool_tiles/pallas_call | solution.py:221
  337.8 1.0 copy-done
  338.8 9.5 %pool_tiles.10 = (bf16[512,768]{1,0:T(8,128)(2,1)}, bf16[512,768]{1,0:T(8,128)(2,1)}) custom-call(s32[12,16]{1,0:T(8,128)} %get-tuple-element.167.place_ref, s32[12,16]{1,0:T(8,128)} %get-tuple-element.168.entry_ref, s32[12]{0:T(128)} %get-tuple-element.179.count_ref, s32[1]{0:T(128)} %bitcast.4.side_ref, ...), custom_call_target="tpu_custom_call" | custom-call | tf_op jit(solution)/shard_map/pool_tiles/pallas_call | solution.py:221
  348.3 0.4 collective-permute-start.19
  348.8 9.7 %pool_tiles.11 = (bf16[512,768]{1,0:T(8,128)(2,1)}, bf16[512,768]{1,0:T(8,128)(2,1)}) custom-call(s32[12,16]{1,0:T(8,128)} %get-tuple-element.167.place_ref, s32[12,16]{1,0:T(8,128)} %get-tuple-element.168.entry_ref, s32[12]{0:T(128)} %get-tuple-element.179.count_ref, s32[1]{0:T(128)} %bitcast.4.side_ref, ...), custom_call_target="tpu_custom_call" | custom-call | tf_op jit(solution)/shard_map/pool_tiles/pallas_call | solution.py:221
  358.5 0.5 collective-permute-start.20
  359.0 0.4 broadcast_in_dim.189
  359.4 0.2 copy-done.9
  359.9 8.2 %collective-permute-done.19 = bf16[512,768]{1,0:T(8,128)(2,1)S(1)} collective-permute-done((bf16[512,768]{1,0:T(8,128)(2,1)}, bf16[512,768]{1,0:T(8,128)(2,1)S(1)}, u32[]{:S(2)}, u32[]{:S(2)}) %collective-permute-start.19) | collective-permute-done | bytes 786464 | tf_op jit(solution)/shard_map/ppermute | solution.py:398
  368.3 15.7 %collective-permute-done.20 = bf16[512,768]{1,0:T(8,128)(2,1)S(1)} collective-permute-done((bf16[512,768]{1,0:T(8,128)(2,1)}, bf16[512,768]{1,0:T(8,128)(2,1)S(1)}, u32[]{:S(2)}, u32[]{:S(2)}) %collective-permute-start.20) | collective-permute-done | bytes 786464 | tf_op jit(solution)/shard_map/ppermute | solution.py:398
  383.9 0.9 constant_dynamic-update-slice_fusion.3
  (72 shorter events, 1.8 us)
Async XLA Ops:
  6.5 255.2 %all-gather.2.cloned.1.call-start = ((), (), s32[]{:S(2)}) async-start(), calls=%async_computation | async-start | bytes 7077888 | tf_op jit(solution)/shard_map/all_gather | solution.py:379
  11.0 7.4 %slice-start = ((bf16[1024,1536]{1,0:T(8,128)(2,1)}), bf16[512,1536]{1,0:T(8,128)(2,1)S(1)}, s32[]{:S(2)}) async-start(bf16[1024,1536]{1,0:T(8,128)(2,1)} %keys_ref.3), calls=%async_computation.1 | async-start | bytes 3145728 | tf_op jit(solution)/shard_map/slice | solution.py:268
  11.0 7.4 %slice-start.1 = ((bf16[1024,1536]{1,0:T(8,128)(2,1)}), bf16[512,1536]{1,0:T(8,128)(2,1)S(1)}, s32[]{:S(2)}) async-start(bf16[1024,1536]{1,0:T(8,128)(2,1)} %values_ref.3), calls=%async_computation.2 | async-start | bytes 3145728 | tf_op jit(solution)/shard_map/slice | solution.py:268
  20.1 18.0 %collective-permute-start = (bf16[256,1536]{1,0:T(8,128)(2,1)}, bf16[256,1536]{1,0:T(8,128)(2,1)}, u32[]{:S(2)}, u32[]{:S(2)}) collective-permute-start(bf16[256,1536]{1,0:T(8,128)(2,1)} %get-tuple-element.185), channel_id=1, source_target_pairs={{0,6},{1,7}} | collective-permute-start | bytes 2359304 | tf_op jit(solution)/shard_map/ppermute | solution.py:240
  21.6 16.5 %collective-permute-start.1 = (bf16[256,1536]{1,0:T(8,128)(2,1)}, bf16[256,1536]{1,0:T(8,128)(2,1)}, u32[]{:S(2)}, u32[]{:S(2)}) collective-permute-start(bf16[256,1536]{1,0:T(8,128)(2,1)} %get-tuple-element.184), channel_id=1, source_target_pairs={{0,4},{1,5}} | collective-permute-start | bytes 2359304 | tf_op jit(solution)/shard_map/ppermute | solution.py:240
  23.1 14.9 %collective-permute-start.2 = (bf16[256,1536]{1,0:T(8,128)(2,1)}, bf16[256,1536]{1,0:T(8,128)(2,1)}, u32[]{:S(2)}, u32[]{:S(2)}) collective-permute-start(bf16[256,1536]{1,0:T(8,128)(2,1)} %get-tuple-element.183), channel_id=1, source_target_pairs={{0,2},{1,3}} | collective-permute-start | bytes 2359304 | tf_op jit(solution)/shard_map/ppermute | solution.py:240
  24.7 22.2 %collective-permute-start.5 = (bf16[12,2,128,128]{3,2,1,0:T(8,128)(2,1)}, bf16[12,2,128,128]{3,2,1,0:T(8,128)(2,1)}, u32[]{:S(2)}, u32[]{:S(2)}) collective-permute-start(bf16[12,2,128,128]{3,2,1,0:T(8,128)(2,1)} %get-tuple-element.93), channel_id=1, source_target_pairs={{0,8},{2,10},{4,12},{6,14},{8,0},{10,2},{12,4},{14,6},{16,24},{18,... | collective-permute-start | bytes 2359304 | tf_op jit(solution)/shard_map/ppermute | solution.py:347
  38.1 5.7 %copy-start.12 = (s32[16]{0:T(128)S(1)}, s32[16]{0:T(128)}, u32[]{:S(2)}) copy-start(s32[16]{0:T(128)} %broadcast_xor_fusion.order_ref) | copy-start | bytes 196
  38.1 7.1 %copy-start.11 = (s32[12,8,12]{2,1,0:T(8,128)S(1)}, s32[12,8,12]{2,1,0:T(8,128)}, u32[]{:S(2)}) copy-start(s32[12,8,12]{2,1,0:T(8,128)} %param.11) | copy-start | bytes 13828
  39.2 12.9 %collective-permute-start.3 = (bf16[12,2,128,128]{3,2,1,0:T(8,128)(2,1)}, bf16[12,2,128,128]{3,2,1,0:T(8,128)(2,1)S(1)}, u32[]{:S(2)}, u32[]{:S(2)}) collective-permute-start(bf16[12,2,128,128]{3,2,1,0:T(8,128)(2,1)} %get-tuple-element.88), channel_id=1, source_target_pairs={{0,2},{2,0},{4,6},{6,4},{8,10},{10,8},{12,14},{14,12},{16,18},{18,... | collective-permute-start | bytes 2359304 | tf_op jit(solution)/shard_map/ppermute | solution.py:347
  43.7 34.3 %collective-permute-start.7 = (bf16[12,2,128,128]{3,2,1,0:T(8,128)(2,1)}, bf16[12,2,128,128]{3,2,1,0:T(8,128)(2,1)S(1)}, u32[]{:S(2)}, u32[]{:S(2)}) collective-permute-start(bf16[12,2,128,128]{3,2,1,0:T(8,128)(2,1)} %get-tuple-element.99), channel_id=1, source_target_pairs={{0,16},{2,18},{4,20},{6,22},{8,24},{10,26},{12,28},{14,30},{16,0},... | collective-permute-start | bytes 2359304 | tf_op jit(solution)/shard_map/ppermute | solution.py:347
  45.9 150.3 %copy-start.1 = (bf16[256,1536]{1,0:T(8,128)(2,1)S(1)}, bf16[256,1536]{1,0:T(8,128)(2,1)}, u32[]{:S(2)}) copy-start(bf16[256,1536]{1,0:T(8,128)(2,1)} %fusion.2) | copy-start | bytes 2359300
  47.0 36.6 %collective-permute-start.10 = (bf16[12,2,128,128]{3,2,1,0:T(8,128)(2,1)}, bf16[12,2,128,128]{3,2,1,0:T(8,128)(2,1)S(1)}, u32[]{:S(2)}, u32[]{:S(2)}) collective-permute-start(bf16[12,2,128,128]{3,2,1,0:T(8,128)(2,1)} %get-tuple-element.96), channel_id=1, source_target_pairs={{0,12},{2,14},{4,8},{6,10},{8,4},{10,6},{12,0},{14,2},{16,28},{18,... | collective-permute-start | bytes 2359304 | tf_op jit(solution)/shard_map/ppermute | solution.py:347
  49.3 62.5 %collective-permute-start.8 = (bf16[12,2,128,128]{3,2,1,0:T(8,128)(2,1)}, bf16[12,2,128,128]{3,2,1,0:T(8,128)(2,1)}, u32[]{:S(2)}, u32[]{:S(2)}) collective-permute-start(bf16[12,2,128,128]{3,2,1,0:T(8,128)(2,1)} %get-tuple-element.100), channel_id=1, source_target_pairs={{0,18},{2,16},{4,22},{6,20},{8,26},{10,24},{12,30},{14,28},{16,2},... | collective-permute-start | bytes 2359304 | tf_op jit(solution)/shard_map/ppermute | solution.py:347
  52.1 65.1 %collective-permute-start.6 = (bf16[12,2,128,128]{3,2,1,0:T(8,128)(2,1)}, bf16[12,2,128,128]{3,2,1,0:T(8,128)(2,1)}, u32[]{:S(2)}, u32[]{:S(2)}) collective-permute-start(bf16[12,2,128,128]{3,2,1,0:T(8,128)(2,1)} %get-tuple-element.94), channel_id=1, source_target_pairs={{0,10},{2,8},{4,14},{6,12},{8,2},{10,0},{12,6},{14,4},{16,26},{18,... | collective-permute-start | bytes 2359304 | tf_op jit(solution)/shard_map/ppermute | solution.py:347
  52.1 145.1 %copy-start.3 = (bf16[12,2,128,128]{3,2,1,0:T(8,128)(2,1)}, bf16[12,2,128,128]{3,2,1,0:T(8,128)(2,1)S(1)}, u32[]{:S(2)}) copy-start(bf16[12,2,128,128]{3,2,1,0:T(8,128)(2,1)S(1)} %collective-permute-done.3.refs_4_) | copy-start | bytes 2359300
  52.1 66.0 %collective-permute-start.4 = (bf16[12,2,128,128]{3,2,1,0:T(8,128)(2,1)}, bf16[12,2,128,128]{3,2,1,0:T(8,128)(2,1)}, u32[]{:S(2)}, u32[]{:S(2)}) collective-permute-start(bf16[12,2,128,128]{3,2,1,0:T(8,128)(2,1)} %get-tuple-element.90), channel_id=1, source_target_pairs={{0,4},{2,6},{4,0},{6,2},{8,12},{10,14},{12,8},{14,10},{16,20},{18,... | collective-permute-start | bytes 2359304 | tf_op jit(solution)/shard_map/ppermute | solution.py:347
  78.1 119.1 %copy-start.4 = (bf16[12,2,128,128]{3,2,1,0:T(8,128)(2,1)}, bf16[12,2,128,128]{3,2,1,0:T(8,128)(2,1)S(1)}, u32[]{:S(2)}) copy-start(bf16[12,2,128,128]{3,2,1,0:T(8,128)(2,1)S(1)} %collective-permute-done.7.refs_1_) | copy-start | bytes 2359300
  78.1 101.3 %collective-permute-start.12 = (bf16[12,2,128,128]{3,2,1,0:T(8,128)(2,1)}, bf16[12,2,128,128]{3,2,1,0:T(8,128)(2,1)}, u32[]{:S(2)}, u32[]{:S(2)}) collective-permute-start(bf16[12,2,128,128]{3,2,1,0:T(8,128)(2,1)} %get-tuple-element.102), channel_id=1, source_target_pairs={{0,20},{2,22},{4,16},{6,18},{8,28},{10,30},{12,24},{14,26},{16,4},... | collective-permute-start | bytes 2359304 | tf_op jit(solution)/shard_map/ppermute | solution.py:347
  83.5 113.7 %copy-start.5 = (bf16[12,2,128,128]{3,2,1,0:T(8,128)(2,1)}, bf16[12,2,128,128]{3,2,1,0:T(8,128)(2,1)S(1)}, u32[]{:S(2)}) copy-start(bf16[12,2,128,128]{3,2,1,0:T(8,128)(2,1)S(1)} %collective-permute-done.10.refs_6_) | copy-start | bytes 2359300
  83.5 95.8 %collective-permute-start.14 = (bf16[256,1536]{1,0:T(8,128)(2,1)}, bf16[256,1536]{1,0:T(8,128)(2,1)S(1)}, u32[]{:S(2)}, u32[]{:S(2)}) collective-permute-start(bf16[256,1536]{1,0:T(8,128)(2,1)} %fusion.2), channel_id=1, source_target_pairs={{0,16},{2,18},{4,20},{6,22},{1,17},{3,19},{5,21},{7,23}} | collective-permute-start | bytes 2359304 | tf_op jit(solution)/shard_map/ppermute | solution.py:373
  111.8 84.4 %collective-permute-start.13 = (bf16[12,2,128,128]{3,2,1,0:T(8,128)(2,1)}, bf16[12,2,128,128]{3,2,1,0:T(8,128)(2,1)}, u32[]{:S(2)}, u32[]{:S(2)}) collective-permute-start(bf16[12,2,128,128]{3,2,1,0:T(8,128)(2,1)} %get-tuple-element.104), channel_id=1, source_target_pairs={{0,22},{2,20},{4,18},{6,16},{8,30},{10,28},{12,26},{14,24},{16,6},... | collective-permute-start | bytes 2359304 | tf_op jit(solution)/shard_map/ppermute | solution.py:347
  117.2 79.0 %collective-permute-start.11 = (bf16[12,2,128,128]{3,2,1,0:T(8,128)(2,1)}, bf16[12,2,128,128]{3,2,1,0:T(8,128)(2,1)}, u32[]{:S(2)}, u32[]{:S(2)}) collective-permute-start(bf16[12,2,128,128]{3,2,1,0:T(8,128)(2,1)} %get-tuple-element.98), channel_id=1, source_target_pairs={{0,14},{2,12},{4,10},{6,8},{8,6},{10,4},{12,2},{14,0},{16,30},{18,... | collective-permute-start | bytes 2359304 | tf_op jit(solution)/shard_map/ppermute | solution.py:347
  118.1 78.1 %collective-permute-start.9 = (bf16[12,2,128,128]{3,2,1,0:T(8,128)(2,1)}, bf16[12,2,128,128]{3,2,1,0:T(8,128)(2,1)}, u32[]{:S(2)}, u32[]{:S(2)}) collective-permute-start(bf16[12,2,128,128]{3,2,1,0:T(8,128)(2,1)} %get-tuple-element.92), channel_id=1, source_target_pairs={{0,6},{2,4},{4,2},{6,0},{8,14},{10,12},{12,10},{14,8},{16,22},{18,... | collective-permute-start | bytes 2359304 | tf_op jit(solution)/shard_map/ppermute | solution.py:347
  198.0 79.9 %collective-permute-start.17 = (bf16[12,2,128,128]{3,2,1,0:T(8,128)(2,1)}, bf16[12,2,128,128]{3,2,1,0:T(8,128)(2,1)S(1)}, u32[]{:S(2)}, u32[]{:S(2)}) collective-permute-start(bf16[12,2,128,128]{3,2,1,0:T(8,128)(2,1)} %get-tuple-element.125), channel_id=1, source_target_pairs={{0,24},{2,26},{4,28},{6,30},{8,16},{10,18},{12,20},{14,22},{16,8},... | collective-permute-start | bytes 2359304 | tf_op jit(solution)/shard_map/ppermute | solution.py:347
  198.0 104.6 %collective-permute-start.18 = (bf16[12,2,128,128]{3,2,1,0:T(8,128)(2,1)}, bf16[12,2,128,128]{3,2,1,0:T(8,128)(2,1)S(1)}, u32[]{:S(2)}, u32[]{:S(2)}) collective-permute-start(bf16[12,2,128,128]{3,2,1,0:T(8,128)(2,1)} %get-tuple-element.126), channel_id=1, source_target_pairs={{0,26},{2,24},{4,30},{6,28},{8,18},{10,16},{12,22},{14,20},{16,10}... | collective-permute-start | bytes 2359304 | tf_op jit(solution)/shard_map/ppermute | solution.py:347
  200.1 121.3 %collective-permute-start.16 = (bf16[12,2,128,128]{3,2,1,0:T(8,128)(2,1)}, bf16[12,2,128,128]{3,2,1,0:T(8,128)(2,1)S(1)}, u32[]{:S(2)}, u32[]{:S(2)}) collective-permute-start(bf16[12,2,128,128]{3,2,1,0:T(8,128)(2,1)} %get-tuple-element.124), channel_id=1, source_target_pairs={{0,28},{2,30},{4,24},{6,26},{8,20},{10,22},{12,16},{14,18},{16,12}... | collective-permute-start | bytes 2359304 | tf_op jit(solution)/shard_map/ppermute | solution.py:347
  200.1 137.7 %collective-permute-start.15 = (bf16[12,2,128,128]{3,2,1,0:T(8,128)(2,1)}, bf16[12,2,128,128]{3,2,1,0:T(8,128)(2,1)S(1)}, u32[]{:S(2)}, u32[]{:S(2)}) collective-permute-start(bf16[12,2,128,128]{3,2,1,0:T(8,128)(2,1)} %get-tuple-element.123), channel_id=1, source_target_pairs={{0,30},{2,28},{4,26},{6,24},{8,22},{10,20},{12,18},{14,16},{16,14}... | collective-permute-start | bytes 2359304 | tf_op jit(solution)/shard_map/ppermute | solution.py:347
  277.9 24.7 %copy-start.7 = (bf16[12,2,128,128]{3,2,1,0:T(8,128)(2,1)}, bf16[12,2,128,128]{3,2,1,0:T(8,128)(2,1)S(1)}, u32[]{:S(2)}) copy-start(bf16[12,2,128,128]{3,2,1,0:T(8,128)(2,1)S(1)} %collective-permute-done.17.refs_0_) | copy-start | bytes 2359300
  302.6 0.9 copy-start.8
  321.4 0.9 copy-start.6
  337.8 1.0 copy-start
  348.3 19.8 %collective-permute-start.19 = (bf16[512,768]{1,0:T(8,128)(2,1)}, bf16[512,768]{1,0:T(8,128)(2,1)S(1)}, u32[]{:S(2)}, u32[]{:S(2)}) collective-permute-start(bf16[512,768]{1,0:T(8,128)(2,1)} %get-tuple-element.157), channel_id=1, source_target_pairs={{0,1},{1,0},{2,3},{3,2},{4,5},{5,4},{6,7},{7,6},{8,9},{9,8},{10,11... | collective-permute-start | bytes 2359304 | tf_op jit(solution)/shard_map/ppermute | solution.py:398
  358.5 1.1 copy-start.9
  358.5 1.4 copy-start.10
  358.5 25.4 %collective-permute-start.20 = (bf16[512,768]{1,0:T(8,128)(2,1)}, bf16[512,768]{1,0:T(8,128)(2,1)S(1)}, u32[]{:S(2)}, u32[]{:S(2)}) collective-permute-start(bf16[512,768]{1,0:T(8,128)(2,1)} %get-tuple-element.158), channel_id=1, source_target_pairs={{0,1},{1,0},{2,3},{3,2},{4,5},{5,4},{6,7},{7,6},{8,9},{9,8},{10,11... | collective-permute-start | bytes 2359304 | tf_op jit(solution)/shard_map/ppermute | solution.py:398
  368.2 15.7 %copy-start.2 = (bf16[512,3072]{1,0:T(8,128)(2,1)}, bf16[512,3072]{1,0:T(8,128)(2,1)S(1)}, u32[]{:S(2)}) copy-start(bf16[512,3072]{1,0:T(8,128)(2,1)S(1)} %constant_dynamic-update-slice_fusion.2) | copy-start | bytes 9437188
Sparse Core Ops, SparseCore 0:
  197.3 64.3 all-gather.1

commit v3 on v2

--- a/solution.py
+++ b/solution.py
@@ -12,6 +12,7 @@
 FAR = 1e30
 LOG2E = 1.4426950408889634
 VMEM_BYTES = 56 * 1024 * 1024
+WORK_BYTES = 12 * 1024 * 1024
 
 
 def pack_kernel(lo, bound, head_size, codes_ref, order_ref, keys_ref, values_ref, *out_refs):
@@ -95,13 +96,13 @@
         in_specs=[
             wide_spec,
             pl.BlockSpec((keys, head_size), lambda h: (0, h)),
-            pl.BlockSpec((keys, head_size), lambda h: (1, h)),
+            pl.BlockSpec((keys, head_size), lambda h: (2, h)),
             wide_spec,
             stat_spec,
             stat_spec,
         ],
         out_specs=[wide_spec, stat_spec, stat_spec],
-        compiler_params=pltpu.CompilerParams(vmem_limit_bytes=VMEM_BYTES),
+        compiler_params=pltpu.CompilerParams(vmem_limit_bytes=WORK_BYTES),
         name="shared_tiles",
     )(qt, shared, shared, *state)
 
@@ -228,27 +229,32 @@
             scratch_shapes=scratch,
         ),
         out_shape=out_shape,
-        compiler_params=pltpu.CompilerParams(vmem_limit_bytes=VMEM_BYTES),
+        compiler_params=pltpu.CompilerParams(
+            vmem_limit_bytes=WORK_BYTES + places * 2 * TILE * head_size * 2
+        ),
         name="pool_tiles",
     )(*tables, q, bias, *tiles, *(() if first else state))
 
 
-def scatter_shared(pieces, axis):
+def share_halves(keys, values, axis, size):
     me = lax.axis_index(axis)
-    own = pieces[0]
-    for k in range(1, pieces.shape[0]):
-        own = jnp.where(me == k, lax.ppermute(pieces[k], axis, [(0, k)]), own)
-    return own
-
-
-def line_shared(own, size, axis):
+    got = lax.ppermute(values, axis, [(0, size // 2)])
+    return jnp.where(me % size == size // 2, got, keys)
+
+
+def share_step(piece, axis, size, step):
     count = lax.axis_size(axis)
     me = lax.axis_index(axis)
-    line = own
-    for first in range(size, count, size):
-        got = lax.ppermute(own, axis, [(k, first + k) for k in range(size)])
-        line = jnp.where(me // size == first // size, got, line)
-    return line
+    pairs = [
+        (j + k, j + k + step) for j in range(0, count, 2 * step) for k in (0, size // 2)
+    ]
+    over = lax.ppermute(piece, axis, pairs)
+    return jnp.where(me // step % 2 == 1, over, piece)
+
+
+def share_within(piece, axis, size):
+    groups = [list(range(i, i + size)) for i in range(0, lax.axis_size(axis), size)]
+    return lax.all_gather(piece, axis, axis=0, tiled=True, axis_index_groups=groups)
 
 
 def body(queries, keys, values, tile_pool, tile_lists, key_slot):
@@ -265,8 +271,8 @@
     scale = head_size ** (-0.5) * LOG2E
     entries = head_count * pool_len
 
-    stacked = jnp.concatenate([keys[: SHARED * TILE], values[: SHARED * TILE]], 0)
-    stacked = stacked.reshape(min(4, seq_count), -1, width)
+    shared_keys, shared_values = keys[: SHARED * TILE], values[: SHARED * TILE]
+    quarter = 4
 
     tiles_all = jnp.arange(key_slot.shape[0], dtype=jnp.int32)
     storage = jnp.sum(
@@ -316,13 +322,13 @@
     split = 2 if side_count == 2 else 1
     part = functools.partial(pool_part, bias=bias, scale=scale, head_size=head_size)
 
-    groups = [
-        list(range(i, i + stacked.shape[0])) for i in range(0, seq_count, stacked.shape[0])
-    ]
-
     if seq_count > 16:
-        piece = line_shared(scatter_shared(stacked, "seq"), stacked.shape[0], "seq")
-        shared = lax.all_gather(piece, "seq", axis=0, tiled=True, axis_index_groups=groups)
+        piece = share_halves(shared_keys, shared_values, "seq", quarter)
+        step = seq_count // 2
+        while step >= quarter:
+            piece = share_step(piece, "seq", quarter, step)
+            step //= 2
+        shared = share_within(piece, "seq", quarter)
         everyone = jnp.arange(seq_count, dtype=jnp.int32)
         (sent,) = pack(send, everyone, keys, values, 0, [seq_count], bound, head_size)
         got = lax.all_to_all(sent, "seq", split_axis=0, concat_axis=0, tiled=True)
@@ -332,7 +338,7 @@
         tables = (*tables[:2], 0 * tables[2], tables[3])
         last = functools.partial(part, tables, qt, [got], state=state)
     else:
-        order = [4, 8, 5, 9, 1, 2, 6, 10, 3, 7, 11, 12, 13, 14, 15, 0]
+        order = [4, 8, 5, 9, 1, 2, 10, 3, 11, 7, 6, 12, 13, 14, 15, 0]
         partners = me ^ jnp.asarray(order, jnp.int32)
         where = {d: i for i, d in enumerate(order)}
 
@@ -351,36 +357,29 @@
         def fence(*values):
             return lax.optimization_barrier(values)
 
-        head_start = 4
-        parts = list(pack(send, partners, keys, values, 0, [1] * head_start, bound, head_size))
-        stacked, parts[0] = fence(stacked, parts[0])
-        rest = len(order) - head_start
-        parts += pack(send, partners, keys, values, head_start, [1] * rest, bound, head_size)
-        parts = dict(zip(order, parts))
-
-        piece = scatter_shared(stacked, "seq")
-        first = order[:11]
-        got = move([4, 8])
-        held = [parts[d] for d in (5, 9, 1)]
-        *held, piece = fence(*held, piece)
-        parts.update(zip((5, 9, 1), held))
-        got.update(move([5, 9, 1]))
-        for d, earlier in ((6, 4), (10, 8), (2, 1), (7, 5), (11, 9), (3, 2)):
+        parts = {}
+        for lo, hi in ((0, 4), (4, 10), (10, len(order))):
+            packed = pack(send, partners, keys, values, lo, [1] * (hi - lo), bound, head_size)
+            parts.update(zip(order[lo:hi], packed))
+
+        piece = share_halves(shared_keys, shared_values, "seq", quarter)
+        first = [5, 1, 2, 10, 3, 11, 7]
+        got = move([4, 8, 5, 9])
+        piece, parts[4] = fence(piece, parts[4])
+        piece = share_step(piece, "seq", quarter, half_count)
+        for d, earlier in ((1, 4), (10, 8), (2, 1), (11, 9), (3, 2), (7, 5)):
             parts[d], got[earlier] = fence(parts[d], got[earlier])
             got.update(move([d]))
-        quarter = stacked.shape[0]
-        piece, got[6] = fence(piece, got[6])
-        over = lax.ppermute(piece, "seq", [(k, half_count + k) for k in range(quarter)])
-        qt, *state = use(None, parts, [0])
-        parts, got, piece, over, qt, state = fence(parts, got, piece, over, qt, state)
-
-        halves = [list(range(half_count)), list(range(half_count, seq_count))]
-        piece = jnp.where(me >= half_count, over, piece)
-        shared = lax.all_gather(piece, "seq", axis=0, tiled=True, axis_index_groups=halves)
-        new = move([12, 13, 14, 15])
+        piece = share_step(piece, "seq", quarter, quarter)
+        got[0] = parts[0]
+        qt, *state = use(None, got, [0, 4, 8, 9])
+        parts, got, piece, qt, state = fence(parts, got, piece, qt, state)
+
+        shared = share_within(piece, "seq", quarter)
+        new = move([6, 12, 13, 14, 15])
         state = use(state, got, first)
         state = shared_part(qt, shared, state, scale)
-        state = use(state, new, [12, 13])
+        state = use(state, new, [6, 12, 13])
         state = use(state, new, [14])
         last = functools.partial(use, state, new, [15])
 
@@ -388,11 +387,11 @@
         (out,) = last(split=1)
         return lax.all_to_all(out, "head", split_axis=0, concat_axis=1, tiled=True)
 
-    half = head_count // 2
+    third = head_count // 3
     result = jnp.zeros((rows // 2, 2 * width), jnp.bfloat16)
     kept = []
     arrived = []
-    for lo, hi in ((0, half), (half, head_count)):
+    for lo, hi in ((0, third), (third, 2 * third), (2 * third, head_count)):
         keep, away = last(split=2, heads=(lo, hi))
         kept.append((lo, keep))
         arrived.append((lo, lax.ppermute(away, "head", [(0, 1), (1, 0)])))

time: 394 us -> 375 us (0.952)
  waiting for transfers between devices: 168 us -> 109 us
  starting transfers between devices: 30.6 us -> 65.7 us
  local copies, waits for them, and re-layouts: 10.1 us -> 42.3 us
  Pallas kernels: 153 us -> 126 us
    ppermute x15, waiting for transfers between devices: 138 us -> 85.2 us  [move(): lax.ppermute(parts[d], 'seq', [(j, j ^ d) for j in range(seq_count)])]
    ppermute x15, starting transfers between devices: 24.1 us -> 59.2 us  [move(): lax.ppermute(parts[d], 'seq', [(j, j ^ d) for j in range(seq_count)])]
    unnamed x27 -> x75, local copies, waits for them, and re-layouts: 3.3 us -> 33.4 us
    pallas_call x6 -> x7, Pallas kernels: 117 us -> 88.6 us  [pool_part(): pl.pallas_call(functools.partial(pool_kernel, scale, min(256, rows), len(...]
    ppermute x2 -> x3, waiting for transfers between devices: 23.9 us -> 16.3 us  [body(): arrived.append((lo, lax.ppermute(away, 'head', [(0, 1), (1, 0)])))]
    select_n x2 -> x3, other arithmetic: 2.05 us -> 6.74 us  [the longest x2 5.43 us: share_step(): return jnp.where(me // step % 2 == 1, over, piece)]
    pallas_call x2 -> x3, Pallas kernels: 20.7 us -> 25 us  [pack(): pl.pallas_call(functools.partial(pack_kernel, lo, bound, head_size), grid...]
  transfers between devices with their start and end apart: 22 -> 22, of which waited for: 10 -> 11; matrix products, arithmetic and copies ran while one was open for 4% -> 6% of each run, Pallas kernels for 35% -> 32%
where the time goes in v3:
time: 375 us; the launch traced here: 373 us
  Pallas kernels  126 us (34%)
  waiting for transfers between devices  109 us (29%)
  starting transfers between devices  65.7 us (18%)
  local copies, waits for them, and re-layouts  42.3 us (11%)
  other arithmetic  16.5 us (4%)
  between operations  13.9 us (4%)
    pallas_call x7, Pallas kernels, pool_part(): pl.pallas_call(functools.partial(pool_kernel, scale, min(256, rows), len(...  88.6 us
    ppermute x15, waiting for transfers between devices, move(): lax.ppermute(parts[d], 'seq', [(j, j ^ d) for j in range(seq_count)])  85.2 us
    ppermute x15, starting transfers between devices, move(): lax.ppermute(parts[d], 'seq', [(j, j ^ d) for j in range(seq_count)])  59.2 us
    unnamed x75, local copies, waits for them, and re-layouts  33.4 us
    pallas_call x3, Pallas kernels, pack(): pl.pallas_call(functools.partial(pack_kernel, lo, bound, head_size), grid...  25 us
    ppermute x3, waiting for transfers between devices, body(): arrived.append((lo, lax.ppermute(away, 'head', [(0, 1), (1, 0)])))  16.3 us
    pallas_call x1, Pallas kernels, shared_part(): pl.pallas_call(functools.partial(shared_kernel, scale, min(256, rows)), g...  12.5 us
  transfers between devices with their start and end apart: 22, of which 11 were waited for; matrix products, arithmetic and copies ran while one was open for 6% of the time, Pallas kernels for 32%

profile of v3, /device:TPU:9, one launch (start us, length us, event | category | flops | bytes accessed | tf_op | source)
XLA Modules:
  0.0 373.4 jit_solution(3211809376073340781)
XLA Ops:
  6.5 1.5 slice.44
  8.1 0.8 collective-permute-start.10
  8.9 1.0 select_reduce_fusion
  11.9 7.4 %pack_tiles.5 = (bf16[12,2,128,128]{3,2,1,0:T(8,128)(2,1)}, bf16[12,2,128,128]{3,2,1,0:T(8,128)(2,1)}, bf16[12,2,128,128]{3,2,1,0:T(8,128)(2,1)}, bf16[12,2,128,128]{3,2,1,0:T(8,128)(2,1)}) custom-call(s32[192]{0:T(256)} %reshape.286.codes_ref, s32[16]{0:T(128)} %broadcast_xor_fusion.order_ref, bf16[1024,1536]{1,0:T(8,128)(2,1)} %keys_ref.5, ...), custom_call_target="tpu_custom_call" | custom-call | tf_op jit(solution)/shard_map/pack_tiles/pallas_call | solution.py:40
  19.3 1.3 slice_select_fusion
  20.6 1.8 collective-permute-start.11
  22.4 2.9 collective-permute-start.5
  25.3 11.2 %collective-permute-start.4 = (bf16[12,2,128,128]{3,2,1,0:T(8,128)(2,1)}, bf16[12,2,128,128]{3,2,1,0:T(8,128)(2,1)S(1)}, u32[]{:S(2)}, u32[]{:S(2)}) collective-permute-start(bf16[12,2,128,128]{3,2,1,0:T(8,128)(2,1)} %get-tuple-element.85), channel_id=1, source_target_pairs={{0,16},{2,18},{4,20},{6,22},{8,24},{10,26},{12,28},{14,30},{16,0},... | collective-permute-start | bytes 2359304 | tf_op jit(solution)/shard_map/ppermute | solution.py:353
  36.7 8.9 %pack_tiles.4 = (bf16[12,2,128,128]{3,2,1,0:T(8,128)(2,1)}, bf16[12,2,128,128]{3,2,1,0:T(8,128)(2,1)}, bf16[12,2,128,128]{3,2,1,0:T(8,128)(2,1)}, bf16[12,2,128,...) custom-call(s32[192]{0:T(256)} %reshape.286.codes_ref, ...), custom_call_target="tpu_custom_call" | custom-call | tf_op jit(solution)/shard_map/pack_tiles/pallas_call | solution.py:40
  48.2 1.4 pad_add_fusion
  50.8 0.9 collective-permute-done.refs_1_
  51.6 33.1 %collective-permute-start.1 = (bf16[12,2,128,128]{3,2,1,0:T(8,128)(2,1)}, bf16[12,2,128,128]{3,2,1,0:T(8,128)(2,1)S(1)}, u32[]{:S(2)}, u32[]{:S(2)}) collective-permute-start(bf16[12,2,128,128]{3,2,1,0:T(8,128)(2,1)} %get-tuple-element.76), channel_id=1, source_target_pairs={{0,2},{2,0},{4,6},{6,4},{8,10},{10,8},{12,14},{14,12},{16,18},{18,... | collective-permute-start | bytes 2359304 | tf_op jit(solution)/shard_map/ppermute | solution.py:353
  84.8 2.7 broadcast_select_fusion
  87.5 1.8 collective-permute-start.12
  90.3 0.9 copy-done.14
  91.1 1.2 collective-permute-start.2
  93.1 10.6 %collective-permute-done.4.refs_2_ = bf16[12,2,128,128]{3,2,1,0:T(8,128)(2,1)S(1)} collective-permute-done((bf16[12,2,128,128]{3,2,1,0:T(8,128)(2,1)}, bf16[12,2,128,128]{3,2,1,0:T(8,128)(2,1)S(1)}, u32[]{:S(2)}, u32[]{:S(2)}) %collective-permute-start.4) | collective-permute-done | bytes 786464 | tf_op jit(solution)/shard_map/ppermute | solution.py:353
  103.6 6.1 %collective-permute-done.3.refs_0_ = bf16[12,2,128,128]{3,2,1,0:T(8,128)(2,1)S(1)} collective-permute-done((bf16[12,2,128,128]{3,2,1,0:T(8,128)(2,1)}, bf16[12,2,128,128]{3,2,1,0:T(8,128)(2,1)S(1)}, u32[]{:S(2)}, u32[]{:S(2)}) %collective-permute-start.3) | collective-permute-done | bytes 786464 | tf_op jit(solution)/shard_map/ppermute | solution.py:353
  110.3 4.7 %collective-permute-start.9 = (bf16[12,2,128,128]{3,2,1,0:T(8,128)(2,1)}, bf16[12,2,128,128]{3,2,1,0:T(8,128)(2,1)}, u32[]{:S(2)}, u32[]{:S(2)}) collective-permute-start(bf16[12,2,128,128]{3,2,1,0:T(8,128)(2,1)} %get-tuple-element.90), channel_id=1, source_target_pairs={{0,22},{2,20},{4,18},{6,16},{8,30},{10,28},{12,26},{14,24},{16,6},... | collective-permute-start | bytes 2359304 | tf_op jit(solution)/shard_map/ppermute | solution.py:353
  115.7 8.7 %pack_tiles.3 = (bf16[12,2,128,128]{3,2,1,0:T(8,128)(2,1)}, bf16[12,2,128,128]{3,2,1,0:T(8,128)(2,1)}, bf16[12,2,128,128]{3,2,1,0:T(8,128)(2,1)}, bf16[12,2,128,...) custom-call(s32[192]{0:T(256)} %reshape.286.codes_ref, ...), custom_call_target="tpu_custom_call" | custom-call | tf_op jit(solution)/shard_map/pack_tiles/pallas_call | solution.py:40
  124.8 1.0 reshape.287.bias_ref
  126.3 1.1 copy-done.2
  127.4 1.9 copy-done.11
  129.3 1.1 copy-done.19
  130.4 1.1 copy-done.21
  131.6 1.1 copy-done.23
  132.7 1.1 copy-done.24
  133.8 19.1 %pool_tiles.7 = (bf16[12,128,1024]{2,1,0:T(8,128)(2,1)S(1)}, f32[12,128,1024]{2,1,0:T(8,128)S(1)}, f32[12,1,1024]{2,1,0:T(1,128)S(1)}, f32[12,1,1024]{2,1,0:T(1,128)S(1)}) custom-call(s32[12,16]{1,0:T(8,128)S(1)} %get-tuple-element.150.place_ref, s32[12,16]{1,0:T(8,128)S(1)} %get-tuple-element.149.entry_ref, s32[12]{0:T(128)S(1)} %get-tuple-element.170.count_ref, ...), custom_call_target="tpu_custom_call" | custom-call | tf_op jit(solution)/shard_map/pool_tiles/pallas_call | solution.py:222
  153.0 2.6 copy-done.7
  155.7 2.7 broadcast_select_fusion.1
  158.4 1.2 collective-permute-done.7.refs_6_
  159.6 8.4 %collective-permute-done.9.refs_5_ = bf16[12,2,128,128]{3,2,1,0:T(8,128)(2,1)} collective-permute-done((bf16[12,2,128,128]{3,2,1,0:T(8,128)(2,1)}, bf16[12,2,128,128]{3,2,1,0:T(8,128)(2,1)}, u32[]{:S(2)}, u32[]{:S(2)}) %collective-permute-start.9) | collective-permute-done | bytes 786464 | tf_op jit(solution)/shard_map/ppermute | solution.py:353
  168.0 15.8 %collective-permute-done.6.refs_4_ = bf16[12,2,128,128]{3,2,1,0:T(8,128)(2,1)} collective-permute-done((bf16[12,2,128,128]{3,2,1,0:T(8,128)(2,1)}, bf16[12,2,128,128]{3,2,1,0:T(8,128)(2,1)}, u32[]{:S(2)}, u32[]{:S(2)}) %collective-permute-start.6) | collective-permute-done | bytes 786464 | tf_op jit(solution)/shard_map/ppermute | solution.py:353
  184.4 3.3 collective-permute-start.17
  189.9 0.9 select_reduce_fusion.6
  190.8 1.2 copy-done.3
  192.0 3.7 copy-done.8
  195.8 1.1 copy-done.13
  196.9 1.1 copy-done.15
  198.0 1.1 copy-done.17
  199.2 31.3 %pool_tiles.8 = (f32[12,128,1024]{2,1,0:T(8,128)S(1)}, f32[12,1,1024]{2,1,0:T(1,128)S(1)}, f32[12,1,1024]{2,1,0:T(1,128)S(1)}) custom-call(s32[12,16]{1,0:T(8,128)S(1)} %get-tuple-element.142.place_ref, s32[12,16]{1,0:T(8,128)S(1)} %get-tuple-element.141.entry_ref, s32[12]{0:T(128)S(1)} %get-tuple-element.166.count_ref, s32[1]{0:T(128)} %bitcast.4.side_ref, ...), custom_call_target="tpu_custom_call" | custom-call | tf_op jit(solution)/shard_map/pool_tiles/pallas_call | solution.py:222
  230.5 2.6 copy-done.9
  233.1 7.1 %all-gather.2.cloned.1.call-done.k_ref.v_ref = bf16[2048,1536]{1,0:T(8,128)(2,1)} async-done(((bf16[512,1536]{1,0:T(8,128)(2,1)}), bf16[2048,1536]{1,0:T(8,128)(2,1)}) %all-gather.2.cloned.1.call-update) | async-done | bytes 6291472 | tf_op jit(solution)/shard_map/all_gather | solution.py:257
  240.2 2.8 copy-done.6
  243.0 2.8 copy-done.10
  245.8 12.5 %shared_tiles.1 = (f32[12,128,1024]{2,1,0:T(8,128)S(1)}, f32[12,1,1024]{2,1,0:T(1,128)S(1)}, f32[12,1,1024]{2,1,0:T(1,128)S(1)}) custom-call(bf16[12,128,1024]{2,1,0:T(8,128)(2,1)S(1)} %get-tuple-element.106.q_ref.qt_ref, bf16[2048,1536]{1,0:T(8,128)(2,1)S(1)} %copy-done.6, bf16[2048,1536]{1,0:T(8,128)(2,1)S(1)} %copy-done.6, ...), custom_call_target="tpu_custom_call" | custom-call | tf_op jit(solution)/shard_map/shared_tiles/pallas_call | solution.py:92
  258.3 32.2 %collective-permute-done.17.refs_2_ = bf16[12,2,128,128]{3,2,1,0:T(8,128)(2,1)} collective-permute-done((bf16[12,2,128,128]{3,2,1,0:T(8,128)(2,1)}, bf16[12,2,128,128]{3,2,1,0:T(8,128)(2,1)}, u32[]{:S(2)}, u32[]{:S(2)}) %collective-permute-start.17) | collective-permute-done | bytes 786464 | tf_op jit(solution)/shard_map/ppermute | solution.py:353
  290.5 15.7 %pool_tiles.9 = (f32[12,128,1024]{2,1,0:T(8,128)S(1)}, f32[12,1,1024]{2,1,0:T(1,128)S(1)}, f32[12,1,1024]{2,1,0:T(1,128)S(1)}) custom-call(s32[12,16]{1,0:T(8,128)S(1)} %get-tuple-element.144.place_ref, s32[12,16]{1,0:T(8,128)S(1)} %get-tuple-element.143.entry_ref, s32[12]{0:T(128)S(1)} %get-tuple-element.168.count_ref, s32[1]{0:T(128)} %bitcast.4.side_ref, ...), custom_call_target="tpu_custom_call" | custom-call | tf_op jit(solution)/shard_map/pool_tiles/pallas_call | solution.py:222
  306.1 7.4 %pool_tiles.10 = (f32[12,128,1024]{2,1,0:T(8,128)S(1)}, f32[12,1,1024]{2,1,0:T(1,128)S(1)}, f32[12,1,1024]{2,1,0:T(1,128)S(1)}) custom-call(s32[12,16]{1,0:T(8,128)S(1)} %get-tuple-element.146.place_ref, s32[12,16]{1,0:T(8,128)S(1)} %get-tuple-element.145.entry_ref, s32[12]{0:T(128)S(1)} %get-tuple-element.156.count_ref, s32[1]{0:T(128)} %bitcast.4.side_ref, ...), custom_call_target="tpu_custom_call" | custom-call | tf_op jit(solution)/shard_map/pool_tiles/pallas_call | solution.py:222
  313.5 10.1 %collective-permute-done.13.refs_0_ = bf16[12,2,128,128]{3,2,1,0:T(8,128)(2,1)} collective-permute-done((bf16[12,2,128,128]{3,2,1,0:T(8,128)(2,1)}, bf16[12,2,128,128]{3,2,1,0:T(8,128)(2,1)}, u32[]{:S(2)}, u32[]{:S(2)}) %collective-permute-start.13) | collective-permute-done | bytes 786464 | tf_op jit(solution)/shard_map/ppermute | solution.py:353
  323.6 5.5 %pool_tiles.11 = (bf16[512,512]{1,0:T(8,128)(2,1)S(1)}, bf16[512,512]{1,0:T(8,128)(2,1)}) custom-call(s32[12,16]{1,0:T(8,128)S(1)} %get-tuple-element.147.place_ref, s32[12,16]{1,0:T(8,128)S(1)} %get-tuple-element.148.entry_ref, s32[12]{0:T(128)S(1)} %get-tuple-element.159.count_ref, s32[1]{0:T(128)} %bitcast.4.side_ref, ...), custom_call_target="tpu_custom_call" | custom-call | tf_op jit(solution)/shard_map/pool_tiles/pallas_call | solution.py:222
  329.1 0.8 copy-done.25
  330.4 5.7 %pool_tiles.12 = (bf16[512,512]{1,0:T(8,128)(2,1)S(1)}, bf16[512,512]{1,0:T(8,128)(2,1)}) custom-call(s32[12,16]{1,0:T(8,128)S(1)} %get-tuple-element.147.place_ref, s32[12,16]{1,0:T(8,128)S(1)} %get-tuple-element.148.entry_ref, s32[12]{0:T(128)S(1)} %get-tuple-element.159.count_ref, s32[1]{0:T(128)} %bitcast.4.side_ref, ...), custom_call_target="tpu_custom_call" | custom-call | tf_op jit(solution)/shard_map/pool_tiles/pallas_call | solution.py:222
  336.2 0.8 copy-done.27
  337.0 0.8 collective-permute-start.19
  337.8 2.8 copy-done.1
  340.6 1.1 copy-done.5
  341.7 3.9 %pool_tiles.13 = (bf16[512,512]{1,0:T(8,128)(2,1)S(1)}, bf16[512,512]{1,0:T(8,128)(2,1)S(1)}) custom-call(s32[12,16]{1,0:T(8,128)S(1)} %get-tuple-element.147.place_ref, s32[12,16]{1,0:T(8,128)S(1)} %get-tuple-element.148.entry_ref, s32[12]{0:T(128)S(1)} %get-tuple-element.159.count_ref, s32[1]{0:T(128)} %bitcast.4.side_ref, ...), custom_call_target="tpu_custom_call" | custom-call | tf_op jit(solution)/shard_map/pool_tiles/pallas_call | solution.py:222
  345.7 0.9 collective-permute-start.20
  347.2 1.1 constant_dynamic-update-slice_fusion.2
  348.3 6.3 %collective-permute-done.19 = bf16[512,512]{1,0:T(8,128)(2,1)} collective-permute-done((bf16[512,512]{1,0:T(8,128)(2,1)}, bf16[512,512]{1,0:T(8,128)(2,1)}, u32[]{:S(2)}, u32[]{:S(2)}) %collective-permute-start.19) | collective-permute-done | bytes 524320 | tf_op jit(solution)/shard_map/ppermute | solution.py:397
  354.6 1.1 constant_dynamic-update-slice_fusion.1
  355.7 10.0 %collective-permute-done.20 = bf16[512,512]{1,0:T(8,128)(2,1)S(1)} collective-permute-done((bf16[512,512]{1,0:T(8,128)(2,1)S(1)}, bf16[512,512]{1,0:T(8,128)(2,1)S(1)}, u32[]{:S(2)}, u32[]{:S(2)}) %collective-permute-start.20) | collective-permute-done | bytes 524320 | tf_op jit(solution)/shard_map/ppermute | solution.py:397
  365.8 0.8 constant_dynamic-update-slice_fusion
  (127 shorter events, 13.5 us)
Async XLA Ops:
  6.5 4.8 %copy-start.36 = (s32[16]{0:T(128)S(1)}, s32[16]{0:T(128)}, u32[]{:S(2)}) copy-start(s32[16]{0:T(128)} %constant.138.clone) | copy-start | bytes 196
  6.5 2.3 copy-start.34
  6.5 2.3 copy-start.35
  6.5 233.7 %all-gather.2.cloned.1.call-start = ((), (), s32[]{:S(2)}) async-start(), calls=%async_computation | async-start | bytes 7864320 | tf_op jit(solution)/shard_map/all_gather | solution.py:257
  8.1 11.2 %collective-permute-start.10 = (bf16[512,1536]{1,0:T(8,128)(2,1)S(1)}, bf16[512,1536]{1,0:T(8,128)(2,1)S(1)}, u32[]{:S(2)}, u32[]{:S(2)}) collective-permute-start(bf16[512,1536]{1,0:T(8,128)(2,1)S(1)} %slice.44), channel_id=1, source_target_pairs={{0,4},{1,5}} | collective-permute-start | bytes 4718600 | tf_op jit(solution)/shard_map/ppermute | solution.py:241
  11.9 7.4 %copy-start.29 = (bf16[1024,1536]{1,0:T(8,128)(2,1)S(1)}, bf16[1024,1536]{1,0:T(8,128)(2,1)}, u32[]{:S(2)}) copy-start(bf16[1024,1536]{1,0:T(8,128)(2,1)} %keys_ref.5) | copy-start | bytes 9437188
  19.3 17.2 %copy-start.32 = (s32[16]{0:T(128)S(1)}, s32[16]{0:T(128)}, u32[]{:S(2)}) copy-start(s32[16]{0:T(128)} %broadcast_xor_fusion.order_ref) | copy-start | bytes 196
  20.6 64.2 %collective-permute-start.11 = (bf16[512,1536]{1,0:T(8,128)(2,1)}, bf16[512,1536]{1,0:T(8,128)(2,1)}, u32[]{:S(2)}, u32[]{:S(2)}) collective-permute-start(bf16[512,1536]{1,0:T(8,128)(2,1)} %slice_select_fusion), channel_id=1, source_target_pairs={{0,16},{4,20},{1,17},{5,21}} | collective-permute-start | bytes 4718600 | tf_op jit(solution)/shard_map/ppermute | solution.py:251
  22.4 29.2 %collective-permute-start = (bf16[12,2,128,128]{3,2,1,0:T(8,128)(2,1)}, bf16[12,2,128,128]{3,2,1,0:T(8,128)(2,1)S(1)}, u32[]{:S(2)}, u32[]{:S(2)}) collective-permute-start(bf16[12,2,128,128]{3,2,1,0:T(8,128)(2,1)} %get-tuple-element.75), channel_id=1, source_target_pairs={{0,8},{2,10},{4,12},{6,14},{8,0},{10,2},{12,4},{14,6},{16,24},{18,... | collective-permute-start | bytes 2359304 | tf_op jit(solution)/shard_map/ppermute | solution.py:353
  22.4 70.6 %collective-permute-start.5 = (bf16[12,2,128,128]{3,2,1,0:T(8,128)(2,1)}, bf16[12,2,128,128]{3,2,1,0:T(8,128)(2,1)S(1)}, u32[]{:S(2)}, u32[]{:S(2)}) collective-permute-start(bf16[12,2,128,128]{3,2,1,0:T(8,128)(2,1)} %get-tuple-element.86), channel_id=1, source_target_pairs={{0,18},{2,16},{4,22},{6,20},{8,26},{10,24},{12,30},{14,28},{16,2},... | collective-permute-start | bytes 2359304 | tf_op jit(solution)/shard_map/ppermute | solution.py:353
  25.3 78.3 %collective-permute-start.4 = (bf16[12,2,128,128]{3,2,1,0:T(8,128)(2,1)}, bf16[12,2,128,128]{3,2,1,0:T(8,128)(2,1)S(1)}, u32[]{:S(2)}, u32[]{:S(2)}) collective-permute-start(bf16[12,2,128,128]{3,2,1,0:T(8,128)(2,1)} %get-tuple-element.85), channel_id=1, source_target_pairs={{0,16},{2,18},{4,20},{6,22},{8,24},{10,26},{12,28},{14,30},{16,0},... | collective-permute-start | bytes 2359304 | tf_op jit(solution)/shard_map/ppermute | solution.py:353
  36.5 73.2 %collective-permute-start.3 = (bf16[12,2,128,128]{3,2,1,0:T(8,128)(2,1)}, bf16[12,2,128,128]{3,2,1,0:T(8,128)(2,1)S(1)}, u32[]{:S(2)}, u32[]{:S(2)}) collective-permute-start(bf16[12,2,128,128]{3,2,1,0:T(8,128)(2,1)} %get-tuple-element.81), channel_id=1, source_target_pairs={{0,10},{2,8},{4,14},{6,12},{8,2},{10,0},{12,6},{14,4},{16,26},{18,... | collective-permute-start | bytes 2359304 | tf_op jit(solution)/shard_map/ppermute | solution.py:353
  36.7 10.2 %copy-start.33 = (s32[16]{0:T(128)S(1)}, s32[16]{0:T(128)}, u32[]{:S(2)}) copy-start(s32[16]{0:T(128)} %broadcast_xor_fusion.order_ref) | copy-start | bytes 196
  45.6 46.8 %copy-start.31 = (s32[12,8,12]{2,1,0:T(8,128)S(1)}, s32[12,8,12]{2,1,0:T(8,128)}, u32[]{:S(2)}) copy-start(s32[12,8,12]{2,1,0:T(8,128)} %param.11) | copy-start | bytes 13828
  51.6 38.6 %copy-start.18 = (bf16[12,2,128,128]{3,2,1,0:T(8,128)(2,1)}, bf16[12,2,128,128]{3,2,1,0:T(8,128)(2,1)S(1)}, u32[]{:S(2)}) copy-start(bf16[12,2,128,128]{3,2,1,0:T(8,128)(2,1)S(1)} %collective-permute-done.refs_1_) | copy-start | bytes 2359300
  51.6 38.6 %collective-permute-start.1 = (bf16[12,2,128,128]{3,2,1,0:T(8,128)(2,1)}, bf16[12,2,128,128]{3,2,1,0:T(8,128)(2,1)S(1)}, u32[]{:S(2)}, u32[]{:S(2)}) collective-permute-start(bf16[12,2,128,128]{3,2,1,0:T(8,128)(2,1)} %get-tuple-element.76), channel_id=1, source_target_pairs={{0,2},{2,0},{4,6},{6,4},{8,10},{10,8},{12,14},{14,12},{16,18},{18,... | collective-permute-start | bytes 2359304 | tf_op jit(solution)/shard_map/ppermute | solution.py:353
  87.5 68.2 %collective-permute-start.12 = (bf16[512,1536]{1,0:T(8,128)(2,1)}, bf16[512,1536]{1,0:T(8,128)(2,1)}, u32[]{:S(2)}, u32[]{:S(2)}) collective-permute-start(bf16[512,1536]{1,0:T(8,128)(2,1)} %broadcast_select_fusion), channel_id=1, source_target_pairs={{0,8},{4,12},{16,24},{20,28},{1,9},{5,13},{17,25},{21,29}} | collective-permute-start | bytes 4718600 | tf_op jit(solution)/shard_map/ppermute | solution.py:251
  90.2 0.9 copy-start.14
  91.1 23.9 %collective-permute-start.2 = (bf16[12,2,128,128]{3,2,1,0:T(8,128)(2,1)}, bf16[12,2,128,128]{3,2,1,0:T(8,128)(2,1)S(1)}, u32[]{:S(2)}, u32[]{:S(2)}) collective-permute-start(bf16[12,2,128,128]{3,2,1,0:T(8,128)(2,1)} %get-tuple-element.78), channel_id=1, source_target_pairs={{0,4},{2,6},{4,0},{6,2},{8,12},{10,14},{12,8},{14,10},{16,20},{18,... | collective-permute-start | bytes 2359304 | tf_op jit(solution)/shard_map/ppermute | solution.py:353
  93.1 31.3 %copy-start.20 = (bf16[12,2,128,128]{3,2,1,0:T(8,128)(2,1)}, bf16[12,2,128,128]{3,2,1,0:T(8,128)(2,1)S(1)}, u32[]{:S(2)}) copy-start(bf16[12,2,128,128]{3,2,1,0:T(8,128)(2,1)S(1)} %collective-permute-done.5.refs_3_) | copy-start | bytes 2359300
  103.6 20.7 %copy-start.22 = (bf16[12,2,128,128]{3,2,1,0:T(8,128)(2,1)}, bf16[12,2,128,128]{3,2,1,0:T(8,128)(2,1)S(1)}, u32[]{:S(2)}) copy-start(bf16[12,2,128,128]{3,2,1,0:T(8,128)(2,1)S(1)} %collective-permute-done.4.refs_2_) | copy-start | bytes 2359300
  109.7 14.6 %copy-start.12 = (bf16[12,2,128,128]{3,2,1,0:T(8,128)(2,1)}, bf16[12,2,128,128]{3,2,1,0:T(8,128)(2,1)S(1)}, u32[]{:S(2)}) copy-start(bf16[12,2,128,128]{3,2,1,0:T(8,128)(2,1)S(1)} %collective-permute-done.3.refs_0_) | copy-start | bytes 2359300
  109.7 49.9 %collective-permute-start.7 = (bf16[12,2,128,128]{3,2,1,0:T(8,128)(2,1)}, bf16[12,2,128,128]{3,2,1,0:T(8,128)(2,1)}, u32[]{:S(2)}, u32[]{:S(2)}) collective-permute-start(bf16[12,2,128,128]{3,2,1,0:T(8,128)(2,1)} %get-tuple-element.84), channel_id=1, source_target_pairs={{0,14},{2,12},{4,10},{6,8},{8,6},{10,4},{12,2},{14,0},{16,30},{18,... | collective-permute-start | bytes 2359304 | tf_op jit(solution)/shard_map/ppermute | solution.py:353
  110.3 49.3 %collective-permute-start.8 = (bf16[12,2,128,128]{3,2,1,0:T(8,128)(2,1)}, bf16[12,2,128,128]{3,2,1,0:T(8,128)(2,1)}, u32[]{:S(2)}, u32[]{:S(2)}) collective-permute-start(bf16[12,2,128,128]{3,2,1,0:T(8,128)(2,1)} %get-tuple-element.88), channel_id=1, source_target_pairs={{0,20},{2,22},{4,16},{6,18},{8,28},{10,30},{12,24},{14,26},{16,4},... | collective-permute-start | bytes 2359304 | tf_op jit(solution)/shard_map/ppermute | solution.py:353
  110.3 57.7 %collective-permute-start.9 = (bf16[12,2,128,128]{3,2,1,0:T(8,128)(2,1)}, bf16[12,2,128,128]{3,2,1,0:T(8,128)(2,1)}, u32[]{:S(2)}, u32[]{:S(2)}) collective-permute-start(bf16[12,2,128,128]{3,2,1,0:T(8,128)(2,1)} %get-tuple-element.90), channel_id=1, source_target_pairs={{0,22},{2,20},{4,18},{6,16},{8,30},{10,28},{12,26},{14,24},{16,6},... | collective-permute-start | bytes 2359304 | tf_op jit(solution)/shard_map/ppermute | solution.py:353
  115.0 9.3 %copy-start.16 = (bf16[12,2,128,128]{3,2,1,0:T(8,128)(2,1)}, bf16[12,2,128,128]{3,2,1,0:T(8,128)(2,1)S(1)}, u32[]{:S(2)}) copy-start(bf16[12,2,128,128]{3,2,1,0:T(8,128)(2,1)S(1)} %collective-permute-done.2.refs_2_) | copy-start | bytes 2359300
  115.0 68.8 %collective-permute-start.6 = (bf16[12,2,128,128]{3,2,1,0:T(8,128)(2,1)}, bf16[12,2,128,128]{3,2,1,0:T(8,128)(2,1)}, u32[]{:S(2)}, u32[]{:S(2)}) collective-permute-start(bf16[12,2,128,128]{3,2,1,0:T(8,128)(2,1)} %get-tuple-element.80), channel_id=1, source_target_pairs={{0,6},{2,4},{4,2},{6,0},{8,14},{10,12},{12,10},{14,8},{16,22},{18,... | collective-permute-start | bytes 2359304 | tf_op jit(solution)/shard_map/ppermute | solution.py:353
  126.3 1.1 copy-start.2
  127.4 1.9 copy-start.11
  129.3 1.1 copy-start.19
  130.4 1.1 copy-start.21
  131.6 1.1 copy-start.23
  132.7 1.1 copy-start.24
  153.0 2.7 copy-start.7
  183.9 74.3 %collective-permute-start.15 = (bf16[12,2,128,128]{3,2,1,0:T(8,128)(2,1)}, bf16[12,2,128,128]{3,2,1,0:T(8,128)(2,1)}, u32[]{:S(2)}, u32[]{:S(2)}) collective-permute-start(bf16[12,2,128,128]{3,2,1,0:T(8,128)(2,1)} %get-tuple-element.109), channel_id=1, source_target_pairs={{0,12},{2,14},{4,8},{6,10},{8,4},{10,6},{12,0},{14,2},{16,28},{18,... | collective-permute-start | bytes 2359304 | tf_op jit(solution)/shard_map/ppermute | solution.py:353
  184.4 73.9 %collective-permute-start.16 = (bf16[12,2,128,128]{3,2,1,0:T(8,128)(2,1)}, bf16[12,2,128,128]{3,2,1,0:T(8,128)(2,1)}, u32[]{:S(2)}, u32[]{:S(2)}) collective-permute-start(bf16[12,2,128,128]{3,2,1,0:T(8,128)(2,1)} %get-tuple-element.110), channel_id=1, source_target_pairs={{0,24},{2,26},{4,28},{6,30},{8,16},{10,18},{12,20},{14,22},{16,8},... | collective-permute-start | bytes 2359304 | tf_op jit(solution)/shard_map/ppermute | solution.py:353
  184.4 106.0 %collective-permute-start.17 = (bf16[12,2,128,128]{3,2,1,0:T(8,128)(2,1)}, bf16[12,2,128,128]{3,2,1,0:T(8,128)(2,1)}, u32[]{:S(2)}, u32[]{:S(2)}) collective-permute-start(bf16[12,2,128,128]{3,2,1,0:T(8,128)(2,1)} %get-tuple-element.111), channel_id=1, source_target_pairs={{0,26},{2,24},{4,30},{6,28},{8,18},{10,16},{12,22},{14,20},{16,10}... | collective-permute-start | bytes 2359304 | tf_op jit(solution)/shard_map/ppermute | solution.py:353
  187.7 118.4 %collective-permute-start.14 = (bf16[12,2,128,128]{3,2,1,0:T(8,128)(2,1)}, bf16[12,2,128,128]{3,2,1,0:T(8,128)(2,1)}, u32[]{:S(2)}, u32[]{:S(2)}) collective-permute-start(bf16[12,2,128,128]{3,2,1,0:T(8,128)(2,1)} %get-tuple-element.108), channel_id=1, source_target_pairs={{0,28},{2,30},{4,24},{6,26},{8,20},{10,22},{12,16},{14,18},{16,12}... | collective-permute-start | bytes 2359304 | tf_op jit(solution)/shard_map/ppermute | solution.py:353
  188.4 135.2 %collective-permute-start.13 = (bf16[12,2,128,128]{3,2,1,0:T(8,128)(2,1)}, bf16[12,2,128,128]{3,2,1,0:T(8,128)(2,1)}, u32[]{:S(2)}, u32[]{:S(2)}) collective-permute-start(bf16[12,2,128,128]{3,2,1,0:T(8,128)(2,1)} %get-tuple-element.107), channel_id=1, source_target_pairs={{0,30},{2,28},{4,26},{6,24},{8,22},{10,20},{12,18},{14,16},{16,14}... | collective-permute-start | bytes 2359304 | tf_op jit(solution)/shard_map/ppermute | solution.py:353
  190.8 1.2 copy-start.3
  192.0 3.7 copy-start.8
  195.7 1.1 copy-start.13
  196.9 1.1 copy-start.15
  198.0 1.1 copy-start.17
  230.5 2.7 copy-start.9
  240.2 2.8 copy-start.6
  243.0 2.8 copy-start.10
  245.8 44.7 %copy-start.4 = (f32[12,16,1024]{2,1,0:T(8,128)S(1)}, f32[12,16,1024]{2,1,0:T(8,128)}, u32[]{:S(2)}) copy-start(f32[12,16,1024]{2,1,0:T(8,128)} %reshape.287.bias_ref) | copy-start | bytes 2359300
  313.5 16.9 %copy-start = (f32[12,128,1024]{2,1,0:T(8,128)}, f32[12,128,1024]{2,1,0:T(8,128)S(1)}, u32[]{:S(2)}) copy-start(f32[12,128,1024]{2,1,0:T(8,128)S(1)} %get-tuple-element.132.refs_1_) | copy-start | bytes 18874372
  329.1 0.8 copy-start.25
  329.9 17.3 %collective-permute-start.18 = (bf16[512,512]{1,0:T(8,128)(2,1)}, bf16[512,512]{1,0:T(8,128)(2,1)}, u32[]{:S(2)}, u32[]{:S(2)}) collective-permute-start(bf16[512,512]{1,0:T(8,128)(2,1)} %get-tuple-element.138), channel_id=1, source_target_pairs={{0,1},{1,0},{2,3},{3,2},{4,5},{5,4},{6,7},{7,6},{8,9},{9,8},{10,11... | collective-permute-start | bytes 1572872 | tf_op jit(solution)/shard_map/ppermute | solution.py:397
  336.2 0.8 copy-start.27
  337.0 17.6 %collective-permute-start.19 = (bf16[512,512]{1,0:T(8,128)(2,1)}, bf16[512,512]{1,0:T(8,128)(2,1)}, u32[]{:S(2)}, u32[]{:S(2)}) collective-permute-start(bf16[512,512]{1,0:T(8,128)(2,1)} %get-tuple-element.139), channel_id=1, source_target_pairs={{0,1},{1,0},{2,3},{3,2},{4,5},{5,4},{6,7},{7,6},{8,9},{9,8},{10,11... | collective-permute-start | bytes 1572872 | tf_op jit(solution)/shard_map/ppermute | solution.py:397
  337.8 2.8 copy-start.1
  340.6 1.1 copy-start.5
  345.7 1.3 copy-start.26
  345.7 1.3 copy-start.28
  345.7 20.1 %collective-permute-start.20 = (bf16[512,512]{1,0:T(8,128)(2,1)S(1)}, bf16[512,512]{1,0:T(8,128)(2,1)S(1)}, u32[]{:S(2)}, u32[]{:S(2)}) collective-permute-start(bf16[512,512]{1,0:T(8,128)(2,1)S(1)} %get-tuple-element.140), channel_id=1, source_target_pairs={{0,1},{1,0},{2,3},{3,2},{4,5},{5,4},{6,7},{7,6},{8,9},{9,8},{10,11... | collective-permute-start | bytes 1572872 | tf_op jit(solution)/shard_map/ppermute | solution.py:397
  355.7 10.0 %copy-start.30 = (bf16[512,3072]{1,0:T(8,128)(2,1)}, bf16[512,3072]{1,0:T(8,128)(2,1)S(1)}, u32[]{:S(2)}) copy-start(bf16[512,3072]{1,0:T(8,128)(2,1)S(1)} %constant_dynamic-update-slice_fusion.1) | copy-start | bytes 9437188
Sparse Core Ops, SparseCore 0:
  183.9 56.2 all-gather.1

commit v4 on v3

--- a/solution.py
+++ b/solution.py
@@ -338,7 +338,7 @@
         tables = (*tables[:2], 0 * tables[2], tables[3])
         last = functools.partial(part, tables, qt, [got], state=state)
     else:
-        order = [4, 8, 5, 9, 1, 2, 10, 3, 11, 7, 6, 12, 13, 14, 15, 0]
+        order = [4, 8, 5, 9, 1, 2, 10, 3, 11, 6, 7, 12, 13, 14, 15, 0]
         partners = me ^ jnp.asarray(order, jnp.int32)
         where = {d: i for i, d in enumerate(order)}
 
@@ -358,16 +358,19 @@
             return lax.optimization_barrier(values)
 
         parts = {}
-        for lo, hi in ((0, 4), (4, 10), (10, len(order))):
-            packed = pack(send, partners, keys, values, lo, [1] * (hi - lo), bound, head_size)
-            parts.update(zip(order[lo:hi], packed))
+        for ds in ([4, 8, 5, 9], [1, 2, 10, 3, 11], [6, 12, 13, 14, 15, 0]):
+            sizes = [2 if d == 6 else 1 for d in ds]
+            lo = order.index(ds[0])
+            parts.update(
+                zip(ds, pack(send, partners, keys, values, lo, sizes, bound, head_size))
+            )
 
         piece = share_halves(shared_keys, shared_values, "seq", quarter)
-        first = [5, 1, 2, 10, 3, 11, 7]
+        first = [5, 1, 2, 10, 3, 11]
         got = move([4, 8, 5, 9])
         piece, parts[4] = fence(piece, parts[4])
         piece = share_step(piece, "seq", quarter, half_count)
-        for d, earlier in ((1, 4), (10, 8), (2, 1), (11, 9), (3, 2), (7, 5)):
+        for d, earlier in ((1, 4), (10, 8), (2, 1), (11, 9), (3, 2)):
             parts[d], got[earlier] = fence(parts[d], got[earlier])
             got.update(move([d]))
         piece = share_step(piece, "seq", quarter, quarter)
@@ -378,9 +381,14 @@
         shared = share_within(piece, "seq", quarter)
         new = move([6, 12, 13, 14, 15])
         state = use(state, got, first)
+        state = use(state, new, [12])
+        shared, *state = fence(shared, *state)
         state = shared_part(qt, shared, state, scale)
-        state = use(state, new, [6, 12, 13])
-        state = use(state, new, [14])
+        both, *state = fence(new[6], *state)
+        new[6], parts[1] = both[:bound], both[bound:]
+        new[7] = move([1])[1]
+        state = use(state, new, [6, 13])
+        state = use(state, new, [7, 14])
         last = functools.partial(use, state, new, [15])
 
     if split == 1:

time: 375 us -> 373 us (level)
  waiting for transfers between devices: 109 us -> 99.7 us
    ppermute x15, waiting for transfers between devices: 85.2 us -> 64.2 us  [move(): lax.ppermute(parts[d], 'seq', [(j, j ^ d) for j in range(seq_count)])]
    all_gather x1, waiting for transfers between devices: 7.08 us -> 18.8 us  [share_within(): lax.all_gather(piece, axis, axis=0, tiled=True, axis_index_groups=groups)]
    pallas_call x7 -> x8, Pallas kernels: 88.6 us -> 87.9 us  [pool_part(): pl.pallas_call(functools.partial(pool_kernel, scale, min(256, rows), len(...]
    unnamed x75 -> x79, local copies, waits for them, and re-layouts: 33.4 us -> 33.2 us
  transfers between devices with their start and end apart: 22 -> 22, of which waited for: 11 -> 8; matrix products, arithmetic and copies ran while one was open for 6% -> 7% of each run, Pallas kernels for 32% -> 32%
where the time goes in v4:
time: 373 us; the launch traced here: 371 us
  Pallas kernels  125 us (34%)
  waiting for transfers between devices  99.7 us (27%)
  starting transfers between devices  68.6 us (18%)
  local copies, waits for them, and re-layouts  44.8 us (12%)
  other arithmetic  18.8 us (5%)
  between operations  14 us (4%)
    pallas_call x8, Pallas kernels, pool_part(): pl.pallas_call(functools.partial(pool_kernel, scale, min(256, rows), len(...  87.9 us
    ppermute x15, waiting for transfers between devices, move(): lax.ppermute(parts[d], 'seq', [(j, j ^ d) for j in range(seq_count)])  64.2 us
    ppermute x15, starting transfers between devices, move(): lax.ppermute(parts[d], 'seq', [(j, j ^ d) for j in range(seq_count)])  61.4 us
    unnamed x79, local copies, waits for them, and re-layouts  33.2 us
    pallas_call x3, Pallas kernels, pack(): pl.pallas_call(functools.partial(pack_kernel, lo, bound, head_size), grid...  24.9 us
    all_gather x1, waiting for transfers between devices, share_within(): lax.all_gather(piece, axis, axis=0, tiled=True, axis_index_groups=groups)  18.8 us
    ppermute x3, waiting for transfers between devices, body(): arrived.append((lo, lax.ppermute(away, 'head', [(0, 1), (1, 0)])))  16.6 us
    pallas_call x1, Pallas kernels, shared_part(): pl.pallas_call(functools.partial(shared_kernel, scale, min(256, rows)), g...  12.3 us
  transfers between devices with their start and end apart: 22, of which 8 were waited for; matrix products, arithmetic and copies ran while one was open for 7% of the time, Pallas kernels for 32%

profile of v4, /device:TPU:9, one launch (start us, length us, event | category | flops | bytes accessed | tf_op | source)
XLA Modules:
  0.0 371.3 jit_solution(11970896561505137944)
XLA Ops:
  6.5 2.7 slice.55
  9.2 1.8 collective-permute-start.9
  11.0 1.0 select_reduce_fusion
  14.0 7.4 %pack_tiles.5 = (bf16[12,2,128,128]{3,2,1,0:T(8,128)(2,1)}, bf16[12,2,128,128]{3,2,1,0:T(8,128)(2,1)}, bf16[12,2,128,128]{3,2,1,0:T(8,128)(2,1)}, bf16[12,2,128,128]{3,2,1,0:T(8,128)(2,1)}) custom-call(s32[192]{0:T(256)} %reshape.301.codes_ref, s32[16]{0:T(128)} %broadcast_xor_fusion.order_ref, bf16[1024,1536]{1,0:T(8,128)(2,1)} %keys_ref.5, ...), custom_call_target="tpu_custom_call" | custom-call | tf_op jit(solution)/shard_map/pack_tiles/pallas_call | solution.py:40
  21.4 2.5 collective-permute-start.3
  23.9 3.9 %collective-permute-start.4 = (bf16[12,2,128,128]{3,2,1,0:T(8,128)(2,1)}, bf16[12,2,128,128]{3,2,1,0:T(8,128)(2,1)S(1)}, u32[]{:S(2)}, u32[]{:S(2)}) collective-permute-start(bf16[12,2,128,128]{3,2,1,0:T(8,128)(2,1)} %get-tuple-element.91), channel_id=1, source_target_pairs={{0,18},{2,16},{4,22},{6,20},{8,26},{10,24},{12,30},{14,28},{16,2},... | collective-permute-start | bytes 2359304 | tf_op jit(solution)/shard_map/ppermute | solution.py:353
  27.9 8.0 %pack_tiles.4 = (bf16[12,2,128,128]{3,2,1,0:T(8,128)(2,1)}, bf16[12,2,128,128]{3,2,1,0:T(8,128)(2,1)}, bf16[12,2,128,128]{3,2,1,0:T(8,128)(2,1)}, bf16[12,2,128,...) custom-call(s32[192]{0:T(256)} %reshape.301.codes_ref, s32[16]{0:T(128)} %broadcast_xor_fusion.order_ref, ...), custom_call_target="tpu_custom_call" | custom-call | tf_op jit(solution)/shard_map/pack_tiles/pallas_call | solution.py:40
  37.0 1.7 slice_select_fusion
  38.6 0.9 collective-permute-start.10
  41.0 1.3 pad_add_fusion
  42.3 2.5 pad_add_fusion.1
  46.1 7.1 %collective-permute-done.refs_1_ = bf16[12,2,128,128]{3,2,1,0:T(8,128)(2,1)S(1)} collective-permute-done((bf16[12,2,128,128]{3,2,1,0:T(8,128)(2,1)}, bf16[12,2,128,128]{3,2,1,0:T(8,128)(2,1)S(1)}, u32[]{:S(2)}, u32[]{:S(2)}) %collective-permute-start) | collective-permute-done | bytes 786464 | tf_op jit(solution)/shard_map/ppermute | solution.py:353
  53.3 5.4 %collective-permute-start.1 = (bf16[12,2,128,128]{3,2,1,0:T(8,128)(2,1)S(1)}, bf16[12,2,128,128]{3,2,1,0:T(8,128)(2,1)S(1)}, u32[]{:S(2)}, u32[]{:S(2)}) collective-permute-start(bf16[12,2,128,128]{3,2,1,0:T(8,128)(2,1)S(1)} %copy-done.37), channel_id=1, source_target_pairs={{0,2},{2,0},{4,6},{6,4},{8,10},{10,8},{12,14},{14,12},{16,18},{18,... | collective-permute-start | bytes 2359304 | tf_op jit(solution)/shard_map/ppermute | solution.py:353
  58.7 1.4 broadcast_select_fusion
  60.1 1.8 collective-permute-start.11
  62.9 0.9 copy-done.15
  64.6 26.0 %collective-permute-done.4.refs_3_ = bf16[12,2,128,128]{3,2,1,0:T(8,128)(2,1)S(1)} collective-permute-done((bf16[12,2,128,128]{3,2,1,0:T(8,128)(2,1)}, bf16[12,2,128,128]{3,2,1,0:T(8,128)(2,1)S(1)}, u32[]{:S(2)}, u32[]{:S(2)}) %collective-permute-start.4) | collective-permute-done | bytes 786464 | tf_op jit(solution)/shard_map/ppermute | solution.py:353
  90.6 30.5 %collective-permute-start.7 = (bf16[12,2,128,128]{3,2,1,0:T(8,128)(2,1)}, bf16[12,2,128,128]{3,2,1,0:T(8,128)(2,1)}, u32[]{:S(2)}, u32[]{:S(2)}) collective-permute-start(bf16[12,2,128,128]{3,2,1,0:T(8,128)(2,1)} %get-tuple-element.93), channel_id=1, source_target_pairs={{0,20},{2,22},{4,16},{6,18},{8,28},{10,30},{12,24},{14,26},{16,4},... | collective-permute-start | bytes 2359304 | tf_op jit(solution)/shard_map/ppermute | solution.py:353
  121.8 9.6 %pack_tiles.3 = (bf16[24,2,128,128]{3,2,1,0:T(8,128)(2,1)}, bf16[12,2,128,128]{3,2,1,0:T(8,128)(2,1)}, bf16[12,2,128,128]{3,2,1,0:T(8,128)(2,1)}, bf16[12,2,128,...) custom-call(s32[192]{0:T(256)} %reshape.301.codes_ref, ...), custom_call_target="tpu_custom_call" | custom-call | tf_op jit(solution)/shard_map/pack_tiles/pallas_call | solution.py:40
  131.8 1.0 reshape.302.bias_ref
  133.3 1.1 copy-done
  134.4 1.9 copy-done.14
  136.3 1.1 copy-done.20
  137.4 1.1 copy-done.22
  138.6 1.1 copy-done.24
  139.7 1.1 copy-done.25
  140.8 19.6 %pool_tiles.8 = (bf16[12,128,1024]{2,1,0:T(8,128)(2,1)S(1)}, f32[12,128,1024]{2,1,0:T(8,128)S(1)}, f32[12,1,1024]{2,1,0:T(1,128)S(1)}, f32[12,1,1024]{2,1,0:T(1,128)S(1)}) custom-call(s32[12,16]{1,0:T(8,128)S(1)} %get-tuple-element.170.place_ref, s32[12,16]{1,0:T(8,128)S(1)} %get-tuple-element.169.entry_ref, s32[12]{0:T(128)S(1)} %get-tuple-element.196.count_ref, ...), custom_call_target="tpu_custom_call" | custom-call | tf_op jit(solution)/shard_map/pool_tiles/pallas_call | solution.py:222
  160.4 2.6 copy-done.10
  163.1 2.8 broadcast_select_fusion.1
  165.9 12.0 %collective-permute-done.8.refs_5_ = bf16[12,2,128,128]{3,2,1,0:T(8,128)(2,1)} collective-permute-done((bf16[12,2,128,128]{3,2,1,0:T(8,128)(2,1)}, bf16[12,2,128,128]{3,2,1,0:T(8,128)(2,1)}, u32[]{:S(2)}, u32[]{:S(2)}) %collective-permute-start.8) | collective-permute-done | bytes 786464 | tf_op jit(solution)/shard_map/ppermute | solution.py:353
  177.9 4.7 %collective-permute-start.13 = (bf16[24,2,128,128]{3,2,1,0:T(8,128)(2,1)}, bf16[24,2,128,128]{3,2,1,0:T(8,128)(2,1)}, u32[]{:S(2)}, u32[]{:S(2)}) collective-permute-start(bf16[24,2,128,128]{3,2,1,0:T(8,128)(2,1)} %get-tuple-element.112), channel_id=1, source_target_pairs={{0,12},{2,14},{4,8},{6,10},{8,4},{10,6},{12,0},{14,2},{16,28},{18,... | collective-permute-start | bytes 4718600 | tf_op jit(solution)/shard_map/ppermute | solution.py:353
  182.6 4.5 %collective-permute-start.14 = (bf16[12,2,128,128]{3,2,1,0:T(8,128)(2,1)}, bf16[12,2,128,128]{3,2,1,0:T(8,128)(2,1)S(1)}, u32[]{:S(2)}, u32[]{:S(2)}) collective-permute-start(bf16[12,2,128,128]{3,2,1,0:T(8,128)(2,1)} %get-tuple-element.114), channel_id=1, source_target_pairs={{0,24},{2,26},{4,28},{6,30},{8,16},{10,18},{12,20},{14,22},{16,8},... | collective-permute-start | bytes 2359304 | tf_op jit(solution)/shard_map/ppermute | solution.py:353
  187.7 0.9 select_reduce_fusion.6
  188.7 2.0 collective-permute-start.16
  190.8 1.2 copy-done.1
  192.0 3.5 copy-done.11
  195.5 1.2 copy-done.16
  196.7 1.2 copy-done.18
  197.9 26.6 %pool_tiles.9 = (f32[12,128,1024]{2,1,0:T(8,128)S(1)}, f32[12,1,1024]{2,1,0:T(1,128)S(1)}, f32[12,1,1024]{2,1,0:T(1,128)S(1)}) custom-call(s32[12,16]{1,0:T(8,128)S(1)} %get-tuple-element.162.place_ref, s32[12,16]{1,0:T(8,128)S(1)} %get-tuple-element.161.entry_ref, s32[12]{0:T(128)S(1)} %get-tuple-element.192.count_ref, s32[1]{0:T(128)} %bitcast.4.side_ref, ...), custom_call_target="tpu_custom_call" | custom-call | tf_op jit(solution)/shard_map/pool_tiles/pallas_call | solution.py:222
  224.5 6.7 %pool_tiles.10 = (f32[12,128,1024]{2,1,0:T(8,128)S(1)}, f32[12,1,1024]{2,1,0:T(1,128)S(1)}, f32[12,1,1024]{2,1,0:T(1,128)S(1)}) custom-call(s32[12,16]{1,0:T(8,128)S(1)} %get-tuple-element.164.place_ref, s32[12,16]{1,0:T(8,128)S(1)} %get-tuple-element.163.entry_ref, s32[12]{0:T(128)S(1)} %get-tuple-element.177.count_ref, s32[1]{0:T(128)} %bitcast.4.side_ref, ...), custom_call_target="tpu_custom_call" | custom-call | tf_op jit(solution)/shard_map/pool_tiles/pallas_call | solution.py:222
  231.2 2.6 copy-done.12
  233.9 18.8 %all-gather.2.cloned.1.call-done.k_ref.v_ref = bf16[2048,1536]{1,0:T(8,128)(2,1)} async-done(((bf16[512,1536]{1,0:T(8,128)(2,1)}), bf16[2048,1536]{1,0:T(8,128)(2,1)}) %all-gather.2.cloned.1.call-update) | async-done | bytes 6291472 | tf_op jit(solution)/shard_map/all_gather | solution.py:257
  252.7 2.8 copy-done.7
  255.5 2.8 copy-done.13
  258.3 12.3 %shared_tiles.1 = (f32[12,128,1024]{2,1,0:T(8,128)S(1)}, f32[12,1,1024]{2,1,0:T(1,128)S(1)}, f32[12,1,1024]{2,1,0:T(1,128)S(1)}) custom-call(bf16[12,128,1024]{2,1,0:T(8,128)(2,1)S(1)} %get-tuple-element.110.q_ref.qt_ref, bf16[2048,1536]{1,0:T(8,128)(2,1)S(1)} %copy-done.7, bf16[2048,1536]{1,0:T(8,128)(2,1)S(1)} %copy-done.7, ...), custom_call_target="tpu_custom_call" | custom-call | tf_op jit(solution)/shard_map/shared_tiles/pallas_call | solution.py:92
  270.7 1.7 fusion.28
  272.6 6.9 %collective-permute-start.12 = (bf16[12,2,128,128]{3,2,1,0:T(8,128)(2,1)S(1)}, bf16[12,2,128,128]{3,2,1,0:T(8,128)(2,1)S(1)}, u32[]{:S(2)}, u32[]{:S(2)}) collective-permute-start(bf16[12,2,128,128]{3,2,1,0:T(8,128)(2,1)S(1)} %copy-done.36), channel_id=1, source_target_pairs={{0,30},{2,28},{4,26},{6,24},{8,22},{10,20},{12,18},{14,16},{16,14}... | collective-permute-start | bytes 2359304 | tf_op jit(solution)/shard_map/ppermute | solution.py:353
  280.7 11.5 %pool_tiles.11 = (f32[12,128,1024]{2,1,0:T(8,128)S(1)}, f32[12,1,1024]{2,1,0:T(1,128)S(1)}, f32[12,1,1024]{2,1,0:T(1,128)S(1)}) custom-call(s32[12,16]{1,0:T(8,128)S(1)} %get-tuple-element.158.place_ref, s32[12,16]{1,0:T(8,128)S(1)} %get-tuple-element.157.entry_ref, s32[12]{0:T(128)S(1)} %get-tuple-element.190.count_ref, s32[1]{0:T(128)} %bitcast.4.side_ref, ...), custom_call_target="tpu_custom_call" | custom-call | tf_op jit(solution)/shard_map/pool_tiles/pallas_call | solution.py:222
  292.3 13.6 %collective-permute-done.16.refs_1_ = bf16[12,2,128,128]{3,2,1,0:T(8,128)(2,1)} collective-permute-done((bf16[12,2,128,128]{3,2,1,0:T(8,128)(2,1)}, bf16[12,2,128,128]{3,2,1,0:T(8,128)(2,1)}, u32[]{:S(2)}, u32[]{:S(2)}) %collective-permute-start.16) | collective-permute-done | bytes 786464 | tf_op jit(solution)/shard_map/ppermute | solution.py:353
  305.9 11.2 %pool_tiles.12 = (f32[12,128,1024]{2,1,0:T(8,128)S(1)}, f32[12,1,1024]{2,1,0:T(1,128)S(1)}, f32[12,1,1024]{2,1,0:T(1,128)S(1)}) custom-call(s32[12,16]{1,0:T(8,128)S(1)} %get-tuple-element.168.place_ref, s32[12,16]{1,0:T(8,128)S(1)} %get-tuple-element.167.entry_ref, s32[12]{0:T(128)S(1)} %get-tuple-element.194.count_ref, s32[1]{0:T(128)} %bitcast.4.side_ref, ...), custom_call_target="tpu_custom_call" | custom-call | tf_op jit(solution)/shard_map/pool_tiles/pallas_call | solution.py:222
  317.1 5.4 %collective-permute-done.12.refs_0_ = bf16[12,2,128,128]{3,2,1,0:T(8,128)(2,1)S(1)} collective-permute-done((bf16[12,2,128,128]{3,2,1,0:T(8,128)(2,1)S(1)}, bf16[12,2,128,128]{3,2,1,0:T(8,128)(2,1)S(1)}, u32[]{:S(2)}, u32[]{:S(2)}) %collective-permute-start.12) | collective-permute-done | bytes 786464 | tf_op jit(solution)/shard_map/ppermute | solution.py:353
  322.4 5.2 %pool_tiles.13 = (bf16[512,512]{1,0:T(8,128)(2,1)S(1)}, bf16[512,512]{1,0:T(8,128)(2,1)}) custom-call(s32[12,16]{1,0:T(8,128)S(1)} %get-tuple-element.165.place_ref, s32[12,16]{1,0:T(8,128)S(1)} %get-tuple-element.166.entry_ref, s32[12]{0:T(128)S(1)} %get-tuple-element.180.count_ref, s32[1]{0:T(128)} %bitcast.4.side_ref, ...), custom_call_target="tpu_custom_call" | custom-call | tf_op jit(solution)/shard_map/pool_tiles/pallas_call | solution.py:222
  327.7 1.3 collective-permute-start.18
  329.0 3.7 pool_tiles.14
  332.6 0.9 copy-done.28
  333.5 1.3 collective-permute-start.19
  334.8 1.1 copy-done.4
  336.0 2.8 copy-done.6
  338.7 1.1 copy-done.9
  339.9 3.5 pool_tiles.15
  344.7 1.1 constant_dynamic-update-slice_fusion.2
  345.9 7.2 %collective-permute-done.19 = bf16[512,512]{1,0:T(8,128)(2,1)} collective-permute-done((bf16[512,512]{1,0:T(8,128)(2,1)}, bf16[512,512]{1,0:T(8,128)(2,1)}, u32[]{:S(2)}, u32[]{:S(2)}) %collective-permute-start.19) | collective-permute-done | bytes 524320 | tf_op jit(solution)/shard_map/ppermute | solution.py:405
  353.0 1.1 constant_dynamic-update-slice_fusion.1
  354.2 9.4 %collective-permute-done.20 = bf16[512,512]{1,0:T(8,128)(2,1)S(1)} collective-permute-done((bf16[512,512]{1,0:T(8,128)(2,1)S(1)}, bf16[512,512]{1,0:T(8,128)(2,1)S(1)}, u32[]{:S(2)}, u32[]{:S(2)}) %collective-permute-start.20) | collective-permute-done | bytes 524320 | tf_op jit(solution)/shard_map/ppermute | solution.py:405
  (136 shorter events, 13.5 us)
Async XLA Ops:
  6.5 7.0 %copy-start.38 = (s32[16]{0:T(128)S(1)}, s32[16]{0:T(128)}, u32[]{:S(2)}) copy-start(s32[16]{0:T(128)} %constant.138.clone) | copy-start | bytes 196
  6.5 4.5 %copy-start.34 = (s32[12,256]{1,0:T(8,128)S(1)}, s32[12,256]{1,0:T(8,128)}, u32[]{:S(2)}) copy-start(s32[12,256]{1,0:T(8,128)} %param.10) | copy-start | bytes 36868
  6.5 4.5 %copy-start.35 = (s32[128]{0:T(128)S(1)}, s32[128]{0:T(128)}, u32[]{:S(2)}) copy-start(s32[128]{0:T(128)} %param.12) | copy-start | bytes 1540
  6.5 246.2 %all-gather.2.cloned.1.call-start = ((), (), s32[]{:S(2)}) async-start(), calls=%async_computation | async-start | bytes 7864320 | tf_op jit(solution)/shard_map/all_gather | solution.py:257
  9.2 27.7 %collective-permute-start.9 = (bf16[512,1536]{1,0:T(8,128)(2,1)}, bf16[512,1536]{1,0:T(8,128)(2,1)}, u32[]{:S(2)}, u32[]{:S(2)}) collective-permute-start(bf16[512,1536]{1,0:T(8,128)(2,1)} %slice.55), channel_id=1, source_target_pairs={{0,4},{1,5}} | collective-permute-start | bytes 4718600 | tf_op jit(solution)/shard_map/ppermute | solution.py:241
  14.0 13.8 %copy-start.31 = (s32[16]{0:T(128)S(1)}, s32[16]{0:T(128)}, u32[]{:S(2)}) copy-start(s32[16]{0:T(128)} %broadcast_xor_fusion.order_ref) | copy-start | bytes 196
  21.4 31.9 %collective-permute-start = (bf16[12,2,128,128]{3,2,1,0:T(8,128)(2,1)}, bf16[12,2,128,128]{3,2,1,0:T(8,128)(2,1)S(1)}, u32[]{:S(2)}, u32[]{:S(2)}) collective-permute-start(bf16[12,2,128,128]{3,2,1,0:T(8,128)(2,1)} %get-tuple-element.82), channel_id=1, source_target_pairs={{0,8},{2,10},{4,12},{6,14},{8,0},{10,2},{12,4},{14,6},{16,24},{18,... | collective-permute-start | bytes 2359304 | tf_op jit(solution)/shard_map/ppermute | solution.py:353
  21.4 43.1 %collective-permute-start.3 = (bf16[12,2,128,128]{3,2,1,0:T(8,128)(2,1)}, bf16[12,2,128,128]{3,2,1,0:T(8,128)(2,1)S(1)}, u32[]{:S(2)}, u32[]{:S(2)}) collective-permute-start(bf16[12,2,128,128]{3,2,1,0:T(8,128)(2,1)} %get-tuple-element.90), channel_id=1, source_target_pairs={{0,16},{2,18},{4,20},{6,22},{8,24},{10,26},{12,28},{14,30},{16,0},... | collective-permute-start | bytes 2359304 | tf_op jit(solution)/shard_map/ppermute | solution.py:353
  23.9 66.7 %collective-permute-start.4 = (bf16[12,2,128,128]{3,2,1,0:T(8,128)(2,1)}, bf16[12,2,128,128]{3,2,1,0:T(8,128)(2,1)S(1)}, u32[]{:S(2)}, u32[]{:S(2)}) collective-permute-start(bf16[12,2,128,128]{3,2,1,0:T(8,128)(2,1)} %get-tuple-element.91), channel_id=1, source_target_pairs={{0,18},{2,16},{4,22},{6,20},{8,26},{10,24},{12,30},{14,28},{16,2},... | collective-permute-start | bytes 2359304 | tf_op jit(solution)/shard_map/ppermute | solution.py:353
  27.8 138.1 %collective-permute-start.6 = (bf16[12,2,128,128]{3,2,1,0:T(8,128)(2,1)}, bf16[12,2,128,128]{3,2,1,0:T(8,128)(2,1)}, u32[]{:S(2)}, u32[]{:S(2)}) collective-permute-start(bf16[12,2,128,128]{3,2,1,0:T(8,128)(2,1)} %get-tuple-element.88), channel_id=1, source_target_pairs={{0,10},{2,8},{4,14},{6,12},{8,2},{10,0},{12,6},{14,4},{16,26},{18,... | collective-permute-start | bytes 2359304 | tf_op jit(solution)/shard_map/ppermute | solution.py:353
  35.8 3.7 %copy-start.32 = (s32[16]{0:T(128)S(1)}, s32[16]{0:T(128)}, u32[]{:S(2)}) copy-start(s32[16]{0:T(128)} %broadcast_xor_fusion.order_ref) | copy-start | bytes 196
  37.0 16.3 %copy-start.37 = (bf16[12,2,128,128]{3,2,1,0:T(8,128)(2,1)S(1)}, bf16[12,2,128,128]{3,2,1,0:T(8,128)(2,1)}, u32[]{:S(2)}) copy-start(bf16[12,2,128,128]{3,2,1,0:T(8,128)(2,1)} %get-tuple-element.83) | copy-start | bytes 2359300
  38.6 25.2 %copy-start.33 = (s32[12,8,12]{2,1,0:T(8,128)S(1)}, s32[12,8,12]{2,1,0:T(8,128)}, u32[]{:S(2)}) copy-start(s32[12,8,12]{2,1,0:T(8,128)} %param.11) | copy-start | bytes 13828
  38.6 20.1 %collective-permute-start.10 = (bf16[512,1536]{1,0:T(8,128)(2,1)S(1)}, bf16[512,1536]{1,0:T(8,128)(2,1)S(1)}, u32[]{:S(2)}, u32[]{:S(2)}) collective-permute-start(bf16[512,1536]{1,0:T(8,128)(2,1)S(1)} %slice_select_fusion), channel_id=1, source_target_pairs={{0,16},{4,20},{1,17},{5,21}} | collective-permute-start | bytes 4718600 | tf_op jit(solution)/shard_map/ppermute | solution.py:251
  53.3 9.6 %copy-start.19 = (bf16[12,2,128,128]{3,2,1,0:T(8,128)(2,1)}, bf16[12,2,128,128]{3,2,1,0:T(8,128)(2,1)S(1)}, u32[]{:S(2)}) copy-start(bf16[12,2,128,128]{3,2,1,0:T(8,128)(2,1)S(1)} %collective-permute-done.refs_1_) | copy-start | bytes 2359300
  53.3 9.6 %collective-permute-start.1 = (bf16[12,2,128,128]{3,2,1,0:T(8,128)(2,1)S(1)}, bf16[12,2,128,128]{3,2,1,0:T(8,128)(2,1)S(1)}, u32[]{:S(2)}, u32[]{:S(2)}) collective-permute-start(bf16[12,2,128,128]{3,2,1,0:T(8,128)(2,1)S(1)} %copy-done.37), channel_id=1, source_target_pairs={{0,2},{2,0},{4,6},{6,4},{8,10},{10,8},{12,14},{14,12},{16,18},{18,... | collective-permute-start | bytes 2359304 | tf_op jit(solution)/shard_map/ppermute | solution.py:353
  60.1 103.0 %collective-permute-start.11 = (bf16[512,1536]{1,0:T(8,128)(2,1)}, bf16[512,1536]{1,0:T(8,128)(2,1)}, u32[]{:S(2)}, u32[]{:S(2)}) collective-permute-start(bf16[512,1536]{1,0:T(8,128)(2,1)} %broadcast_select_fusion), channel_id=1, source_target_pairs={{0,8},{4,12},{16,24},{20,28},{1,9},{5,13},{17,25},{21,29}} | collective-permute-start | bytes 4718600 | tf_op jit(solution)/shard_map/ppermute | solution.py:251
  62.9 0.9 copy-start.15
  63.8 57.5 %collective-permute-start.2 = (bf16[12,2,128,128]{3,2,1,0:T(8,128)(2,1)}, bf16[12,2,128,128]{3,2,1,0:T(8,128)(2,1)S(1)}, u32[]{:S(2)}, u32[]{:S(2)}) collective-permute-start(bf16[12,2,128,128]{3,2,1,0:T(8,128)(2,1)} %get-tuple-element.85), channel_id=1, source_target_pairs={{0,4},{2,6},{4,0},{6,2},{8,12},{10,14},{12,8},{14,10},{16,20},{18,... | collective-permute-start | bytes 2359304 | tf_op jit(solution)/shard_map/ppermute | solution.py:353
  64.5 66.8 %copy-start.21 = (bf16[12,2,128,128]{3,2,1,0:T(8,128)(2,1)}, bf16[12,2,128,128]{3,2,1,0:T(8,128)(2,1)S(1)}, u32[]{:S(2)}) copy-start(bf16[12,2,128,128]{3,2,1,0:T(8,128)(2,1)S(1)} %collective-permute-done.3.refs_2_) | copy-start | bytes 2359300
  90.6 40.8 %copy-start.23 = (bf16[12,2,128,128]{3,2,1,0:T(8,128)(2,1)}, bf16[12,2,128,128]{3,2,1,0:T(8,128)(2,1)S(1)}, u32[]{:S(2)}) copy-start(bf16[12,2,128,128]{3,2,1,0:T(8,128)(2,1)S(1)} %collective-permute-done.4.refs_3_) | copy-start | bytes 2359300
  90.6 75.3 %collective-permute-start.7 = (bf16[12,2,128,128]{3,2,1,0:T(8,128)(2,1)}, bf16[12,2,128,128]{3,2,1,0:T(8,128)(2,1)}, u32[]{:S(2)}, u32[]{:S(2)}) collective-permute-start(bf16[12,2,128,128]{3,2,1,0:T(8,128)(2,1)} %get-tuple-element.93), channel_id=1, source_target_pairs={{0,20},{2,22},{4,16},{6,18},{8,28},{10,30},{12,24},{14,26},{16,4},... | collective-permute-start | bytes 2359304 | tf_op jit(solution)/shard_map/ppermute | solution.py:353
  121.1 56.8 %collective-permute-start.8 = (bf16[12,2,128,128]{3,2,1,0:T(8,128)(2,1)}, bf16[12,2,128,128]{3,2,1,0:T(8,128)(2,1)}, u32[]{:S(2)}, u32[]{:S(2)}) collective-permute-start(bf16[12,2,128,128]{3,2,1,0:T(8,128)(2,1)} %get-tuple-element.95), channel_id=1, source_target_pairs={{0,22},{2,20},{4,18},{6,16},{8,30},{10,28},{12,26},{14,24},{16,6},... | collective-permute-start | bytes 2359304 | tf_op jit(solution)/shard_map/ppermute | solution.py:353
  121.3 10.1 %copy-start.17 = (bf16[12,2,128,128]{3,2,1,0:T(8,128)(2,1)}, bf16[12,2,128,128]{3,2,1,0:T(8,128)(2,1)S(1)}, u32[]{:S(2)}) copy-start(bf16[12,2,128,128]{3,2,1,0:T(8,128)(2,1)S(1)} %collective-permute-done.2.refs_2_) | copy-start | bytes 2359300
  121.3 56.6 %collective-permute-start.5 = (bf16[12,2,128,128]{3,2,1,0:T(8,128)(2,1)}, bf16[12,2,128,128]{3,2,1,0:T(8,128)(2,1)}, u32[]{:S(2)}, u32[]{:S(2)}) collective-permute-start(bf16[12,2,128,128]{3,2,1,0:T(8,128)(2,1)} %get-tuple-element.87), channel_id=1, source_target_pairs={{0,6},{2,4},{4,2},{6,0},{8,14},{10,12},{12,10},{14,8},{16,22},{18,... | collective-permute-start | bytes 2359304 | tf_op jit(solution)/shard_map/ppermute | solution.py:353
  133.3 1.1 copy-start
  134.4 1.9 copy-start.14
  136.3 1.1 copy-start.20
  137.4 1.1 copy-start.22
  138.6 1.1 copy-start.24
  139.7 1.1 copy-start.25
  160.4 2.7 copy-start.10
  177.9 92.7 %collective-permute-start.13 = (bf16[24,2,128,128]{3,2,1,0:T(8,128)(2,1)}, bf16[24,2,128,128]{3,2,1,0:T(8,128)(2,1)}, u32[]{:S(2)}, u32[]{:S(2)}) collective-permute-start(bf16[24,2,128,128]{3,2,1,0:T(8,128)(2,1)} %get-tuple-element.112), channel_id=1, source_target_pairs={{0,12},{2,14},{4,8},{6,10},{8,4},{10,6},{12,0},{14,2},{16,28},{18,... | collective-permute-start | bytes 4718600 | tf_op jit(solution)/shard_map/ppermute | solution.py:353
  182.6 41.9 %collective-permute-start.14 = (bf16[12,2,128,128]{3,2,1,0:T(8,128)(2,1)}, bf16[12,2,128,128]{3,2,1,0:T(8,128)(2,1)S(1)}, u32[]{:S(2)}, u32[]{:S(2)}) collective-permute-start(bf16[12,2,128,128]{3,2,1,0:T(8,128)(2,1)} %get-tuple-element.114), channel_id=1, source_target_pairs={{0,24},{2,26},{4,28},{6,30},{8,16},{10,18},{12,20},{14,22},{16,8},... | collective-permute-start | bytes 2359304 | tf_op jit(solution)/shard_map/ppermute | solution.py:353
  188.6 92.1 %collective-permute-start.17 = (bf16[12,2,128,128]{3,2,1,0:T(8,128)(2,1)}, bf16[12,2,128,128]{3,2,1,0:T(8,128)(2,1)}, u32[]{:S(2)}, u32[]{:S(2)}) collective-permute-start(bf16[12,2,128,128]{3,2,1,0:T(8,128)(2,1)} %get-tuple-element.139), channel_id=1, source_target_pairs={{0,26},{2,24},{4,30},{6,28},{8,18},{10,16},{12,22},{14,20},{16,10}... | collective-permute-start | bytes 2359304 | tf_op jit(solution)/shard_map/ppermute | solution.py:353
  188.7 117.2 %collective-permute-start.16 = (bf16[12,2,128,128]{3,2,1,0:T(8,128)(2,1)}, bf16[12,2,128,128]{3,2,1,0:T(8,128)(2,1)}, u32[]{:S(2)}, u32[]{:S(2)}) collective-permute-start(bf16[12,2,128,128]{3,2,1,0:T(8,128)(2,1)} %get-tuple-element.138), channel_id=1, source_target_pairs={{0,28},{2,30},{4,24},{6,26},{8,20},{10,22},{12,16},{14,18},{16,12}... | collective-permute-start | bytes 2359304 | tf_op jit(solution)/shard_map/ppermute | solution.py:353
  190.8 1.2 copy-start.1
  192.0 3.5 copy-start.11
  195.5 1.2 copy-start.16
  196.7 1.2 copy-start.18
  197.9 26.6 %copy-start.2 = (f32[12,16,1024]{2,1,0:T(8,128)S(1)}, f32[12,16,1024]{2,1,0:T(8,128)}, u32[]{:S(2)}) copy-start(f32[12,16,1024]{2,1,0:T(8,128)} %reshape.302.bias_ref) | copy-start | bytes 2359300
  231.2 2.7 copy-start.12
  252.7 2.8 copy-start.7
  255.5 2.8 copy-start.13
  270.6 2.0 copy-start.36
  270.6 10.1 %copy-start.3 = (f32[12,16,1024]{2,1,0:T(8,128)S(1)}, f32[12,16,1024]{2,1,0:T(8,128)}, u32[]{:S(2)}) copy-start(f32[12,16,1024]{2,1,0:T(8,128)} %reshape.302.bias_ref) | copy-start | bytes 2359300
  272.3 33.5 %collective-permute-start.15 = (bf16[12,2,128,128]{3,2,1,0:T(8,128)(2,1)S(1)}, bf16[12,2,128,128]{3,2,1,0:T(8,128)(2,1)S(1)}, u32[]{:S(2)}, u32[]{:S(2)}) collective-permute-start(bf16[12,2,128,128]{3,2,1,0:T(8,128)(2,1)S(1)} %get-tuple-element.185), channel_id=1, source_target_pairs={{0,2},{2,0},{4,6},{6,4},{8,10},{10,8},{12,14},{14,12},{16,18},{18,... | collective-permute-start | bytes 2359304 | tf_op jit(solution)/shard_map/ppermute | solution.py:353
  272.6 49.8 %collective-permute-start.12 = (bf16[12,2,128,128]{3,2,1,0:T(8,128)(2,1)S(1)}, bf16[12,2,128,128]{3,2,1,0:T(8,128)(2,1)S(1)}, u32[]{:S(2)}, u32[]{:S(2)}) collective-permute-start(bf16[12,2,128,128]{3,2,1,0:T(8,128)(2,1)S(1)} %copy-done.36), channel_id=1, source_target_pairs={{0,30},{2,28},{4,26},{6,24},{8,22},{10,20},{12,18},{14,16},{16,14}... | collective-permute-start | bytes 2359304 | tf_op jit(solution)/shard_map/ppermute | solution.py:353
  317.1 11.9 %copy-start.5 = (f32[12,128,1024]{2,1,0:T(8,128)}, f32[12,128,1024]{2,1,0:T(8,128)S(1)}, u32[]{:S(2)}) copy-start(f32[12,128,1024]{2,1,0:T(8,128)S(1)} %get-tuple-element.146.refs_1_) | copy-start | bytes 18874372
  322.4 6.5 %copy-start.8 = (bf16[12,2,128,128]{3,2,1,0:T(8,128)(2,1)}, bf16[12,2,128,128]{3,2,1,0:T(8,128)(2,1)S(1)}, u32[]{:S(2)}) copy-start(bf16[12,2,128,128]{3,2,1,0:T(8,128)(2,1)S(1)} %collective-permute-done.12.refs_0_) | copy-start | bytes 2359300
  327.6 5.0 %copy-start.26 = (bf16[512,512]{1,0:T(8,128)(2,1)}, bf16[512,512]{1,0:T(8,128)(2,1)S(1)}, u32[]{:S(2)}) copy-start(bf16[512,512]{1,0:T(8,128)(2,1)S(1)} %get-tuple-element.149) | copy-start | bytes 1572868
  327.7 17.1 %collective-permute-start.18 = (bf16[512,512]{1,0:T(8,128)(2,1)}, bf16[512,512]{1,0:T(8,128)(2,1)}, u32[]{:S(2)}, u32[]{:S(2)}) collective-permute-start(bf16[512,512]{1,0:T(8,128)(2,1)} %get-tuple-element.152), channel_id=1, source_target_pairs={{0,1},{1,0},{2,3},{3,2},{4,5},{5,4},{6,7},{7,6},{8,9},{9,8},{10,11... | collective-permute-start | bytes 1572872 | tf_op jit(solution)/shard_map/ppermute | solution.py:405
  332.6 0.9 copy-start.28
  333.5 19.5 %collective-permute-start.19 = (bf16[512,512]{1,0:T(8,128)(2,1)}, bf16[512,512]{1,0:T(8,128)(2,1)}, u32[]{:S(2)}, u32[]{:S(2)}) collective-permute-start(bf16[512,512]{1,0:T(8,128)(2,1)} %get-tuple-element.153), channel_id=1, source_target_pairs={{0,1},{1,0},{2,3},{3,2},{4,5},{5,4},{6,7},{7,6},{8,9},{9,8},{10,11... | collective-permute-start | bytes 1572872 | tf_op jit(solution)/shard_map/ppermute | solution.py:405
  334.8 1.1 copy-start.4
  336.0 2.8 copy-start.6
  338.7 1.1 copy-start.9
  343.4 1.0 copy-start.27
  343.4 1.2 copy-start.29
  343.4 20.2 %collective-permute-start.20 = (bf16[512,512]{1,0:T(8,128)(2,1)S(1)}, bf16[512,512]{1,0:T(8,128)(2,1)S(1)}, u32[]{:S(2)}, u32[]{:S(2)}) collective-permute-start(bf16[512,512]{1,0:T(8,128)(2,1)S(1)} %get-tuple-element.154), channel_id=1, source_target_pairs={{0,1},{1,0},{2,3},{3,2},{4,5},{5,4},{6,7},{7,6},{8,9},{9,8},{10,11... | collective-permute-start | bytes 1572872 | tf_op jit(solution)/shard_map/ppermute | solution.py:405
  354.1 9.5 %copy-start.30 = (bf16[512,3072]{1,0:T(8,128)(2,1)}, bf16[512,3072]{1,0:T(8,128)(2,1)S(1)}, u32[]{:S(2)}) copy-start(bf16[512,3072]{1,0:T(8,128)(2,1)S(1)} %constant_dynamic-update-slice_fusion.1) | copy-start | bytes 9437188
Sparse Core Ops, SparseCore 0:
  178.1 74.6 all-gather.1

commit v5 on v4

--- a/solution.py
+++ b/solution.py
@@ -395,11 +395,12 @@
         (out,) = last(split=1)
         return lax.all_to_all(out, "head", split_axis=0, concat_axis=1, tiled=True)
 
-    third = head_count // 3
+    fourth = head_count // 4
     result = jnp.zeros((rows // 2, 2 * width), jnp.bfloat16)
     kept = []
     arrived = []
-    for lo, hi in ((0, third), (third, 2 * third), (2 * third, head_count)):
+    for lo in range(0, head_count, fourth):
+        hi = lo + fourth
         keep, away = last(split=2, heads=(lo, hi))
         kept.append((lo, keep))
         arrived.append((lo, lax.ppermute(away, "head", [(0, 1), (1, 0)])))

time: 373 us -> 372 us (level)
  waiting for transfers between devices: 99.7 us -> 94 us
  Pallas kernels: 125 us -> 129 us
    ppermute x15, waiting for transfers between devices: 64.2 us -> 55.8 us  [move(): lax.ppermute(parts[d], 'seq', [(j, j ^ d) for j in range(seq_count)])]
    pallas_call x8 -> x9, Pallas kernels: 87.9 us -> 91.1 us  [pool_part(): pl.pallas_call(functools.partial(pool_kernel, scale, min(256, rows), len(...]
    ppermute x3 -> x4, waiting for transfers between devices: 16.6 us -> 19.6 us  [body(): arrived.append((lo, lax.ppermute(away, 'head', [(0, 1), (1, 0)])))]
    unnamed x79 -> x65, local copies, waits for them, and re-layouts: 33.2 us -> 34.4 us
  transfers between devices with their start and end apart: 22 -> 23, of which waited for: 8 -> 9; matrix products, arithmetic and copies ran while one was open for 7% -> 7% of each run, Pallas kernels for 32% -> 34%
where the time goes in v5:
time: 372 us; the launch traced here: 371 us
  Pallas kernels  129 us (35%)
  waiting for transfers between devices  94 us (25%)
  starting transfers between devices  70 us (19%)
  local copies, waits for them, and re-layouts  45.4 us (12%)
  other arithmetic  18.8 us (5%)
  between operations  13.9 us (4%)
    pallas_call x9, Pallas kernels, pool_part(): pl.pallas_call(functools.partial(pool_kernel, scale, min(256, rows), len(...  91.1 us
    ppermute x15, starting transfers between devices, move(): lax.ppermute(parts[d], 'seq', [(j, j ^ d) for j in range(seq_count)])  61.8 us
    ppermute x15, waiting for transfers between devices, move(): lax.ppermute(parts[d], 'seq', [(j, j ^ d) for j in range(seq_count)])  55.8 us
    unnamed x65, local copies, waits for them, and re-layouts  34.4 us
    pallas_call x3, Pallas kernels, pack(): pl.pallas_call(functools.partial(pack_kernel, lo, bound, head_size), grid...  24.9 us
    ppermute x4, waiting for transfers between devices, body(): arrived.append((lo, lax.ppermute(away, 'head', [(0, 1), (1, 0)])))  19.6 us
    all_gather x1, waiting for transfers between devices, share_within(): lax.all_gather(piece, axis, axis=0, tiled=True, axis_index_groups=groups)  18.5 us
    pallas_call x1, Pallas kernels, shared_part(): pl.pallas_call(functools.partial(shared_kernel, scale, min(256, rows)), g...  12.7 us
  transfers between devices with their start and end apart: 23, of which 9 were waited for; matrix products, arithmetic and copies ran while one was open for 7% of the time, Pallas kernels for 34%

profile of v5, /device:TPU:9, one launch (start us, length us, event | category | flops | bytes accessed | tf_op | source)
XLA Modules:
  0.0 370.9 jit_solution(6586167319944951774)
XLA Ops:
  6.5 2.7 slice.56
  9.2 1.8 collective-permute-start.9
  11.0 1.0 select_reduce_fusion
  14.2 7.4 %pack_tiles.5 = (bf16[12,2,128,128]{3,2,1,0:T(8,128)(2,1)}, bf16[12,2,128,128]{3,2,1,0:T(8,128)(2,1)}, bf16[12,2,128,128]{3,2,1,0:T(8,128)(2,1)}, bf16[12,2,128,128]{3,2,1,0:T(8,128)(2,1)}) custom-call(s32[192]{0:T(256)} %reshape.302.codes_ref, s32[16]{0:T(128)} %broadcast_xor_fusion.order_ref, bf16[1024,1536]{1,0:T(8,128)(2,1)} %keys_ref.5, ...), custom_call_target="tpu_custom_call" | custom-call | tf_op jit(solution)/shard_map/pack_tiles/pallas_call | solution.py:40
  21.5 2.5 collective-permute-start.3
  24.0 3.9 %collective-permute-start.4 = (bf16[12,2,128,128]{3,2,1,0:T(8,128)(2,1)}, bf16[12,2,128,128]{3,2,1,0:T(8,128)(2,1)S(1)}, u32[]{:S(2)}, u32[]{:S(2)}) collective-permute-start(bf16[12,2,128,128]{3,2,1,0:T(8,128)(2,1)} %get-tuple-element.93), channel_id=1, source_target_pairs={{0,18},{2,16},{4,22},{6,20},{8,26},{10,24},{12,30},{14,28},{16,2},... | collective-permute-start | bytes 2359304 | tf_op jit(solution)/shard_map/ppermute | solution.py:353
  28.0 8.0 %pack_tiles.4 = (bf16[12,2,128,128]{3,2,1,0:T(8,128)(2,1)}, bf16[12,2,128,128]{3,2,1,0:T(8,128)(2,1)}, bf16[12,2,128,128]{3,2,1,0:T(8,128)(2,1)}, bf16[12,2,128,...) custom-call(s32[192]{0:T(256)} %reshape.302.codes_ref, s32[16]{0:T(128)} %broadcast_xor_fusion.order_ref, ...), custom_call_target="tpu_custom_call" | custom-call | tf_op jit(solution)/shard_map/pack_tiles/pallas_call | solution.py:40
  37.2 1.7 slice_select_fusion
  38.9 0.9 collective-permute-start.10
  41.1 1.3 pad_add_fusion
  42.4 2.6 pad_add_fusion.1
  46.2 7.2 %collective-permute-done.refs_1_ = bf16[12,2,128,128]{3,2,1,0:T(8,128)(2,1)S(1)} collective-permute-done((bf16[12,2,128,128]{3,2,1,0:T(8,128)(2,1)}, bf16[12,2,128,128]{3,2,1,0:T(8,128)(2,1)S(1)}, u32[]{:S(2)}, u32[]{:S(2)}) %collective-permute-start) | collective-permute-done | bytes 786464 | tf_op jit(solution)/shard_map/ppermute | solution.py:353
  53.4 5.4 %collective-permute-start.1 = (bf16[12,2,128,128]{3,2,1,0:T(8,128)(2,1)S(1)}, bf16[12,2,128,128]{3,2,1,0:T(8,128)(2,1)S(1)}, u32[]{:S(2)}, u32[]{:S(2)}) collective-permute-start(bf16[12,2,128,128]{3,2,1,0:T(8,128)(2,1)S(1)} %copy-done.30), channel_id=1, source_target_pairs={{0,2},{2,0},{4,6},{6,4},{8,10},{10,8},{12,14},{14,12},{16,18},{18,... | collective-permute-start | bytes 2359304 | tf_op jit(solution)/shard_map/ppermute | solution.py:353
  58.8 1.4 broadcast_select_fusion
  60.2 1.8 collective-permute-start.11
  63.0 0.9 copy-done.13
  64.7 26.0 %collective-permute-done.4.refs_3_ = bf16[12,2,128,128]{3,2,1,0:T(8,128)(2,1)S(1)} collective-permute-done((bf16[12,2,128,128]{3,2,1,0:T(8,128)(2,1)}, bf16[12,2,128,128]{3,2,1,0:T(8,128)(2,1)S(1)}, u32[]{:S(2)}, u32[]{:S(2)}) %collective-permute-start.4) | collective-permute-done | bytes 786464 | tf_op jit(solution)/shard_map/ppermute | solution.py:353
  90.7 30.5 %collective-permute-start.7 = (bf16[12,2,128,128]{3,2,1,0:T(8,128)(2,1)}, bf16[12,2,128,128]{3,2,1,0:T(8,128)(2,1)}, u32[]{:S(2)}, u32[]{:S(2)}) collective-permute-start(bf16[12,2,128,128]{3,2,1,0:T(8,128)(2,1)} %get-tuple-element.95), channel_id=1, source_target_pairs={{0,20},{2,22},{4,16},{6,18},{8,28},{10,30},{12,24},{14,26},{16,4},... | collective-permute-start | bytes 2359304 | tf_op jit(solution)/shard_map/ppermute | solution.py:353
  121.9 9.6 %pack_tiles.3 = (bf16[24,2,128,128]{3,2,1,0:T(8,128)(2,1)}, bf16[12,2,128,128]{3,2,1,0:T(8,128)(2,1)}, bf16[12,2,128,128]{3,2,1,0:T(8,128)(2,1)}, bf16[12,2,128,...) custom-call(s32[192]{0:T(256)} %reshape.302.codes_ref, ...), custom_call_target="tpu_custom_call" | custom-call | tf_op jit(solution)/shard_map/pack_tiles/pallas_call | solution.py:40
  131.9 1.0 reshape.303.bias_ref
  133.4 1.1 copy-done
  134.5 1.9 copy-done.12
  136.4 1.1 copy-done.18
  137.5 1.1 copy-done.20
  138.6 1.1 copy-done.22
  139.8 1.1 copy-done.23
  140.9 19.5 %pool_tiles.9 = (bf16[12,128,1024]{2,1,0:T(8,128)(2,1)S(1)}, f32[12,128,1024]{2,1,0:T(8,128)S(1)}, f32[12,1,1024]{2,1,0:T(1,128)S(1)}, f32[12,1,1024]{2,1,0:T(1,128)S(1)}) custom-call(s32[12,16]{1,0:T(8,128)S(1)} %get-tuple-element.174.place_ref, s32[12,16]{1,0:T(8,128)S(1)} %get-tuple-element.173.entry_ref, s32[12]{0:T(128)S(1)} %get-tuple-element.200.count_ref, ...), custom_call_target="tpu_custom_call" | custom-call | tf_op jit(solution)/shard_map/pool_tiles/pallas_call | solution.py:222
  160.4 2.6 copy-done.7
  163.1 2.8 broadcast_select_fusion.1
  165.8 12.2 %collective-permute-done.8.refs_5_ = bf16[12,2,128,128]{3,2,1,0:T(8,128)(2,1)} collective-permute-done((bf16[12,2,128,128]{3,2,1,0:T(8,128)(2,1)}, bf16[12,2,128,128]{3,2,1,0:T(8,128)(2,1)}, u32[]{:S(2)}, u32[]{:S(2)}) %collective-permute-start.8) | collective-permute-done | bytes 786464 | tf_op jit(solution)/shard_map/ppermute | solution.py:353
  178.0 4.7 %collective-permute-start.13 = (bf16[24,2,128,128]{3,2,1,0:T(8,128)(2,1)}, bf16[24,2,128,128]{3,2,1,0:T(8,128)(2,1)}, u32[]{:S(2)}, u32[]{:S(2)}) collective-permute-start(bf16[24,2,128,128]{3,2,1,0:T(8,128)(2,1)} %get-tuple-element.114), channel_id=1, source_target_pairs={{0,12},{2,14},{4,8},{6,10},{8,4},{10,6},{12,0},{14,2},{16,28},{18,... | collective-permute-start | bytes 4718600 | tf_op jit(solution)/shard_map/ppermute | solution.py:353
  182.7 4.7 %collective-permute-start.14 = (bf16[12,2,128,128]{3,2,1,0:T(8,128)(2,1)}, bf16[12,2,128,128]{3,2,1,0:T(8,128)(2,1)S(1)}, u32[]{:S(2)}, u32[]{:S(2)}) collective-permute-start(bf16[12,2,128,128]{3,2,1,0:T(8,128)(2,1)} %get-tuple-element.116), channel_id=1, source_target_pairs={{0,24},{2,26},{4,28},{6,30},{8,16},{10,18},{12,20},{14,22},{16,8},... | collective-permute-start | bytes 2359304 | tf_op jit(solution)/shard_map/ppermute | solution.py:353
  188.0 0.9 select_reduce_fusion.6
  189.0 1.5 collective-permute-start.16
  190.5 1.2 copy-done.1
  191.7 3.6 copy-done.8
  195.3 1.2 copy-done.14
  196.5 1.2 copy-done.16
  197.7 27.2 %pool_tiles.10 = (f32[12,128,1024]{2,1,0:T(8,128)S(1)}, f32[12,1,1024]{2,1,0:T(1,128)S(1)}, f32[12,1,1024]{2,1,0:T(1,128)S(1)}) custom-call(s32[12,16]{1,0:T(8,128)S(1)} %get-tuple-element.166.place_ref, s32[12,16]{1,0:T(8,128)S(1)} %get-tuple-element.165.entry_ref, s32[12]{0:T(128)S(1)} %get-tuple-element.196.count_ref, s32[1]{0:T(128)} %bitcast.4.side_ref, ...), custom_call_target="tpu_custom_call" | custom-call | tf_op jit(solution)/shard_map/pool_tiles/pallas_call | solution.py:222
  224.9 6.1 %pool_tiles.11 = (f32[12,128,1024]{2,1,0:T(8,128)S(1)}, f32[12,1,1024]{2,1,0:T(1,128)S(1)}, f32[12,1,1024]{2,1,0:T(1,128)S(1)}) custom-call(s32[12,16]{1,0:T(8,128)S(1)} %get-tuple-element.168.place_ref, s32[12,16]{1,0:T(8,128)S(1)} %get-tuple-element.167.entry_ref, s32[12]{0:T(128)S(1)} %get-tuple-element.181.count_ref, s32[1]{0:T(128)} %bitcast.4.side_ref, ...), custom_call_target="tpu_custom_call" | custom-call | tf_op jit(solution)/shard_map/pool_tiles/pallas_call | solution.py:222
  231.0 2.6 copy-done.9
  233.6 18.5 %all-gather.2.cloned.1.call-done.k_ref.v_ref = bf16[2048,1536]{1,0:T(8,128)(2,1)} async-done(((bf16[512,1536]{1,0:T(8,128)(2,1)}), bf16[2048,1536]{1,0:T(8,128)(2,1)}) %all-gather.2.cloned.1.call-update) | async-done | bytes 6291472 | tf_op jit(solution)/shard_map/all_gather | solution.py:257
  252.1 2.8 copy-done.4
  254.9 2.8 copy-done.10
  257.7 12.7 %shared_tiles.1 = (f32[12,128,1024]{2,1,0:T(8,128)S(1)}, f32[12,1,1024]{2,1,0:T(1,128)S(1)}, f32[12,1,1024]{2,1,0:T(1,128)S(1)}) custom-call(bf16[12,128,1024]{2,1,0:T(8,128)(2,1)S(1)} %get-tuple-element.112.q_ref.qt_ref, bf16[2048,1536]{1,0:T(8,128)(2,1)S(1)} %copy-done.4, bf16[2048,1536]{1,0:T(8,128)(2,1)S(1)} %copy-done.4, ...), custom_call_target="tpu_custom_call" | custom-call | tf_op jit(solution)/shard_map/shared_tiles/pallas_call | solution.py:92
  270.4 2.7 copy-done.5
  273.0 2.7 fusion.28
  276.0 7.8 %collective-permute-start.12 = (bf16[12,2,128,128]{3,2,1,0:T(8,128)(2,1)}, bf16[12,2,128,128]{3,2,1,0:T(8,128)(2,1)}, u32[]{:S(2)}, u32[]{:S(2)}) collective-permute-start(bf16[12,2,128,128]{3,2,1,0:T(8,128)(2,1)} %get-tuple-element.113), channel_id=1, source_target_pairs={{0,30},{2,28},{4,26},{6,24},{8,22},{10,20},{12,18},{14,16},{16,14}... | collective-permute-start | bytes 2359304 | tf_op jit(solution)/shard_map/ppermute | solution.py:353
  285.0 1.1 copy-done.3
  286.1 2.8 copy-done.6
  288.9 1.1 copy-done.11
  290.0 11.2 %pool_tiles.12 = (f32[12,128,1024]{2,1,0:T(8,128)S(1)}, f32[12,1,1024]{2,1,0:T(1,128)S(1)}, f32[12,1,1024]{2,1,0:T(1,128)S(1)}) custom-call(s32[12,16]{1,0:T(8,128)S(1)} %get-tuple-element.162.place_ref, s32[12,16]{1,0:T(8,128)S(1)} %get-tuple-element.161.entry_ref, s32[12]{0:T(128)S(1)} %get-tuple-element.194.count_ref, s32[1]{0:T(128)} %bitcast.4.side_ref, ...), custom_call_target="tpu_custom_call" | custom-call | tf_op jit(solution)/shard_map/pool_tiles/pallas_call | solution.py:222
  301.3 5.0 %collective-permute-done.16.refs_1_ = bf16[12,2,128,128]{3,2,1,0:T(8,128)(2,1)} collective-permute-done((bf16[12,2,128,128]{3,2,1,0:T(8,128)(2,1)}, bf16[12,2,128,128]{3,2,1,0:T(8,128)(2,1)}, u32[]{:S(2)}, u32[]{:S(2)}) %collective-permute-start.16) | collective-permute-done | bytes 786464 | tf_op jit(solution)/shard_map/ppermute | solution.py:353
  306.3 11.1 %pool_tiles.13 = (f32[12,128,1024]{2,1,0:T(8,128)S(1)}, f32[12,1,1024]{2,1,0:T(1,128)S(1)}, f32[12,1,1024]{2,1,0:T(1,128)S(1)}) custom-call(s32[12,16]{1,0:T(8,128)S(1)} %get-tuple-element.172.place_ref, s32[12,16]{1,0:T(8,128)S(1)} %get-tuple-element.171.entry_ref, s32[12]{0:T(128)S(1)} %get-tuple-element.198.count_ref, s32[1]{0:T(128)} %bitcast.4.side_ref, ...), custom_call_target="tpu_custom_call" | custom-call | tf_op jit(solution)/shard_map/pool_tiles/pallas_call | solution.py:222
  317.4 5.5 %collective-permute-done.12.refs_0_ = bf16[12,2,128,128]{3,2,1,0:T(8,128)(2,1)} collective-permute-done((bf16[12,2,128,128]{3,2,1,0:T(8,128)(2,1)}, bf16[12,2,128,128]{3,2,1,0:T(8,128)(2,1)}, u32[]{:S(2)}, u32[]{:S(2)}) %collective-permute-start.12) | collective-permute-done | bytes 786464 | tf_op jit(solution)/shard_map/ppermute | solution.py:353
  322.9 4.4 %pool_tiles.14 = (bf16[512,384]{1,0:T(8,128)(2,1)S(1)}, bf16[512,384]{1,0:T(8,128)(2,1)S(1)}) custom-call(s32[12,16]{1,0:T(8,128)S(1)} %get-tuple-element.169.place_ref, s32[12,16]{1,0:T(8,128)S(1)} %get-tuple-element.170.entry_ref, s32[12]{0:T(128)S(1)} %get-tuple-element.184.count_ref, s32[1]{0:T(128)} %bitcast.4.side_ref, ...), custom_call_target="tpu_custom_call" | custom-call | tf_op jit(solution)/shard_map/pool_tiles/pallas_call | solution.py:222
  327.8 4.3 %pool_tiles.15 = (bf16[512,384]{1,0:T(8,128)(2,1)S(1)}, bf16[512,384]{1,0:T(8,128)(2,1)S(1)}) custom-call(s32[12,16]{1,0:T(8,128)S(1)} %get-tuple-element.169.place_ref, s32[12,16]{1,0:T(8,128)S(1)} %get-tuple-element.170.entry_ref, s32[12]{0:T(128)S(1)} %get-tuple-element.184.count_ref, s32[1]{0:T(128)} %bitcast.4.side_ref, ...), custom_call_target="tpu_custom_call" | custom-call | tf_op jit(solution)/shard_map/pool_tiles/pallas_call | solution.py:222
  332.1 1.1 collective-permute-start.19
  333.2 3.6 pool_tiles.16
  337.7 3.6 pool_tiles.17
  341.3 1.2 collective-permute-start.21
  343.5 3.0 collective-permute-done.19
  346.5 8.3 %collective-permute-done.20 = bf16[512,384]{1,0:T(8,128)(2,1)S(1)} collective-permute-done((bf16[512,384]{1,0:T(8,128)(2,1)S(1)}, bf16[512,384]{1,0:T(8,128)(2,1)S(1)}, u32[]{:S(2)}, u32[]{:S(2)}) %collective-permute-start.20) | collective-permute-done | bytes 393248 | tf_op jit(solution)/shard_map/ppermute | solution.py:406
  355.0 8.3 %collective-permute-done.21 = bf16[512,384]{1,0:T(8,128)(2,1)S(1)} collective-permute-done((bf16[512,384]{1,0:T(8,128)(2,1)S(1)}, bf16[512,384]{1,0:T(8,128)(2,1)S(1)}, u32[]{:S(2)}, u32[]{:S(2)}) %collective-permute-start.21) | collective-permute-done | bytes 393248 | tf_op jit(solution)/shard_map/ppermute | solution.py:406
  (127 shorter events, 14.5 us)
Async XLA Ops:
  6.5 7.0 %copy-start.31 = (s32[16]{0:T(128)S(1)}, s32[16]{0:T(128)}, u32[]{:S(2)}) copy-start(s32[16]{0:T(128)} %constant.143.clone) | copy-start | bytes 196
  6.5 4.5 %copy-start.28 = (s32[12,256]{1,0:T(8,128)S(1)}, s32[12,256]{1,0:T(8,128)}, u32[]{:S(2)}) copy-start(s32[12,256]{1,0:T(8,128)} %param.10) | copy-start | bytes 36868
  6.5 4.5 %copy-start.29 = (s32[128]{0:T(128)S(1)}, s32[128]{0:T(128)}, u32[]{:S(2)}) copy-start(s32[128]{0:T(128)} %param.12) | copy-start | bytes 1540
  6.5 245.6 %all-gather.2.cloned.1.call-start = ((), (), s32[]{:S(2)}) async-start(), calls=%async_computation | async-start | bytes 7864320 | tf_op jit(solution)/shard_map/all_gather | solution.py:257
  9.2 28.0 %collective-permute-start.9 = (bf16[512,1536]{1,0:T(8,128)(2,1)}, bf16[512,1536]{1,0:T(8,128)(2,1)}, u32[]{:S(2)}, u32[]{:S(2)}) collective-permute-start(bf16[512,1536]{1,0:T(8,128)(2,1)} %slice.56), channel_id=1, source_target_pairs={{0,4},{1,5}} | collective-permute-start | bytes 4718600 | tf_op jit(solution)/shard_map/ppermute | solution.py:241
  14.2 13.8 %copy-start.25 = (s32[16]{0:T(128)S(1)}, s32[16]{0:T(128)}, u32[]{:S(2)}) copy-start(s32[16]{0:T(128)} %broadcast_xor_fusion.order_ref) | copy-start | bytes 196
  21.5 31.9 %collective-permute-start = (bf16[12,2,128,128]{3,2,1,0:T(8,128)(2,1)}, bf16[12,2,128,128]{3,2,1,0:T(8,128)(2,1)S(1)}, u32[]{:S(2)}, u32[]{:S(2)}) collective-permute-start(bf16[12,2,128,128]{3,2,1,0:T(8,128)(2,1)} %get-tuple-element.84), channel_id=1, source_target_pairs={{0,8},{2,10},{4,12},{6,14},{8,0},{10,2},{12,4},{14,6},{16,24},{18,... | collective-permute-start | bytes 2359304 | tf_op jit(solution)/shard_map/ppermute | solution.py:353
  21.5 43.2 %collective-permute-start.3 = (bf16[12,2,128,128]{3,2,1,0:T(8,128)(2,1)}, bf16[12,2,128,128]{3,2,1,0:T(8,128)(2,1)S(1)}, u32[]{:S(2)}, u32[]{:S(2)}) collective-permute-start(bf16[12,2,128,128]{3,2,1,0:T(8,128)(2,1)} %get-tuple-element.92), channel_id=1, source_target_pairs={{0,16},{2,18},{4,20},{6,22},{8,24},{10,26},{12,28},{14,30},{16,0},... | collective-permute-start | bytes 2359304 | tf_op jit(solution)/shard_map/ppermute | solution.py:353
  24.0 66.7 %collective-permute-start.4 = (bf16[12,2,128,128]{3,2,1,0:T(8,128)(2,1)}, bf16[12,2,128,128]{3,2,1,0:T(8,128)(2,1)S(1)}, u32[]{:S(2)}, u32[]{:S(2)}) collective-permute-start(bf16[12,2,128,128]{3,2,1,0:T(8,128)(2,1)} %get-tuple-element.93), channel_id=1, source_target_pairs={{0,18},{2,16},{4,22},{6,20},{8,26},{10,24},{12,30},{14,28},{16,2},... | collective-permute-start | bytes 2359304 | tf_op jit(solution)/shard_map/ppermute | solution.py:353
  27.9 137.9 %collective-permute-start.6 = (bf16[12,2,128,128]{3,2,1,0:T(8,128)(2,1)}, bf16[12,2,128,128]{3,2,1,0:T(8,128)(2,1)}, u32[]{:S(2)}, u32[]{:S(2)}) collective-permute-start(bf16[12,2,128,128]{3,2,1,0:T(8,128)(2,1)} %get-tuple-element.90), channel_id=1, source_target_pairs={{0,10},{2,8},{4,14},{6,12},{8,2},{10,0},{12,6},{14,4},{16,26},{18,... | collective-permute-start | bytes 2359304 | tf_op jit(solution)/shard_map/ppermute | solution.py:353
  36.0 3.9 %copy-start.26 = (s32[16]{0:T(128)S(1)}, s32[16]{0:T(128)}, u32[]{:S(2)}) copy-start(s32[16]{0:T(128)} %broadcast_xor_fusion.order_ref) | copy-start | bytes 196
  37.2 16.2 %copy-start.30 = (bf16[12,2,128,128]{3,2,1,0:T(8,128)(2,1)S(1)}, bf16[12,2,128,128]{3,2,1,0:T(8,128)(2,1)}, u32[]{:S(2)}) copy-start(bf16[12,2,128,128]{3,2,1,0:T(8,128)(2,1)} %get-tuple-element.85) | copy-start | bytes 2359300
  38.9 25.1 %copy-start.27 = (s32[12,8,12]{2,1,0:T(8,128)S(1)}, s32[12,8,12]{2,1,0:T(8,128)}, u32[]{:S(2)}) copy-start(s32[12,8,12]{2,1,0:T(8,128)} %param.11) | copy-start | bytes 13828
  38.9 20.0 %collective-permute-start.10 = (bf16[512,1536]{1,0:T(8,128)(2,1)S(1)}, bf16[512,1536]{1,0:T(8,128)(2,1)S(1)}, u32[]{:S(2)}, u32[]{:S(2)}) collective-permute-start(bf16[512,1536]{1,0:T(8,128)(2,1)S(1)} %slice_select_fusion), channel_id=1, source_target_pairs={{0,16},{4,20},{1,17},{5,21}} | collective-permute-start | bytes 4718600 | tf_op jit(solution)/shard_map/ppermute | solution.py:251
  53.4 9.6 %copy-start.17 = (bf16[12,2,128,128]{3,2,1,0:T(8,128)(2,1)}, bf16[12,2,128,128]{3,2,1,0:T(8,128)(2,1)S(1)}, u32[]{:S(2)}) copy-start(bf16[12,2,128,128]{3,2,1,0:T(8,128)(2,1)S(1)} %collective-permute-done.refs_1_) | copy-start | bytes 2359300
  53.4 9.6 %collective-permute-start.1 = (bf16[12,2,128,128]{3,2,1,0:T(8,128)(2,1)S(1)}, bf16[12,2,128,128]{3,2,1,0:T(8,128)(2,1)S(1)}, u32[]{:S(2)}, u32[]{:S(2)}) collective-permute-start(bf16[12,2,128,128]{3,2,1,0:T(8,128)(2,1)S(1)} %copy-done.30), channel_id=1, source_target_pairs={{0,2},{2,0},{4,6},{6,4},{8,10},{10,8},{12,14},{14,12},{16,18},{18,... | collective-permute-start | bytes 2359304 | tf_op jit(solution)/shard_map/ppermute | solution.py:353
  60.2 102.8 %collective-permute-start.11 = (bf16[512,1536]{1,0:T(8,128)(2,1)}, bf16[512,1536]{1,0:T(8,128)(2,1)}, u32[]{:S(2)}, u32[]{:S(2)}) collective-permute-start(bf16[512,1536]{1,0:T(8,128)(2,1)} %broadcast_select_fusion), channel_id=1, source_target_pairs={{0,8},{4,12},{16,24},{20,28},{1,9},{5,13},{17,25},{21,29}} | collective-permute-start | bytes 4718600 | tf_op jit(solution)/shard_map/ppermute | solution.py:251
  63.0 0.9 copy-start.13
  63.9 57.5 %collective-permute-start.2 = (bf16[12,2,128,128]{3,2,1,0:T(8,128)(2,1)}, bf16[12,2,128,128]{3,2,1,0:T(8,128)(2,1)S(1)}, u32[]{:S(2)}, u32[]{:S(2)}) collective-permute-start(bf16[12,2,128,128]{3,2,1,0:T(8,128)(2,1)} %get-tuple-element.87), channel_id=1, source_target_pairs={{0,4},{2,6},{4,0},{6,2},{8,12},{10,14},{12,8},{14,10},{16,20},{18,... | collective-permute-start | bytes 2359304 | tf_op jit(solution)/shard_map/ppermute | solution.py:353
  64.7 66.8 %copy-start.19 = (bf16[12,2,128,128]{3,2,1,0:T(8,128)(2,1)}, bf16[12,2,128,128]{3,2,1,0:T(8,128)(2,1)S(1)}, u32[]{:S(2)}) copy-start(bf16[12,2,128,128]{3,2,1,0:T(8,128)(2,1)S(1)} %collective-permute-done.3.refs_2_) | copy-start | bytes 2359300
  90.7 40.8 %copy-start.21 = (bf16[12,2,128,128]{3,2,1,0:T(8,128)(2,1)}, bf16[12,2,128,128]{3,2,1,0:T(8,128)(2,1)S(1)}, u32[]{:S(2)}) copy-start(bf16[12,2,128,128]{3,2,1,0:T(8,128)(2,1)S(1)} %collective-permute-done.4.refs_3_) | copy-start | bytes 2359300
  90.7 75.2 %collective-permute-start.7 = (bf16[12,2,128,128]{3,2,1,0:T(8,128)(2,1)}, bf16[12,2,128,128]{3,2,1,0:T(8,128)(2,1)}, u32[]{:S(2)}, u32[]{:S(2)}) collective-permute-start(bf16[12,2,128,128]{3,2,1,0:T(8,128)(2,1)} %get-tuple-element.95), channel_id=1, source_target_pairs={{0,20},{2,22},{4,16},{6,18},{8,28},{10,30},{12,24},{14,26},{16,4},... | collective-permute-start | bytes 2359304 | tf_op jit(solution)/shard_map/ppermute | solution.py:353
  121.2 56.8 %collective-permute-start.8 = (bf16[12,2,128,128]{3,2,1,0:T(8,128)(2,1)}, bf16[12,2,128,128]{3,2,1,0:T(8,128)(2,1)}, u32[]{:S(2)}, u32[]{:S(2)}) collective-permute-start(bf16[12,2,128,128]{3,2,1,0:T(8,128)(2,1)} %get-tuple-element.97), channel_id=1, source_target_pairs={{0,22},{2,20},{4,18},{6,16},{8,30},{10,28},{12,26},{14,24},{16,6},... | collective-permute-start | bytes 2359304 | tf_op jit(solution)/shard_map/ppermute | solution.py:353
  121.4 10.1 %copy-start.15 = (bf16[12,2,128,128]{3,2,1,0:T(8,128)(2,1)}, bf16[12,2,128,128]{3,2,1,0:T(8,128)(2,1)S(1)}, u32[]{:S(2)}) copy-start(bf16[12,2,128,128]{3,2,1,0:T(8,128)(2,1)S(1)} %collective-permute-done.2.refs_2_) | copy-start | bytes 2359300
  121.4 56.6 %collective-permute-start.5 = (bf16[12,2,128,128]{3,2,1,0:T(8,128)(2,1)}, bf16[12,2,128,128]{3,2,1,0:T(8,128)(2,1)}, u32[]{:S(2)}, u32[]{:S(2)}) collective-permute-start(bf16[12,2,128,128]{3,2,1,0:T(8,128)(2,1)} %get-tuple-element.89), channel_id=1, source_target_pairs={{0,6},{2,4},{4,2},{6,0},{8,14},{10,12},{12,10},{14,8},{16,22},{18,... | collective-permute-start | bytes 2359304 | tf_op jit(solution)/shard_map/ppermute | solution.py:353
  133.3 1.1 copy-start
  134.5 1.9 copy-start.12
  136.4 1.1 copy-start.18
  137.5 1.1 copy-start.20
  138.6 1.1 copy-start.22
  139.8 1.1 copy-start.23
  160.4 2.7 copy-start.7
  178.0 95.0 %collective-permute-start.13 = (bf16[24,2,128,128]{3,2,1,0:T(8,128)(2,1)}, bf16[24,2,128,128]{3,2,1,0:T(8,128)(2,1)}, u32[]{:S(2)}, u32[]{:S(2)}) collective-permute-start(bf16[24,2,128,128]{3,2,1,0:T(8,128)(2,1)} %get-tuple-element.114), channel_id=1, source_target_pairs={{0,12},{2,14},{4,8},{6,10},{8,4},{10,6},{12,0},{14,2},{16,28},{18,... | collective-permute-start | bytes 4718600 | tf_op jit(solution)/shard_map/ppermute | solution.py:353
  182.7 42.1 %collective-permute-start.14 = (bf16[12,2,128,128]{3,2,1,0:T(8,128)(2,1)}, bf16[12,2,128,128]{3,2,1,0:T(8,128)(2,1)S(1)}, u32[]{:S(2)}, u32[]{:S(2)}) collective-permute-start(bf16[12,2,128,128]{3,2,1,0:T(8,128)(2,1)} %get-tuple-element.116), channel_id=1, source_target_pairs={{0,24},{2,26},{4,28},{6,30},{8,16},{10,18},{12,20},{14,22},{16,8},... | collective-permute-start | bytes 2359304 | tf_op jit(solution)/shard_map/ppermute | solution.py:353
  188.9 96.0 %collective-permute-start.17 = (bf16[12,2,128,128]{3,2,1,0:T(8,128)(2,1)}, bf16[12,2,128,128]{3,2,1,0:T(8,128)(2,1)}, u32[]{:S(2)}, u32[]{:S(2)}) collective-permute-start(bf16[12,2,128,128]{3,2,1,0:T(8,128)(2,1)} %get-tuple-element.141), channel_id=1, source_target_pairs={{0,26},{2,24},{4,30},{6,28},{8,18},{10,16},{12,22},{14,20},{16,10}... | collective-permute-start | bytes 2359304 | tf_op jit(solution)/shard_map/ppermute | solution.py:353
  189.0 117.3 %collective-permute-start.16 = (bf16[12,2,128,128]{3,2,1,0:T(8,128)(2,1)}, bf16[12,2,128,128]{3,2,1,0:T(8,128)(2,1)}, u32[]{:S(2)}, u32[]{:S(2)}) collective-permute-start(bf16[12,2,128,128]{3,2,1,0:T(8,128)(2,1)} %get-tuple-element.140), channel_id=1, source_target_pairs={{0,28},{2,30},{4,24},{6,26},{8,20},{10,22},{12,16},{14,18},{16,12}... | collective-permute-start | bytes 2359304 | tf_op jit(solution)/shard_map/ppermute | solution.py:353
  190.5 1.2 copy-start.1
  191.7 3.6 copy-start.8
  195.3 1.2 copy-start.14
  196.5 1.2 copy-start.16
  197.7 27.2 %copy-start.2 = (f32[12,16,1024]{2,1,0:T(8,128)S(1)}, f32[12,16,1024]{2,1,0:T(8,128)}, u32[]{:S(2)}) copy-start(f32[12,16,1024]{2,1,0:T(8,128)} %reshape.303.bias_ref) | copy-start | bytes 2359300
  230.9 2.7 copy-start.9
  252.1 2.8 copy-start.4
  254.9 2.8 copy-start.10
  270.4 2.7 copy-start.5
  275.8 30.5 %collective-permute-start.15 = (bf16[12,2,128,128]{3,2,1,0:T(8,128)(2,1)}, bf16[12,2,128,128]{3,2,1,0:T(8,128)(2,1)}, u32[]{:S(2)}, u32[]{:S(2)}) collective-permute-start(bf16[12,2,128,128]{3,2,1,0:T(8,128)(2,1)} %get-tuple-element.189), channel_id=1, source_target_pairs={{0,2},{2,0},{4,6},{6,4},{8,10},{10,8},{12,14},{14,12},{16,18},{18,... | collective-permute-start | bytes 2359304 | tf_op jit(solution)/shard_map/ppermute | solution.py:353
  276.0 46.9 %collective-permute-start.12 = (bf16[12,2,128,128]{3,2,1,0:T(8,128)(2,1)}, bf16[12,2,128,128]{3,2,1,0:T(8,128)(2,1)}, u32[]{:S(2)}, u32[]{:S(2)}) collective-permute-start(bf16[12,2,128,128]{3,2,1,0:T(8,128)(2,1)} %get-tuple-element.113), channel_id=1, source_target_pairs={{0,30},{2,28},{4,26},{6,24},{8,22},{10,20},{12,18},{14,16},{16,14}... | collective-permute-start | bytes 2359304 | tf_op jit(solution)/shard_map/ppermute | solution.py:353
  285.0 1.1 copy-start.3
  286.1 2.8 copy-start.6
  288.9 1.1 copy-start.11
  327.3 16.1 %collective-permute-start.18 = (bf16[512,384]{1,0:T(8,128)(2,1)S(1)}, bf16[512,384]{1,0:T(8,128)(2,1)S(1)}, u32[]{:S(2)}, u32[]{:S(2)}) collective-permute-start(bf16[512,384]{1,0:T(8,128)(2,1)S(1)} %get-tuple-element.155), channel_id=1, source_target_pairs={{0,1},{1,0},{2,3},{3,2},{4,5},{5,4},{6,7},{7,6},{8,9},{9,8},{10,11... | collective-permute-start | bytes 1179656 | tf_op jit(solution)/shard_map/ppermute | solution.py:406
  332.1 14.3 %collective-permute-start.19 = (bf16[512,384]{1,0:T(8,128)(2,1)S(1)}, bf16[512,384]{1,0:T(8,128)(2,1)S(1)}, u32[]{:S(2)}, u32[]{:S(2)}) collective-permute-start(bf16[512,384]{1,0:T(8,128)(2,1)S(1)} %get-tuple-element.156), channel_id=1, source_target_pairs={{0,1},{1,0},{2,3},{3,2},{4,5},{5,4},{6,7},{7,6},{8,9},{9,8},{10,11... | collective-permute-start | bytes 1179656 | tf_op jit(solution)/shard_map/ppermute | solution.py:406
  336.9 18.0 %collective-permute-start.20 = (bf16[512,384]{1,0:T(8,128)(2,1)S(1)}, bf16[512,384]{1,0:T(8,128)(2,1)S(1)}, u32[]{:S(2)}, u32[]{:S(2)}) collective-permute-start(bf16[512,384]{1,0:T(8,128)(2,1)S(1)} %get-tuple-element.157), channel_id=1, source_target_pairs={{0,1},{1,0},{2,3},{3,2},{4,5},{5,4},{6,7},{7,6},{8,9},{9,8},{10,11... | collective-permute-start | bytes 1179656 | tf_op jit(solution)/shard_map/ppermute | solution.py:406
  341.3 22.0 %collective-permute-start.21 = (bf16[512,384]{1,0:T(8,128)(2,1)S(1)}, bf16[512,384]{1,0:T(8,128)(2,1)S(1)}, u32[]{:S(2)}, u32[]{:S(2)}) collective-permute-start(bf16[512,384]{1,0:T(8,128)(2,1)S(1)} %get-tuple-element.158), channel_id=1, source_target_pairs={{0,1},{1,0},{2,3},{3,2},{4,5},{5,4},{6,7},{7,6},{8,9},{9,8},{10,11... | collective-permute-start | bytes 1179656 | tf_op jit(solution)/shard_map/ppermute | solution.py:406
  355.0 8.3 %copy-start.24 = (bf16[512,3072]{1,0:T(8,128)(2,1)}, bf16[512,3072]{1,0:T(8,128)(2,1)S(1)}, u32[]{:S(2)}) copy-start(bf16[512,3072]{1,0:T(8,128)(2,1)S(1)} %constant_dynamic-update-slice_fusion.1) | copy-start | bytes 9437188
Sparse Core Ops, SparseCore 0:
  178.2 73.9 all-gather.1
